TPU v7x, 32 devices: a whole 2x2x4 slice. The times are simulated.
32 devices in a mesh: batch: 16 (over z, y, x), unit: 2 (over core).
Axes of the slice: x: 2, y: 2, z: 4, core: 2. Of those that a mesh axis runs over, the one named last changes fastest.
Arguments:
- memory: bfloat16 [2, 192, 64, 512], P(None, 'batch'), may hold values from -6 to 6
- targets: bfloat16 [2, 192, 6, 80], P(None, 'batch'), may hold values from -6 to 6
- segments: int32 [2, 192, 6], P(None, 'batch'), may hold values from 0 to 2, never falling along the last dimension, each value on 1 to 3 neighbouring positions
- text_lengths: int32 [2, 192, 3], P(None, 'batch'), may hold values from 1 to 32, 64 in all within a row
- zone_first: int32 [2, 192, 6, 1024], P(None, 'batch', None, 'unit'), may hold values 0 or 1
- zone_second: int32 [2, 192, 6, 1024], P(None, 'batch', None, 'unit'), may hold values 0 or 1
- drop_first: int32 [2, 192, 6, 256], P(None, 'batch'), may hold values 0 or 1
- drop_second: int32 [2, 192, 6, 256], P(None, 'batch'), may hold values 0 or 1
- prenet_first: bfloat16 [80, 256], replicated, may hold values from -0.625 to 0.625
- prenet_second: bfloat16 [256, 256], replicated, may hold values from -0.375 to 0.375
- query_weight: bfloat16 [1024, 128], replicated, may hold values from -0.1875 to 0.1875
- memory_weight: bfloat16 [512, 128], replicated, may hold values from -0.25 to 0.25
- location_conv: bfloat16 [32, 2, 31], replicated, may hold values from -0.75 to 0.75
- location_dense: bfloat16 [32, 128], replicated, may hold values from -1 to 1
- energy_vector: bfloat16 [128], replicated, may hold values from -1.5 to 1.5
- lstm_first: bfloat16 [1792, 4, 1024], P('batch', None, 'unit'), may hold values from -0.125 to 0.125
- bias_first: float32 [4, 1024], P(None, 'unit'), may hold values from -3 to 3
- lstm_second: bfloat16 [2560, 4, 1024], P('batch', None, 'unit'), may hold values from -0.125 to 0.125
- bias_second: float32 [4, 1024], P(None, 'unit'), may hold values from -3 to 3
- frame_weight: bfloat16 [1536, 81], replicated, may hold values from -0.15625 to 0.15625
- frame_bias: float32 [81], replicated, may hold values from -3 to 3
- post_first: bfloat16 [5, 80, 512], P(None, None, 'unit'), may hold values from -0.3125 to 0.3125
- post_middle: bfloat16 [3, 5, 512, 512], P(None, None, 'batch', 'unit'), may hold values from -0.125 to 0.125
- post_last: bfloat16 [5, 512, 80], P(None, 'batch', 'unit'), may hold values from -0.125 to 0.125
- middle_norm: float32 [2, 4, 512], P(None, None, 'unit'), may hold values from 0.1 to 1.9
- last_norm: float32 [2, 80], P(None, 'unit'), may hold values from 0.1 to 1.9
Outputs:
- prenet_first_grad: float32 [80, 256], replicated
- prenet_second_grad: float32 [256, 256], replicated
- query_weight_grad: float32 [1024, 128], replicated
- memory_weight_grad: float32 [512, 128], replicated
- location_conv_grad: float32 [32, 2, 31], replicated
- location_dense_grad: float32 [32, 128], replicated
- energy_vector_grad: float32 [128], replicated
- lstm_first_grad: float32 [1792, 4, 1024], P('batch', None, 'unit')
- bias_first_grad: float32 [4, 1024], P(None, 'unit')
- lstm_second_grad: float32 [2560, 4, 1024], P('batch', None, 'unit')
- bias_second_grad: float32 [4, 1024], P(None, 'unit')
- frame_weight_grad: float32 [1536, 81], replicated
- frame_bias_grad: float32 [81], replicated
- post_first_grad: float32 [5, 80, 512], P(None, None, 'unit')
- post_middle_grad: float32 [3, 5, 512, 512], P(None, None, 'batch', 'unit')
- post_last_grad: float32 [5, 512, 80], P(None, 'batch', 'unit')
- middle_norm_grad: float32 [2, 4, 512], P(None, None, 'unit')
- last_norm_grad: float32 [2, 80], P(None, 'unit')
- memory_grad: float32 [2, 192, 64, 512], P(None, 'batch')
Inputs may be any that keep to these rules, and one draw needn't show every extreme that they name: `segments`: each row numbers its frames by utterance in order, never falling; every one of the 3 utterances has 1 to 3 frames. `text_lengths`: the 3 counts of a row sum to 64.
All inputs are finite; a program needn't handle non-finite values. No bound on the sum of `zone_first` or of `zone_second` or of `drop_first` or of `drop_second` on one device may be relied on, other than what follows from the above.
Results may differ from a plain program's by a relative error of at most 0.03.
Values may be sent and summed in bfloat16 or wider, within the bound.
No kernel may reach another device: no remote copies, remote signals or barrier semaphores. Data moves between devices by JAX's collectives and lax.ppermute only.
A program may use at most 256 MiB of HBM per device.

v0:
```python
import functools

import jax
import jax.numpy as jnp
from jax import lax
from jax.experimental import pallas as pl
from jax.experimental.pallas import tpu as pltpu
from jax.sharding import PartitionSpec as P

precise = lax.Precision.HIGHEST
norm_eps = 1e-05
f32 = jnp.float32
bf16 = jnp.bfloat16
lanes = 128
kernel_vmem = 60 * 1024 * 1024


def split(value):
    high = value.astype(bf16)
    return high, (value - high.astype(f32)).astype(bf16)


def dot(a, b, contract=((1,), (0,))):
    return lax.dot_general(a, b, (contract, ((), ())), preferred_element_type=f32)


def dot_left(exact, value, contract=((1,), (0,))):
    high, low = split(value)
    return dot(exact, high, contract) + dot(exact, low, contract)


def dot_right(value, exact, contract=((1,), (0,))):
    high, low = split(value)
    return dot(high, exact, contract) + dot(low, exact, contract)


def dot_both(a, b, contract=((1,), (0,))):
    a_high, a_low = split(a)
    b_high, b_low = split(b)
    return (
        dot(a_high, b_high, contract) + dot(a_low, b_high, contract) + dot(a_high, b_low, contract)
    )


rows_first = ((0,), (0,))
lanes_both = ((1,), (1,))


def position_hot(position_count, text_width, reverse):
    place = lax.broadcasted_iota(jnp.int32, (position_count, lanes), 0) & (text_width - 1)
    lane = lax.broadcasted_iota(jnp.int32, (position_count, lanes), 1)
    place = (lanes - 1) - place if reverse else place + 1
    return (place == lane).astype(bf16)


def slant(value, text_width):
    blocks = [
        pltpu.roll(value[start : start + text_width], 0, 1, stride=1, stride_axis=0)
        for start in range(0, value.shape[0], text_width)
    ]
    return jnp.concatenate(blocks, axis=0)


def pad_rows(value):
    return jnp.concatenate(
        [value, jnp.zeros((lanes - value.shape[0], value.shape[1]), value.dtype)], axis=0
    )


def unit_spot(chunk, unit, per_half):
    half = (chunk // per_half + unit) % 2
    return pl.multiple_of((half * per_half + chunk % per_half) * lanes, lanes)


def gate_spot(chunk, gate, per_half):
    start = (chunk // per_half) * 4 * per_half + gate * per_half + chunk % per_half
    return pl.multiple_of(start * lanes, lanes)


def forward_kernel(
    unit_ref,
    own_one,
    peer_one,
    own_two,
    peer_two,
    previous_ref,
    drop_one,
    drop_two,
    layer_one,
    layer_two,
    slot_ref,
    zone_one,
    zone_two,
    bias_one,
    bias_two,
    hot_ref,
    memory_ref,
    project_ref,
    query_ref,
    vector_ref,
    conv_ref,
    dense_ref,
    frame_ref,
    frame_bias,
    gates_one,
    gates_two,
    prior_one,
    prior_two,
    round_one,
    round_two,
    context_ref,
    mixed_ref,
    alpha_ref,
    taps_ref,
    prenet_one,
    prenet_two,
    prenet_hidden,
    prenet_out,
    frame_out,
    held_one,
    held_two,
    input_ref,
    prenet_ref,
    processed_ref,
    filter_ref,
    state_one,
    cell_one,
    state_two,
    cell_two,
    sems,
):
    unit = unit_ref[0]
    steps, slots, hidden = round_one.shape
    prenet_width = layer_two.shape[1]
    context_width = context_ref.shape[2]
    half = hidden // 2
    per_half = half // lanes
    position_count = hot_ref.shape[0]
    text_width = position_count // (slots // 4)
    copies_two = [
        pltpu.make_async_copy(own_two, held_two.at[0], sems.at[0]),
        pltpu.make_async_copy(peer_two, held_two.at[1], sems.at[1]),
    ]
    copies_one = [
        pltpu.make_async_copy(own_one, held_one.at[0], sems.at[2]),
        pltpu.make_async_copy(peer_one, held_one.at[1], sems.at[3]),
    ]
    for copy in copies_two + copies_one:
        copy.start()
    for ref in (state_one, cell_one, state_two, cell_two):
        ref[...] = jnp.zeros_like(ref)

    def gates_into(held, depth, bias_ref, out_ref, step):
        def one(block, _):
            side = block // 4
            inputs = input_ref[:, :depth]
            for pair in range(per_half // 2):
                tile = (block % 4) * per_half + 2 * pair
                outside = pl.ds(
                    pl.multiple_of(block * half + 2 * pair * lanes, 2 * lanes), 2 * lanes
                )
                kernel = jnp.concatenate(
                    [held[side, tile, :depth, :], held[side, tile + 1, :depth, :]], axis=1
                )
                out_ref[step, :, outside] = dot(inputs, kernel) + bias_ref[:, outside]
            return 0

        lax.fori_loop(0, 8, one, 0)

    def cell(gates_ref, zone_ref, prior_ref, state, cells, round_ref, step):
        def one(chunk, _):
            spot = pl.ds(pl.multiple_of(chunk * lanes, lanes), lanes)
            values = [
                gates_ref[step, :, pl.ds(gate_spot(chunk, gate, per_half), lanes)]
                for gate in range(4)
            ]
            zone = zone_ref[step, :, spot]
            before = cells[:, spot]
            prior_ref[step, :, spot] = before
            fresh = jax.nn.sigmoid(values[1]) * before + jax.nn.sigmoid(values[0]) * jnp.tanh(
                values[2]
            )
            output = jax.nn.sigmoid(values[3]) * jnp.tanh(fresh)
            now = zone * state[:, spot] + (1.0 - zone) * output
            state[:, spot] = now
            cells[:, spot] = zone * before + (1.0 - zone) * fresh
            round_ref[step, :, pl.ds(unit_spot(chunk, unit, per_half), lanes)] = now.astype(bf16).astype(
                f32
            )
            return 0

        lax.fori_loop(0, 2 * per_half, one, 0)

    def attention(step, location):
        inside = hot_ref[...] > 0.0
        hot = hot_ref[...].astype(bf16)
        query = pad_rows(dot(round_one[step].astype(bf16), query_ref[...].astype(bf16)))
        summed = dot_left(hot, query) + processed_ref[...]
        if location is not None:
            summed = summed + location
        mixed = jnp.tanh(summed)
        mixed_ref[step] = mixed
        energy = dot_right(mixed, vector_ref[...].astype(bf16))
        most = jnp.max(jnp.where(inside, energy, -1000000000.0), axis=0, keepdims=True)
        shifted = jnp.where(inside, jnp.exp(energy - most), 0.0)
        total = jnp.sum(shifted, axis=0, keepdims=True)
        alpha = shifted / jnp.where(total > 0.0, total, 1.0)
        alpha_ref[step] = alpha
        context = dot_right(alpha, memory_ref[...].astype(bf16), rows_first)[:slots]
        context_ref[step] = context.astype(bf16).astype(f32)

    def taps_of(step):
        spread = dot_right(
            alpha_ref[step], position_hot(position_count, text_width, True), rows_first
        )
        taps_ref[step] = slant(dot_left(hot_ref[...].astype(bf16), spread), text_width)

    def second_layer(step, depth):
        input_ref[:, :hidden] = round_one[step].astype(bf16)
        input_ref[:, hidden : hidden + context_width] = context_ref[step].astype(bf16)
        gates_into(held_two, depth, bias_two, gates_two, step)
        cell(gates_two, zone_two, prior_two, state_two, cell_two, round_two, step)

    slot_hot = slot_ref[...].astype(bf16)

    def prenet_layer(source, layer, drops, mixed_out, out):
        mixed = dot(source.astype(bf16), layer[...].astype(bf16))
        mixed_out[...] = mixed
        value = (mixed * jax.nn.sigmoid(mixed) * drops[...] * 2.0).astype(bf16)
        out[...] = value.astype(f32)
        return value

    hidden_value = prenet_layer(previous_ref[...], layer_one, drop_one, prenet_one, prenet_hidden)
    prenet_value = prenet_layer(hidden_value, layer_two, drop_two, prenet_two, prenet_out)
    prenet_slots = dot(slot_hot, prenet_value, rows_first)
    for step in range(steps):
        prenet_ref[step] = prenet_slots[step * slots : (step + 1) * slots]
    processed_ref[...] = dot(memory_ref[...].astype(bf16), project_ref[...].astype(bf16))
    for channel in range(2):
        filter_ref[channel] = dot(
            conv_ref[channel].astype(bf16), dense_ref[...].astype(bf16)
        )

    gates_one[0] = jnp.broadcast_to(bias_one[...], gates_one.shape[1:])
    cell(gates_one, zone_one, prior_one, state_one, cell_one, round_one, 0)
    attention(0, None)
    taps_of(0)
    for copy in copies_two:
        copy.wait()
    second_layer(0, hidden + context_width)
    for copy in copies_one:
        copy.wait()

    def later(step, _):
        input_ref[:, :prenet_width] = prenet_ref[step].astype(bf16)
        input_ref[:, prenet_width : prenet_width + context_width] = context_ref[step - 1].astype(
            bf16
        )
        input_ref[:, prenet_width + context_width : prenet_width + context_width + hidden] = (
            round_one[step - 1].astype(bf16)
        )
        gates_into(
            held_one, prenet_width + context_width + hidden, bias_one, gates_one, step
        )
        cell(gates_one, zone_one, prior_one, state_one, cell_one, round_one, step)
        previous = taps_ref[step - 1]
        summed = jnp.where(step == 2, taps_ref[0] + previous, previous)
        attention(step, dot_both(previous, filter_ref[0]) + dot_both(summed, filter_ref[1]))

        @pl.when(step < steps - 1)
        def _():
            taps_of(step)

        input_ref[:, hidden + context_width :] = round_two[step - 1].astype(bf16)
        second_layer(step, 2 * hidden + context_width)
        return 0

    lax.fori_loop(1, steps, later, 0)
    for step in range(steps):
        values = dot(round_two[step].astype(bf16), frame_ref[:hidden].astype(bf16)) + dot(
            context_ref[step].astype(bf16), frame_ref[hidden:].astype(bf16)
        )
        high = values.astype(bf16)
        rest = values - high.astype(f32)
        middle = rest.astype(bf16)
        low = (rest - middle.astype(f32)).astype(bf16)
        chosen = slot_hot[:, step * slots : (step + 1) * slots]
        picked = (dot(chosen, high) + dot(chosen, middle)) + dot(chosen, low)
        frame_out[...] = (frame_bias[...] if step == 0 else frame_out[...]) + picked


def backward_kernel(
    unit_ref,
    own_one,
    peer_one,
    own_two,
    peer_two,
    gates_one,
    gates_two,
    prior_one,
    prior_two,
    zone_one,
    zone_two,
    hot_ref,
    memory_ref,
    query_ref,
    vector_ref,
    conv_ref,
    dense_ref,
    mixed_ref,
    alpha_ref,
    taps_ref,
    frame_grad,
    frame_weight,
    slot_ref,
    sent_ref,
    prenet_grad,
    context_grad,
    query_grad,
    processed_grad,
    vector_grad,
    filter_grad,
    held_one,
    held_two,
    grads_one,
    grads_two,
    back_one,
    back_two,
    state_one,
    cell_one,
    state_two,
    cell_two,
    previous_grad,
    summed_grad,
    from_query,
    frame_ref,
    filter_ref,
    sems,
):
    unit = unit_ref[0]
    steps, slots, prenet_width = prenet_grad.shape
    context_width = context_grad.shape[2]
    hidden = state_one.shape[1]
    half = hidden // 2
    per_half = half // lanes
    position_count = hot_ref.shape[0]
    text_width = position_count // (slots // 4)
    copies_two = [
        pltpu.make_async_copy(own_two, held_two.at[0], sems.at[0]),
        pltpu.make_async_copy(peer_two, held_two.at[1], sems.at[1]),
    ]
    copies_one = [
        pltpu.make_async_copy(own_one, held_one.at[0], sems.at[2]),
        pltpu.make_async_copy(peer_one, held_one.at[1], sems.at[3]),
    ]
    for copy in copies_two + copies_one:
        copy.start()
    for ref in (
        state_one,
        cell_one,
        state_two,
        cell_two,
        back_one,
        back_two,
        previous_grad,
        summed_grad,
        processed_grad,
        vector_grad,
        filter_grad,
    ):
        ref[...] = jnp.zeros_like(ref)

    def cell(gates_ref, prior_ref, zone_ref, state, cells, grads_ref, step, incoming):
        def one(chunk, _):
            spot = pl.ds(pl.multiple_of(chunk * lanes, lanes), lanes)
            places = [pl.ds(gate_spot(chunk, gate, per_half), lanes) for gate in range(4)]
            values = [gates_ref[step, :, place] for place in places]
            zone = zone_ref[step, :, spot]
            keep = 1.0 - zone
            before = prior_ref[step, :, spot]
            gate_in = jax.nn.sigmoid(values[0])
            gate_forget = jax.nn.sigmoid(values[1])
            candidate = jnp.tanh(values[2])
            gate_out = jax.nn.sigmoid(values[3])
            bent = jnp.tanh(gate_forget * before + gate_in * candidate)
            grad_state = incoming(unit_spot(chunk, unit, per_half)) + state[:, spot]
            grad_cell = cells[:, spot]
            grad_new = keep * grad_state
            grad_fresh = grad_new * gate_out * (1.0 - bent * bent) + keep * grad_cell
            state[:, spot] = zone * grad_state
            cells[:, spot] = zone * grad_cell + gate_forget * grad_fresh
            results = (
                grad_fresh * candidate * gate_in * (1.0 - gate_in),
                grad_fresh * before * gate_forget * (1.0 - gate_forget),
                grad_fresh * gate_in * (1.0 - candidate * candidate),
                grad_new * bent * gate_out * (1.0 - gate_out),
            )
            for place, result in zip(places, results):
                grads_ref[step, :, place] = result.astype(bf16)
            return 0

        lax.fori_loop(0, 2 * per_half, one, 0)

    def inputs_back(grads_ref, held, out_ref, step, blocks):
        def one(block, _):
            spot = pl.ds(pl.multiple_of(block * 256, 256), 256)
            total = None
            for tile in range(0, 8 * per_half, 2):
                side, inside = tile // (4 * per_half), tile % (4 * per_half)
                kernel = jnp.concatenate(
                    [held[side, inside, spot, :], held[side, inside + 1, spot, :]], axis=1
                )
                grads = grads_ref[step, :, tile * lanes : (tile + 2) * lanes]
                product = dot(grads, kernel, lanes_both)
                total = product if total is None else total + product
            out_ref[:, spot] = total
            return 0

        lax.fori_loop(0, blocks, one, 0)

    def attention(step, located):
        inside = hot_ref[...] > 0.0
        hot = hot_ref[...].astype(bf16)
        alpha = alpha_ref[step]
        mixed = mixed_ref[step]
        context_now = pad_rows(context_grad[step])
        weights_grad = jnp.where(
            inside,
            dot_left(memory_ref[...].astype(bf16), context_now, lanes_both)
            + previous_grad[...]
            + summed_grad[...],
            0.0,
        )
        product = alpha * weights_grad
        energy_grad = product - alpha * jnp.sum(product, axis=0, keepdims=True)
        spread = jnp.sum(energy_grad, axis=1, keepdims=True)
        vector_grad[...] += jnp.sum(spread * mixed, axis=0, keepdims=True)
        mixed_grad = spread * vector_ref[...] * (1.0 - mixed * mixed)
        processed_grad[...] += mixed_grad
        high, low = split(mixed_grad)
        query_now = (dot(hot, high, rows_first) + dot(hot, low, rows_first))[:slots]
        query_grad[step] = query_now
        from_query[...] = dot_right(query_now, query_ref[...].astype(bf16), lanes_both)
        if located:
            previous = taps_ref[step - 1]
            summed = jnp.where(step == 2, taps_ref[0] + previous, previous)
            filter_grad[0] += dot_both(previous, mixed_grad, rows_first)
            filter_grad[1] += dot_both(summed, mixed_grad, rows_first)
            place_hot = position_hot(position_count, text_width, False)

            def taps_back(channel):
                taps_grad = slant(
                    dot_both(mixed_grad, filter_ref[channel], lanes_both), text_width
                )
                gathered = dot_right(taps_grad, hot, rows_first)
                return jnp.where(inside, dot_left(place_hot, gathered), 0.0)

            previous_grad[...] = taps_back(0)
            summed_grad[...] += taps_back(1)

    def arrived(step, copies):
        @pl.when(step == steps - 1)
        def _():
            for copy in copies:
                copy.wait()

    def step_back(step, located):
        cell(
            gates_two,
            prior_two,
            zone_two,
            state_two,
            cell_two,
            grads_two,
            step,
            lambda spot: frame_ref[step, :, pl.ds(spot, lanes)]
            + back_two[:, pl.ds(spot + hidden + context_width, lanes)],
        )
        blocks_two = (hidden + context_width + (hidden if located else 0)) // 256
        if located:
            arrived(step, copies_two)
        inputs_back(grads_two, held_two, back_two, step, blocks_two)
        context_grad[step] = (
            back_two[:, hidden : hidden + context_width]
            + frame_ref[step, :, hidden:]
            + back_one[:, prenet_width : prenet_width + context_width]
        )
        attention(step, located)
        cell(
            gates_one,
            prior_one,
            zone_one,
            state_one,
            cell_one,
            grads_one,
            step,
            lambda spot: back_two[:, pl.ds(spot, lanes)]
            + from_query[:, pl.ds(spot, lanes)]
            + back_one[:, pl.ds(spot + prenet_width + context_width, lanes)],
        )
        blocks_one = (prenet_width + (hidden + context_width if located else 0)) // 256
        if located:
            arrived(step, copies_one)
        inputs_back(grads_one, held_one, back_one, step, blocks_one)
        prenet_grad[step] = back_one[:, :prenet_width]

    for channel in range(2):
        filter_ref[channel] = dot(
            conv_ref[channel].astype(bf16), dense_ref[...].astype(bf16)
        )
    for step in range(steps):
        frame_ref[step] = dot(
            frame_grad[step].astype(bf16), frame_weight[...].astype(bf16), lanes_both
        )

    def later(index, _):
        step_back(steps - 1 - index, True)
        return 0

    lax.fori_loop(0, steps - 1, later, 0)
    step_back(0, False)
    slot_hot = slot_ref[...].astype(bf16)

    def tile_out(tile, _):
        for layer, grads_ref in ((0, grads_one), (1, grads_two)):
            for side in range(2):
                place = ((side + unit) % 2) * 4 * half + tile * lanes
                grads = grads_ref[:, :, pl.ds(pl.multiple_of(place, lanes), lanes)]
                chosen = dot(slot_hot, grads.reshape(steps * slots, lanes)).astype(bf16)
                spot = (2 * layer + side) * lanes
                sent_ref[tile, :, spot : spot + lanes] = chosen
        return 0

    lax.fori_loop(0, 4 * per_half, tile_out, 0)


def call_forward(unit, weights, small, sizes):
    own_one, peer_one, own_two, peer_two = weights
    steps, slots, hidden, context_width, positions, frame_rows, prenet_width = sizes

    def shape(*dims):
        return jax.ShapeDtypeStruct(dims, f32)

    outs = [
        shape(steps, slots, 4 * hidden),
        shape(steps, slots, 4 * hidden),
        shape(steps, slots, hidden),
        shape(steps, slots, hidden),
        shape(steps, slots, hidden),
        shape(steps, slots, hidden),
        shape(steps, slots, context_width),
        shape(steps, positions, lanes),
        shape(steps, positions, lanes),
        shape(steps - 1, positions, lanes),
        shape(frame_rows, prenet_width),
        shape(frame_rows, prenet_width),
        shape(frame_rows, prenet_width),
        shape(frame_rows, prenet_width),
        shape(frame_rows, lanes),
    ]
    vmem = pl.BlockSpec(memory_space=pltpu.VMEM)
    return pl.pallas_call(
        forward_kernel,
        out_shape=outs,
        in_specs=[pl.BlockSpec(memory_space=pltpu.SMEM)]
        + [pl.BlockSpec(memory_space=pl.ANY)] * 4
        + [vmem] * len(small),
        out_specs=[vmem] * len(outs),
        scratch_shapes=[
            pltpu.VMEM((2,) + own_one.shape, bf16),
            pltpu.VMEM((2,) + own_two.shape, bf16),
            pltpu.VMEM((slots, own_two.shape[1]), bf16),
            pltpu.VMEM((steps, slots, prenet_width), f32),
            pltpu.VMEM((positions, lanes), f32),
            pltpu.VMEM((2, lanes, lanes), f32),
            pltpu.VMEM((slots, hidden), f32),
            pltpu.VMEM((slots, hidden), f32),
            pltpu.VMEM((slots, hidden), f32),
            pltpu.VMEM((slots, hidden), f32),
            pltpu.SemaphoreType.DMA((4,)),
        ],
        compiler_params=pltpu.CompilerParams(vmem_limit_bytes=kernel_vmem),
        name="decoder_forward",
    )(unit, *weights, *small)


def call_backward(unit, weights, small):
    own_one, peer_one, own_two, peer_two = weights
    gates_one = small[0]
    steps, slots, gate_width = gates_one.shape
    hidden = gate_width // 4
    positions, context_width = small[7].shape
    prenet_width = own_one.shape[1] - hidden - context_width

    def shape(dims, kind):
        return jax.ShapeDtypeStruct(dims, kind)

    outs = [
        shape((gate_width // (2 * lanes), small[-1].shape[0], 4 * lanes), bf16),
        shape((steps, slots, prenet_width), f32),
        shape((steps, slots, context_width), f32),
        shape((steps, slots, lanes), f32),
        shape((positions, lanes), f32),
        shape((1, lanes), f32),
        shape((2, lanes, lanes), f32),
    ]
    vmem = pl.BlockSpec(memory_space=pltpu.VMEM)
    return pl.pallas_call(
        backward_kernel,
        out_shape=outs,
        in_specs=[pl.BlockSpec(memory_space=pltpu.SMEM)]
        + [pl.BlockSpec(memory_space=pl.ANY)] * 4
        + [vmem] * len(small),
        out_specs=[vmem] * len(outs),
        scratch_shapes=[
            pltpu.VMEM((2,) + own_one.shape, bf16),
            pltpu.VMEM((2,) + own_two.shape, bf16),
            pltpu.VMEM((steps, slots, gate_width), bf16),
            pltpu.VMEM((steps, slots, gate_width), bf16),
            pltpu.VMEM((slots, own_one.shape[1]), f32),
            pltpu.VMEM((slots, own_two.shape[1]), f32),
            pltpu.VMEM((slots, hidden), f32),
            pltpu.VMEM((slots, hidden), f32),
            pltpu.VMEM((slots, hidden), f32),
            pltpu.VMEM((slots, hidden), f32),
            pltpu.VMEM((positions, lanes), f32),
            pltpu.VMEM((positions, lanes), f32),
            pltpu.VMEM((slots, hidden), f32),
            pltpu.VMEM((steps, slots, hidden + context_width), f32),
            pltpu.VMEM((2, lanes, lanes), f32),
            pltpu.SemaphoreType.DMA((4,)),
        ],
        compiler_params=pltpu.CompilerParams(vmem_limit_bytes=kernel_vmem),
        name="decoder_backward",
    )(unit, *weights, *small)


def postnet_kernel(
    mel_width,
    loss_scale,
    unit_ref,
    mel_ref,
    target_ref,
    mask_ref,
    first_ref,
    own_ref,
    peer_ref,
    last_ref,
    gain_ref,
    shift_ref,
    inputs_first,
    inputs_later,
    grads_early,
    grads_last,
    norm_grads,
    mel_grad,
    padded,
    padded_mel,
    held,
    normed_early,
    normed_last,
    inverse_ref,
    post_grad,
):
    unit = unit_ref[0]
    count, channels = held.shape
    side = channels // 2
    frames = padded.shape[0] - count
    rows_each = frames // 4
    chunk = 2 * rows_each
    tall = float(count)
    body_rows = slice(2 * rows_each, 2 * rows_each + count)

    for ref in (padded, padded_mel):
        ref[: 2 * rows_each] = jnp.zeros((2 * rows_each, ref.shape[1]), bf16)
        ref[2 * rows_each + count :] = jnp.zeros((2 * rows_each, ref.shape[1]), bf16)

    def piece(source, start, tap, width, lane=None):
        spot = pl.ds(pl.multiple_of(start + tap * rows_each, rows_each), chunk)
        mask = mask_ref[tap, pl.ds(pl.multiple_of(start, rows_each), chunk), :]
        if width < lanes:
            mask = mask[:, :width]
        else:
            mask = jnp.concatenate([mask] * (width // lanes), axis=1)
        value = source[spot, :] if lane is None else source[spot, pl.ds(lane, width)]
        return value * mask

    def chunks(work):
        def one(index, _):
            work(pl.multiple_of(index * chunk, chunk))
            return 0

        lax.fori_loop(0, count // chunk, one, 0)

    def half_spot(which):
        return pl.multiple_of(((which + unit) % 2) * side, side)

    def norm_forward(value, layer, lane, width):
        mean = jnp.sum(value, axis=0, keepdims=True) / tall
        centered = value - mean
        inverse = lax.rsqrt(jnp.sum(centered * centered, axis=0, keepdims=True) / tall + norm_eps)
        inverse_ref[layer, :, pl.ds(lane, width)] = inverse
        return centered * inverse

    def each_lane_block(work):
        def one(index, _):
            work(pl.multiple_of(index * lanes, lanes))
            return 0

        lax.fori_loop(0, channels // lanes, one, 0)

    def activate(layer):
        def block(lane):
            spot = pl.ds(lane, lanes)
            normed = norm_forward(held[:, spot], layer, lane, lanes)
            normed_early[layer, :, spot] = normed
            active = jnp.tanh(
                normed * gain_ref[layer, :, spot] + shift_ref[layer, :, spot]
            ).astype(bf16)
            inputs_later[layer, :, spot] = active
            padded[body_rows, spot] = active

        each_lane_block(block)

    source = mel_ref[...].astype(bf16)
    inputs_first[...] = source
    padded_mel[body_rows] = source

    def first_chunk(start):
        total = None
        for tap in range(5):
            product = dot(piece(padded_mel, start, tap, mel_width), first_ref[tap])
            total = product if total is None else total + product
        held[pl.ds(start, chunk), :] = total

    chunks(first_chunk)
    activate(0)

    def middle(index, _):
        for which, ref in ((0, own_ref), (1, peer_ref)):

            def middle_chunk(start, which=which, ref=ref):
                total = None
                for tap in range(5):
                    product = dot(piece(padded, start, tap, channels), ref[index * 5 + tap])
                    total = product if total is None else total + product
                held[pl.ds(start, chunk), pl.ds(half_spot(which), side)] = total

            chunks(middle_chunk)
        activate(index + 1)
        return 0

    lax.fori_loop(0, 3, middle, 0)

    def last_chunk(start):
        total = None
        for tap in range(5):
            product = dot(piece(padded, start, tap, channels), last_ref[tap])
            total = product if total is None else total + product
        normed_last[pl.ds(start, chunk), :] = total

    chunks(last_chunk)
    normed = norm_forward(normed_last[...], 4, 0, mel_width)
    normed_last[...] = normed

    def norm_back(grad, normed, layer, lane, width):
        spot = pl.ds(lane, width)
        shift_grad = jnp.sum(grad, axis=0, keepdims=True)
        gain_grad = jnp.sum(grad * normed, axis=0, keepdims=True)
        norm_grads[0, layer, :, spot] = gain_grad
        norm_grads[1, layer, :, spot] = shift_grad
        return (
            gain_ref[layer, :, spot]
            * inverse_ref[layer, :, spot]
            * (grad - shift_grad / tall - normed * (gain_grad / tall))
        ).astype(bf16)

    output = normed * gain_ref[4, :, :mel_width] + shift_ref[4, :, :mel_width]
    grad = loss_scale * (mel_ref[...] + output - target_ref[...])
    post_grad[...] = grad
    grad_norm = norm_back(grad, normed, 4, 0, mel_width)
    grads_last[...] = grad_norm
    padded_mel[body_rows] = grad_norm

    def last_back(start):
        total = None
        for tap in range(5):
            product = dot(
                piece(padded_mel, start, tap, mel_width), last_ref[4 - tap], lanes_both
            )
            total = product if total is None else total + product
        held[pl.ds(start, chunk), :] = total

    chunks(last_back)

    def deactivate(layer):
        def block(lane):
            spot = pl.ds(lane, lanes)
            normed = normed_early[layer, :, spot]
            active = jnp.tanh(normed * gain_ref[layer, :, spot] + shift_ref[layer, :, spot])
            grad = held[:, spot] * (1.0 - active * active)
            grad_norm = norm_back(grad, normed, layer, lane, lanes)
            grads_early[layer, :, spot] = grad_norm
            padded[body_rows, spot] = grad_norm

        each_lane_block(block)

    def middle_back(back, _):
        index = 2 - back
        deactivate(index + 1)

        def chunk_back(start):
            total = None
            for which, ref in ((0, own_ref), (1, peer_ref)):
                for tap in range(5):
                    product = dot(
                        piece(padded, start, tap, side, half_spot(which)),
                        ref[index * 5 + 4 - tap],
                        lanes_both,
                    )
                    total = product if total is None else total + product
            held[pl.ds(start, chunk), :] = total

        chunks(chunk_back)
        return 0

    lax.fori_loop(0, 3, middle_back, 0)
    deactivate(0)

    def first_back(start):
        total = None
        for tap in range(5):
            product = dot(piece(padded, start, tap, channels), first_ref[4 - tap], lanes_both)
            total = product if total is None else total + product
        spot = pl.ds(start, chunk)
        mel_grad[spot, :] = (
            loss_scale * (mel_ref[spot, :] - target_ref[spot, :]) + post_grad[spot, :] + total
        )

    chunks(first_back)


def call_postnet(unit, small, loss_scale, rows_all):
    mel = small[0]
    count, mel_width = mel.shape
    channels = small[3].shape[2]

    def shape(kind, *dims):
        return jax.ShapeDtypeStruct(dims, kind)

    outs = [
        shape(bf16, count, mel_width),
        shape(bf16, 4, count, channels),
        shape(bf16, 4, count, channels),
        shape(bf16, count, mel_width),
        shape(f32, 2, 5, 1, channels),
        shape(f32, count, mel_width),
    ]
    vmem = pl.BlockSpec(memory_space=pltpu.VMEM)
    tall = count + 4 * rows_all
    return pl.pallas_call(
        functools.partial(postnet_kernel, mel_width, loss_scale),
        out_shape=outs,
        in_specs=[pl.BlockSpec(memory_space=pltpu.SMEM)] + [vmem] * len(small),
        out_specs=[vmem] * len(outs),
        scratch_shapes=[
            pltpu.VMEM((tall, channels), bf16),
            pltpu.VMEM((tall, mel_width), bf16),
            pltpu.VMEM((count, channels), f32),
            pltpu.VMEM((4, count, channels), f32),
            pltpu.VMEM((count, mel_width), f32),
            pltpu.VMEM((5, 1, channels), f32),
            pltpu.VMEM((count, mel_width), f32),
        ],
        compiler_params=pltpu.CompilerParams(vmem_limit_bytes=kernel_vmem),
        name="postnet",
    )(unit, *small)


def shifted_frames(source, same):
    steps = source.shape[0]
    padded = jnp.pad(source, ((2, 2), (0, 0), (0, 0)))
    return [
        padded[offset : offset + steps] * same[:, :, offset, None].astype(source.dtype)
        for offset in range(5)
    ]


def by_rows(work, roomy, arrays, summed=False):
    if roomy:
        return work(*arrays)
    parts = arrays[0].shape[1] // 192

    def cut(value):
        value = value.reshape((value.shape[0], parts, -1) + value.shape[2:])
        return jnp.moveaxis(value, 1, 0)

    pieces = tuple(cut(value) for value in arrays)
    if summed:
        first = jax.eval_shape(work, *[value[0] for value in pieces])
        start = jnp.zeros(first.shape, first.dtype)
        return lax.scan(lambda total, now: (total + work(*now), None), start, pieces)[0]
    result = jnp.moveaxis(lax.map(lambda now: work(*now), pieces), 0, 1)
    return result.reshape((result.shape[0], -1) + result.shape[3:])


def post_layer(source, kernel, same):
    wide = jnp.concatenate(shifted_frames(source, same), axis=2)
    return jnp.einsum(
        "src,co->sro", wide, kernel.reshape(-1, kernel.shape[2]), preferred_element_type=f32
    )


def post_layer_back(grad, kernel, same):
    wide = jnp.concatenate(shifted_frames(grad, same), axis=2)
    turned = jnp.transpose(kernel[::-1], (0, 2, 1)).reshape(-1, kernel.shape[1])
    return jnp.einsum("sro,oc->src", wide, turned, preferred_element_type=f32)


def post_kernel_grad(source, grad, same):
    wide = jnp.concatenate(shifted_frames(source, same), axis=2)
    return jnp.einsum("src,sro->co", wide, grad, preferred_element_type=f32)


def on_device(
    memory,
    targets,
    segments,
    text_lengths,
    zone_first,
    zone_second,
    drop_first,
    drop_second,
    prenet_first,
    prenet_second,
    query_weight,
    memory_weight,
    location_conv,
    location_dense,
    energy_vector,
    lstm_first,
    bias_first,
    lstm_second,
    bias_second,
    frame_weight,
    frame_bias,
    post_first,
    post_middle,
    post_last,
    middle_norm,
    last_norm,
):
    micro_count, rows, text_width, memory_width = memory.shape
    frames = segments.shape[2]
    utterances = text_lengths.shape[2]
    mel_width = targets.shape[3]
    hidden = query_weight.shape[0]
    prenet_width = prenet_first.shape[1]
    attention_width = query_weight.shape[1]
    half = lstm_first.shape[2]
    depth_one, depth_two = lstm_first.shape[0], lstm_second.shape[0]
    unit = lax.axis_index("unit")
    place = lax.axis_index("batch")
    batch_size = lax.axis_size("batch")
    total_rows = rows * batch_size
    frame_count = float(total_rows * frames)
    first_unit = unit == 0
    longest = 3
    slots = 4 * rows

    def exchange(value):
        return lax.ppermute(value, "unit", [(0, 1), (1, 0)])

    def ordered(own, peer):
        return jnp.where(first_unit, own, peer), jnp.where(first_unit, peer, own)

    def whole(value, axis):
        return jnp.concatenate(ordered(value, exchange(value)), axis=axis)

    def mine(value):
        return lax.dynamic_index_in_dim(value, unit, 0, keepdims=False)

    def others(value):
        return lax.dynamic_index_in_dim(value, 1 - unit, 0, keepdims=False)

    def swapped(value, bit):
        pairs = [(index, index ^ bit) for index in range(batch_size)]
        other = lax.ppermute(value, "batch", pairs)
        upper = (place & bit) != 0
        return jnp.where(upper, other, value), jnp.where(upper, value, other)

    def gather_rows(value):
        bit = 1
        while bit < batch_size:
            value = jnp.concatenate(swapped(value, bit), axis=0)
            bit *= 2
        return value

    def gather_tiles(value):
        tiles = jnp.transpose(value.reshape(value.shape[0], -1, lanes), (1, 0, 2))
        return lax.all_gather(tiles, "batch", axis=1, tiled=True)

    own_two = gather_tiles(lstm_second)
    own_one = gather_tiles(lstm_first)
    peer_two = exchange(own_two)
    channel_rows = post_middle.shape[2]
    middle_width = post_middle.shape[3]
    middle_half = lax.all_gather(
        post_middle.reshape(-1, channel_rows, middle_width), "batch", axis=1, tiled=True
    )
    last_half = gather_rows(jnp.transpose(post_last, (1, 0, 2)).reshape(channel_rows, -1))
    last_half = jnp.transpose(
        last_half.reshape(-1, post_last.shape[0], post_last.shape[2]), (1, 0, 2)
    )
    memory_now = mine(memory).reshape(rows * text_width, memory_width)
    segments_now = mine(segments)
    targets_now = mine(targets)
    frame_info = gather_rows(
        jnp.concatenate([targets_now, segments_now[:, :, None].astype(bf16)], axis=2).astype(f32)
    )

    same_frames = segments_now[:, :, None] == segments_now[:, None, :]
    earlier = jnp.tril(jnp.ones((frames, frames), jnp.bool_), -1)
    order = jnp.sum((same_frames & earlier[None]).astype(jnp.int32), axis=2)
    slot_of = order * slots + segments_now * rows + jnp.arange(rows, dtype=jnp.int32)[:, None]
    frame_rows = rows * frames
    padding = -frame_rows % 16
    slot_hot = (
        jnp.pad(slot_of.reshape(-1, 1), ((0, padding), (0, 0)), constant_values=-1)
        == jnp.arange(longest * slots, dtype=jnp.int32)[None, :]
    ).astype(bf16)
    slot_hot_frames = slot_hot[:frame_rows]
    carry_on = jnp.pad(
        (segments_now[:, 1:] == segments_now[:, :-1]).astype(f32), ((0, 0), (1, 0))
    )
    finished = jnp.pad(
        (segments_now[:, 1:] != segments_now[:, :-1]).astype(f32),
        ((0, 0), (0, 1)),
        constant_values=1.0,
    )

    def to_slots(value, kind=bf16):
        return lax.dot_general(
            slot_hot_frames,
            value.astype(bf16),
            (((0,), (0,)), ((), ())),
            preferred_element_type=f32,
        ).astype(kind)

    def to_frames(value):
        return jnp.dot(slot_hot, value.astype(bf16), preferred_element_type=f32).astype(bf16)

    def pad_frames(value):
        return jnp.pad(
            value.astype(f32).reshape(frame_rows, -1), ((0, padding), (0, 0))
        )

    previous = pad_frames(
        jnp.pad(targets_now[:, :-1], ((0, 0), (1, 0), (0, 0))).astype(f32)
        * carry_on[:, :, None]
    )
    drops_one = pad_frames(mine(drop_first))
    drops_two = pad_frames(mine(drop_second))

    zones_own = jnp.concatenate([mine(zone_first), mine(zone_second)], axis=2).astype(f32)
    zones_peer = exchange(
        jnp.concatenate([others(zone_first), others(zone_second)], axis=2).astype(f32)
    )
    zones_slots = to_slots(
        jnp.concatenate([zones_own, zones_peer], axis=2).reshape(rows * frames, -1), f32
    ).reshape(longest, slots, 4 * half)
    zone_one = jnp.concatenate(
        [zones_slots[:, :, :half], zones_slots[:, :, 2 * half : 3 * half]], axis=2
    )
    zone_two = jnp.concatenate(
        [zones_slots[:, :, half : 2 * half], zones_slots[:, :, 3 * half :]], axis=2
    )
    biases = jnp.stack([bias_first.reshape(-1), bias_second.reshape(-1)])
    biases = jnp.concatenate([biases, exchange(biases)], axis=1)
    text_ends = jnp.cumsum(mine(text_lengths), axis=1)
    owner = jnp.sum(
        (jnp.arange(text_width, dtype=jnp.int32)[None, :, None] >= text_ends[:, None, :]).astype(
            jnp.int32
        ),
        axis=2,
    )
    owner_slot = owner * rows + jnp.arange(rows, dtype=jnp.int32)[:, None]
    owner_hot = (
        owner_slot.reshape(-1, 1) == jnp.arange(lanes, dtype=jnp.int32)[None, :]
    ).astype(f32)
    conv_float = location_conv.astype(f32)
    dense_float = location_dense.astype(f32)
    reach = location_conv.shape[2] // 2
    taps_first = jnp.transpose(conv_float, (1, 2, 0))
    taps_first = jnp.pad(
        taps_first,
        ((0, 0), (0, lanes - taps_first.shape[1]), (0, lanes - taps_first.shape[2])),
    )
    dense_wide = jnp.pad(dense_float, ((0, lanes - dense_float.shape[0]), (0, 0)))
    taps_forward = jnp.roll(taps_first[:, ::-1], reach, axis=1)
    taps_back = jnp.roll(taps_first, 1 - reach, axis=1)
    frame_wide = jnp.pad(
        frame_weight.astype(f32), ((0, 0), (0, lanes - frame_weight.shape[1]))
    )
    frame_bias_wide = jnp.pad(frame_bias, (0, lanes - frame_bias.shape[0]))[None, :]
    vector_float = energy_vector.astype(f32)
    vector_wide = jnp.broadcast_to(vector_float[:, None], (attention_width, lanes))
    memory_float = memory_now.astype(f32)
    query_float = query_weight.astype(f32)
    unit_array = unit.astype(jnp.int32).reshape(1)

    targets_all = jnp.transpose(frame_info[:, :, :mel_width].astype(f32), (1, 0, 2))
    segments_all = jnp.transpose(frame_info[:, :, mel_width].astype(jnp.int32))
    padded = jnp.pad(segments_all, ((2, 2), (0, 0)), constant_values=-1)
    same = jnp.stack([padded[offset : offset + frames] == segments_all for offset in range(5)])
    same = jnp.moveaxis(same, 0, 2)
    first_full = whole(post_first, 2)
    last_full = whole(last_half, 2)
    middle_gain = whole(middle_norm, 2)
    last_gain = whole(last_norm, 1)
    loss_scale = 2.0 / (mel_width * total_rows)
    count = total_rows * frames
    channels = middle_norm.shape[2] * 2
    masks = jnp.broadcast_to(
        jnp.transpose(same, (2, 0, 1)).reshape(5, count, 1).astype(bf16), (5, count, lanes)
    )
    wide_gain = jnp.pad(last_gain, ((0, 0), (0, channels - mel_width)))
    norms = jnp.concatenate([middle_gain, wide_gain[:, None, :]], axis=1)[:, :, None, :]
    forward_small = (
        previous,
        drops_one,
        drops_two,
        prenet_first.astype(f32),
        prenet_second.astype(f32),
        slot_hot.astype(f32),
        zone_one,
        zone_two,
        biases[0:1],
        biases[1:2],
        owner_hot,
        memory_float,
        memory_weight.astype(f32),
        query_float,
        vector_wide,
        taps_forward,
        dense_wide,
        frame_wide,
        frame_bias_wide,
    )
    (
        own_one,
        own_two,
        forward_small,
        taps_back,
        vector_row,
        targets_all,
        masks,
        first_full,
        last_full,
        norms,
    ) = lax.optimization_barrier(
        (
            own_one,
            own_two,
            forward_small,
            taps_back,
            vector_float[None, :],
            targets_all,
            masks,
            first_full,
            last_full,
            norms,
        )
    )
    weights = (own_one, exchange(own_one), own_two, peer_two)
    slot_wide, zone_one, zone_two = forward_small[5], forward_small[6], forward_small[7]
    memory_float, query_float = forward_small[11], forward_small[13]
    dense_wide, frame_wide = forward_small[16], forward_small[17]

    (
        gates_one,
        gates_two,
        prior_one,
        prior_two,
        round_one,
        round_two,
        contexts,
        mixed_all,
        alphas,
        taps,
        mixed_one,
        mixed_two,
        hidden_round,
        prenet_round,
        frame_out,
    ) = call_forward(
        unit_array,
        weights,
        forward_small,
        (
            longest,
            slots,
            hidden,
            memory_width,
            rows * text_width,
            frame_rows + padding,
            prenet_width,
        ),
    )

    middle_half = lax.optimization_barrier((middle_half, frame_out))[0]
    middle_peer = exchange(middle_half)
    states = to_frames(
        jnp.concatenate([round_one, contexts, round_two], axis=2).reshape(longest * slots, -1)
    )
    frame_in = jnp.concatenate(
        [states[:, hidden + memory_width :], states[:, hidden : hidden + memory_width]], axis=1
    )
    frame_in = frame_in[:frame_rows]
    frame_out = frame_out[:frame_rows]
    mel_own = frame_out[:, :mel_width].reshape(rows, frames, mel_width)
    stop_logit = frame_out[:, mel_width].reshape(rows, frames)
    mel_all = jnp.transpose(
        gather_rows(mel_own), (1, 0, 2)
    )
    inputs_own = jnp.concatenate([prenet_round.astype(bf16), states], axis=1)
    roomy = total_rows * frames <= 2048
    if roomy:
        inputs_own, mel_all = lax.optimization_barrier((inputs_own, mel_all))
        inputs_all = lax.all_gather(inputs_own, "batch", axis=0, tiled=True)

    if roomy:
        (
            inputs_first,
            inputs_later,
            grads_early,
            grads_last,
            norm_grads,
            grad_mel,
        ) = call_postnet(
            unit_array,
            (
                mel_all.reshape(count, mel_width),
                targets_all.reshape(count, mel_width),
                masks,
                first_full,
                middle_half,
                middle_peer,
                last_full,
                norms[0],
                norms[1],
            ),
            loss_scale,
            total_rows,
        )
        gain_grads = [norm_grads[0, layer, 0] for layer in range(5)]
        shift_grads = [norm_grads[1, layer, 0] for layer in range(5)]
        gain_grads[4], shift_grads[4] = gain_grads[4][:mel_width], shift_grads[4][:mel_width]
        grad_mel = jnp.transpose(
            lax.dynamic_slice_in_dim(
                grad_mel.reshape(frames, total_rows, mel_width), place * rows, rows, 1
            ),
            (1, 0, 2),
        )
    else:
        middle_full = whole(middle_half, 2).reshape(post_middle.shape[:2] + (channels, channels))
        kernels = [first_full, middle_full[0], middle_full[1], middle_full[2], last_full]
        gains = [middle_gain[0, layer] for layer in range(4)] + [last_gain[0]]
        shifts = [middle_gain[1, layer] for layer in range(4)] + [last_gain[1]]
        layer_in = mel_all.astype(bf16)
        layer_inputs, normed_all, inverses = [], [], []
        output = None
        for layer in range(5):
            layer_inputs.append(layer_in)
            pre_norm = by_rows(
                lambda source, same_now: post_layer(source, kernels[layer], same_now),
                roomy,
                (layer_in, same),
            )
            mean_now = jnp.sum(pre_norm, axis=(0, 1)) / frame_count
            centered = pre_norm - mean_now
            inverse = lax.rsqrt(jnp.sum(centered * centered, axis=(0, 1)) / frame_count + norm_eps)
            normed = centered * inverse
            output = normed * gains[layer] + shifts[layer]
            normed_all.append(normed)
            inverses.append(inverse)
            if layer < 4:
                layer_in = jnp.tanh(output).astype(bf16)
                if not roomy:
                    layer_in, normed_all[layer] = lax.optimization_barrier(
                        (layer_in, normed_all[layer])
                    )

        grad_post = loss_scale * (mel_all + output - targets_all)
        kernel_grads, gain_grads, shift_grads = [None] * 5, [None] * 5, [None] * 5
        grad_output = grad_post
        grad_input = None
        for layer in (4, 3, 2, 1, 0):
            if layer < 4:
                normed_all[layer] = lax.optimization_barrier(normed_all[layer])
                active = jnp.tanh(normed_all[layer] * gains[layer] + shifts[layer])
                grad_output = grad_input * (1.0 - active * active)
            shift_grads[layer] = jnp.sum(grad_output, axis=(0, 1))
            gain_grads[layer] = jnp.sum(grad_output * normed_all[layer], axis=(0, 1))
            grad_norm = (
                gains[layer]
                * inverses[layer]
                * (
                    grad_output
                    - shift_grads[layer] / frame_count
                    - normed_all[layer] * (gain_grads[layer] / frame_count)
                )
            ).astype(bf16)
            grad_input = by_rows(
                lambda grad, same_now: post_layer_back(grad, kernels[layer], same_now),
                roomy,
                (grad_norm, same),
            )
            source = layer_inputs[layer]
            if layer > 0:
                source = lax.dynamic_slice_in_dim(source, place * channel_rows, channel_rows, 2)
            kernel_grads[layer] = by_rows(post_kernel_grad, roomy, (source, grad_norm, same), True)
            kernel_grads[layer] = kernel_grads[layer].reshape(5, source.shape[2], -1)
            if not roomy:
                grad_input, kernel_grads[layer] = lax.optimization_barrier(
                    (grad_input, kernel_grads[layer])
                )
        grad_mel = loss_scale * (mel_all - targets_all) + grad_post + grad_input
        grad_mel = jnp.transpose(
            lax.dynamic_slice_in_dim(grad_mel, place * rows, rows, 1), (1, 0, 2)
        )

    if not roomy:
        inputs_own, grad_mel = lax.optimization_barrier((inputs_own, grad_mel))
        inputs_all = lax.all_gather(inputs_own, "batch", axis=0, tiled=True)

    def add_units(value, axis):
        width = value.shape[axis] // 2
        halves = [
            lax.slice_in_dim(value, start, start + width, axis=axis) for start in (0, width)
        ]
        keep = jnp.where(first_unit, halves[0], halves[1])
        give = jnp.where(first_unit, halves[1], halves[0])
        return keep + exchange(give)

    grad_stop = (jax.nn.sigmoid(stop_logit) - finished) / total_rows
    grad_frame = (
        jnp.concatenate([grad_mel, grad_stop[:, :, None]], axis=2)
        .reshape(rows * frames, mel_width + 1)
        .astype(bf16)
    )
    frame_weight_grad = lax.dot_general(
        frame_in, grad_frame, (((0,), (0,)), ((), ())), preferred_element_type=f32
    )
    frame_bias_grad = jnp.sum(grad_frame.astype(f32), axis=0)
    grad_frame_slots = to_slots(
        jnp.pad(grad_frame, ((0, 0), (0, lanes - mel_width - 1))), f32
    ).reshape(longest, slots, lanes)

    (
        sent,
        prenet_back,
        context_grads,
        query_back,
        processed_back,
        vector_back,
        filter_back,
    ) = call_backward(
        unit_array,
        weights,
        (
            gates_one,
            gates_two,
            prior_one,
            prior_two,
            zone_one,
            zone_two,
            owner_hot,
            memory_float,
            query_float,
            vector_row,
            taps_back,
            dense_wide,
            mixed_all,
            alphas,
            taps,
            grad_frame_slots,
            frame_wide,
            slot_wide,
        ),
    )

    bias_sums = jnp.transpose(
        jnp.sum(sent.astype(f32), axis=1).reshape(-1, 4, lanes), (1, 0, 2)
    ).reshape(-1, lanes)
    slice_width = 2 * hidden // batch_size
    if slice_width != lanes:
        sent = sent.reshape(sent.shape[0], sent.shape[1], 4, -1, slice_width)
        sent = jnp.transpose(sent, (0, 3, 1, 2, 4)).reshape(batch_size, sent.shape[1], -1)
    received = lax.all_to_all(sent, "batch", 0, 0, tiled=True)
    grad_prenet = lax.dot_general(
        slot_hot.astype(f32),
        prenet_back.reshape(longest * slots, prenet_width),
        (((1,), (0,)), ((), ())),
        precision=precise,
    )

    def silu_back(grad, mixed, drops):
        gate = jax.nn.sigmoid(mixed)
        return grad * drops * 2.0 * gate * (1.0 + mixed * (1.0 - gate))

    def exact(a, b, contract):
        return lax.dot_general(
            a.astype(f32), b.astype(f32), (contract, ((), ())), precision=precise
        )

    grad_mixed_two = silu_back(grad_prenet, mixed_two, drops_two)
    prenet_second_grad = exact(hidden_round, grad_mixed_two, ((0,), (0,)))
    grad_hidden = exact(grad_mixed_two, prenet_second, ((1,), (1,)))
    grad_mixed_one = silu_back(grad_hidden, mixed_one, drops_one)
    prenet_first_grad = exact(previous, grad_mixed_one, ((0,), (0,)))

    query_weight_grad = exact(
        round_one.reshape(longest * slots, hidden),
        query_back.reshape(longest * slots, attention_width),
        ((0,), (0,)),
    )
    processed_round = processed_back.astype(bf16)
    memory_weight_grad = lax.dot_general(
        memory_now, processed_round, (((0,), (0,)), ((), ())), preferred_element_type=f32
    )
    filter_grads = jnp.roll(filter_back, -reach, axis=1)[:, ::-1][:, : location_conv.shape[2]]
    conv_grad = jnp.einsum("cka,fa->fck", filter_grads, dense_float, precision=precise)
    dense_grad = jnp.einsum("cka,fck->fa", filter_grads, conv_float, precision=precise)

    def two_columns(value):
        return jnp.concatenate([value[:, :lanes], value[:, lanes:]], axis=0)

    def to_lanes(value):
        return jnp.pad(value, ((0, 0), (0, lanes - value.shape[1])))

    filter_count, _, tap_count = location_conv.shape
    packed = [
        two_columns(prenet_first_grad),
        two_columns(prenet_second_grad),
        query_weight_grad,
        memory_weight_grad,
        to_lanes(frame_weight_grad),
        to_lanes(conv_grad.reshape(filter_count, -1)),
        dense_grad,
        bias_sums,
        vector_back,
        to_lanes(frame_bias_grad[None, :]),
    ]
    heights = [value.shape[0] for value in packed]
    shares = 2 * batch_size
    surplus = -sum(heights) % (8 * shares)
    packed = jnp.concatenate(packed + [jnp.zeros((surplus, lanes), f32)], axis=0)
    packed = add_units(packed, 0)
    received, packed = lax.optimization_barrier((received, packed))

    segments_rows = segments_all.T
    carried = jnp.pad(
        (segments_rows[:, 1:] == segments_rows[:, :-1]).astype(bf16), ((0, 0), (0, 1))
    ).reshape(batch_size, frame_rows)
    carried = jnp.pad(carried, ((0, 0), (0, padding)))
    after = jnp.pad(received[:, 1:], ((0, 0), (0, 1), (0, 0))) * carried[:, :, None]
    received = received.reshape(batch_size * (frame_rows + padding), -1)
    after = after.reshape(batch_size * (frame_rows + padding), -1)

    def product(start, width, grads):
        return lax.dot_general(
            inputs_all[:, start : start + width],
            grads,
            (((0,), (0,)), ((), ())),
            preferred_element_type=f32,
        )

    pair = 2 * slice_width
    first_part = jnp.concatenate(
        [
            product(0, prenet_width, received[:, :pair]),
            product(prenet_width + hidden, memory_width, after[:, :pair]),
            product(prenet_width, hidden, after[:, :pair]),
        ],
        axis=0,
    )
    second_part = jnp.concatenate(
        [
            product(prenet_width, hidden + memory_width, received[:, pair:]),
            product(prenet_width + hidden + memory_width, hidden, after[:, pair:]),
        ],
        axis=0,
    )
    parts = jnp.concatenate(
        [
            first_part.reshape(batch_size, depth_one, pair),
            second_part.reshape(batch_size, depth_two, pair),
        ],
        axis=1,
    )
    parts = add_units(parts, 2).astype(bf16)
    depth_both = depth_one + depth_two
    parts = jnp.concatenate(
        [parts, packed.astype(bf16).reshape(batch_size, -1, slice_width)], axis=1
    )
    if roomy:
        (
            parts,
            inputs_first,
            inputs_later,
            grads_early,
            grads_last,
            alphas,
            context_grads,
            processed_round,
        ) = lax.optimization_barrier(
            (
                parts,
                inputs_first,
                inputs_later,
                grads_early,
                grads_last,
                alphas,
                context_grads,
                processed_round,
            )
        )
        kernel_grads = []
        for layer in range(5):
            if layer == 0:
                source = inputs_first
            else:
                source = lax.dynamic_slice_in_dim(
                    inputs_later[layer - 1], place * channel_rows, channel_rows, 1
                )
            grad_norm = grads_early[layer] if layer < 4 else grads_last
            kernel_grads.append(
                post_kernel_grad(
                    source.reshape(frames, total_rows, -1),
                    grad_norm.reshape(frames, total_rows, -1),
                    same,
                ).reshape(5, source.shape[1], grad_norm.shape[1])
            )
    parts = lax.all_to_all(parts, "batch", 0, 0, tiled=True)
    share = jnp.sum(parts[:, depth_both:].astype(f32), axis=0)
    parts = parts[:, :depth_both].astype(f32)
    parts = jnp.transpose(parts, (1, 0, 2)).reshape(depth_both, 4, half)

    memory_grad = lax.dot_general(
        processed_round, memory_weight, (((1,), (1,)), ((), ())), preferred_element_type=f32
    )
    for step in range(longest):
        memory_grad = memory_grad + exact(
            alphas[step][:, :slots], context_grads[step], ((1,), (0,))
        )
    memory_grad = memory_grad.reshape(rows, text_width, memory_width)
    memory_grads = jnp.stack(ordered(memory_grad, exchange(memory_grad)))
    post_first_grad = add_units(kernel_grads[0], 2)
    post_middle_grad = add_units(jnp.stack(kernel_grads[1:4]), 3)
    post_last_grad = add_units(kernel_grads[4], 2)
    middle_norm_grad = add_units(
        jnp.stack([jnp.stack(gain_grads[:4]), jnp.stack(shift_grads[:4])]), 2
    )
    last_norm_grad = add_units(jnp.stack([gain_grads[4], shift_grads[4]]), 1)

    packed = whole(gather_rows(share).reshape(-1, lanes), 0)
    small, start = [], 0
    for height in heights:
        small.append(packed[start : start + height])
        start += height

    def from_columns(value):
        tall = value.shape[0] // 2
        return jnp.concatenate([value[:tall], value[tall:]], axis=1)

    biases_grad = small[7].reshape(2, 2, -1)
    biases_grad = jnp.where(first_unit, biases_grad[:, 0], biases_grad[:, 1])
    biases_grad = biases_grad.reshape(2, 4, half)
    small = [
        from_columns(small[0]),
        from_columns(small[1]),
        small[2],
        small[3],
        small[5][:, : 2 * tap_count].reshape(filter_count, 2, tap_count),
        small[6],
        small[8][0],
        small[4][:, : mel_width + 1],
        small[9][0, : mel_width + 1],
    ]
    return (
        small[0],
        small[1],
        small[2],
        small[3],
        small[4],
        small[5],
        small[6],
        parts[:depth_one],
        biases_grad[0],
        parts[depth_one:],
        biases_grad[1],
        small[7],
        small[8],
        post_first_grad,
        post_middle_grad,
        post_last_grad,
        middle_norm_grad,
        last_norm_grad,
        memory_grads,
    )


def solution(mesh):
    in_specs = (
        P(None, "batch", None, None),
        P(None, "batch", None, None),
        P(None, "batch", None),
        P(None, "batch", None),
        P(None, "batch", None, "unit"),
        P(None, "batch", None, "unit"),
        P(None, "batch", None, None),
        P(None, "batch", None, None),
        P(),
        P(),
        P(),
        P(),
        P(),
        P(),
        P(),
        P("batch", None, "unit"),
        P(None, "unit"),
        P("batch", None, "unit"),
        P(None, "unit"),
        P(),
        P(),
        P(None, None, "unit"),
        P(None, None, "batch", "unit"),
        P(None, "batch", "unit"),
        P(None, None, "unit"),
        P(None, "unit"),
    )
    out_specs = (
        P(),
        P(),
        P(),
        P(),
        P(),
        P(),
        P(),
        P("batch", None, "unit"),
        P(None, "unit"),
        P("batch", None, "unit"),
        P(None, "unit"),
        P(),
        P(),
        P(None, None, "unit"),
        P(None, None, "batch", "unit"),
        P(None, "batch", "unit"),
        P(None, None, "unit"),
        P(None, "unit"),
        P(None, "batch", None, None),
    )
    return jax.shard_map(
        on_device, mesh=mesh, in_specs=in_specs, out_specs=out_specs, check_vma=False
    )
```

profile of v0, /device:TPU:1, one launch (start us, length us, event | category | flops | bytes accessed | tf_op | source)
XLA Modules:
  0.0 651.3 jit_solution(13288360745935127657)
XLA Ops:
  35.7 2.9 collective-permute-done.7
  44.2 7.0 %collective-permute-done.3 = f32[24,6,81]{0,2,1:T(8,128)S(1)} collective-permute-done((f32[24,6,81]{0,2,1:T(8,128)S(1)}, f32[24,6,81]{0,2,1:T(8,128)S(1)}, u32[]{:S(2)}, u32[]{:S(2)}) %collective-permute-start.3) | collective-permute-done | bytes 46688 | tf_op jit(solution)/shard_map/ppermute | solution.py:988
  57.6 95.0 %all-gather.7.cloned.1.call-done.own_two = bf16[16,2560,128]{2,1,0:T(8,128)(2,1)} async-done(((bf16[16,160,128]{2,1,0:T(8,128)(2,1)}), bf16[16,2560,128]{2,1,0:T(8,128)(2,1)}) %all-gather.7.cloned.1.call-update) | async-done | bytes 10485776 | tf_op jit(solution)/shard_map/all_gather | solution.py:1001
  162.3 17.2 %collective-permute-done.5 = f32[96,6,81]{0,2,1:T(8,128)S(1)} collective-permute-done((f32[96,6,81]{0,2,1:T(8,128)S(1)}, f32[96,6,81]{0,2,1:T(8,128)S(1)}, u32[]{:S(2)}, u32[]{:S(2)}) %collective-permute-start.5) | collective-permute-done | bytes 186656 | tf_op jit(solution)/shard_map/ppermute | solution.py:988
  183.3 77.9 %all-gather.5.cloned.1.call-done.own_one = bf16[16,1792,128]{2,1,0:T(8,128)(2,1)} async-done(((bf16[16,112,128]{2,1,0:T(8,128)(2,1)}), bf16[16,1792,128]{2,1,0:T(8,128)(2,1)}) %all-gather.5.cloned.1.call-update) | async-done | bytes 7340048 | tf_op jit(solution)/shard_map/all_gather | solution.py:1001
  264.8 11.6 %collective-permute-done.14.peer_one = bf16[16,1792,128]{2,1,0:T(8,128)(2,1)} collective-permute-done((bf16[16,1792,128]{2,1,0:T(8,128)(2,1)}, bf16[16,1792,128]{2,1,0:T(8,128)(2,1)}, u32[]{:S(2)}, u32[]{:S(2)}) %collective-permute-start.14) | collective-permute-done | bytes 7340064 | tf_op jit(solution)/shard_map/ppermute | solution.py:972
  276.4 39.8 %decoder_forward.1 = (f32[3,48,4096]{2,1,0:T(8,128)}, f32[3,48,4096]{2,1,0:T(8,128)}, f32[3,48,1024]{2,1,0:T(8,128)}, f32[3,48,1024]{2,1,0:T(8,128)}, f32[3,48,1...) custom-call(s32[1]{0:T(128)} %bitcast.unit_ref, ...), custom_call_target="tpu_custom_call" | custom-call | tf_op jit(solution)/shard_map/decoder_forward/pallas_call | solution.py:562
  323.1 4.0 collective-permute-done.17
  327.9 11.7 %collective-permute-done.18 = f32[48,6,80]{2,0,1:T(8,128)S(1)} collective-permute-done((f32[48,6,80]{2,0,1:T(8,128)S(1)}, f32[48,6,80]{2,0,1:T(8,128)S(1)}, u32[]{:S(2)}, u32[]{:S(2)}) %collective-permute-start.18) | collective-permute-done | bytes 92192 | tf_op jit(solution)/shard_map/ppermute | solution.py:988
  340.5 14.2 %collective-permute-done.19 = f32[96,6,80]{2,0,1:T(8,128)S(1)} collective-permute-done((f32[96,6,80]{2,0,1:T(8,128)S(1)}, f32[96,6,80]{2,0,1:T(8,128)S(1)}, u32[]{:S(2)}, u32[]{:S(2)}) %collective-permute-start.19) | collective-permute-done | bytes 184352 | tf_op jit(solution)/shard_map/ppermute | solution.py:988
  358.6 4.5 collective-permute-done.20.peer_ref
  363.0 56.7 %postnet.1 = (bf16[1152,80]{1,0:T(8,128)(2,1)}, bf16[4,1152,512]{2,1,0:T(8,128)(2,1)}, bf16[4,1152,512]{2,1,0:T(8,128)(2,1)}, bf16[1152,80]{1,0:T(8,128)(2,1)}, ...) custom-call(s32[1]{0:T(128)} %bitcast.unit_ref, f32[1152,80]{1,0:T(8,128)} %bitcast.271, f32[1152,80]{1,0:T(8,128)} %bitcast.272, ...), custom_call_target="tpu_custom_call" | custom-call | tf_op jit(solution)/shard_map/postnet/pallas_call | solution.py:861
  421.6 57.8 %decoder_backward.1 = (bf16[16,80,512]{2,1,0:T(8,128)(2,1)}, f32[3,48,256]{2,1,0:T(8,128)}, f32[3,48,512]{2,1,0:T(8,128)}, f32[3,48,128]{2,1,0:T(8,128)}, f32[76...) custom-call(s32[1]{0:T(128)} %bitcast.unit_ref, ...), custom_call_target="tpu_custom_call" | custom-call | tf_op jit(solution)/shard_map/decoder_backward/pallas_call | solution.py:608
  481.1 5.2 all-to-all-start
  493.0 2.4 concatenate.209
  501.9 11.3 %all-to-all-done = bf16[16,80,512]{2,1,0:T(8,128)(2,1)} async-done(((bf16[16,80,512]{2,1,0:T(8,128)(2,1)}), bf16[16,80,512]{2,1,0:T(8,128)(2,1)}, u32[]{:S(2)}, u32[]{:S(2)}) %all-to-all-start) | async-done | bytes 1310752 | tf_op jit(solution)/shard_map/all_to_all | solution.py:1400
  515.4 2.8 fusion.2
  526.4 3.4 collective-permute-start.22
  530.6 3.1 collective-permute-done.32
  534.9 2.8 add_convert_fusion
  539.0 7.1 %all-to-all-start.1 = ((bf16[16,400,128]{2,1,0:T(8,128)(2,1)}), bf16[16,400,128]{2,1,0:T(8,128)(2,1)S(1)}, u32[]{:S(2)}, u32[]{:S(2)}) async-start(bf16[16,400,128]{2,1,0:T(8,128)(2,1)} %pad_maximum_fusion.4), calls=%async_computation.1 | async-start | bytes 3276800 | tf_op jit(solution)/shard_map/all_to_all | solution.py:1545
  546.3 4.2 fusion.122
  552.9 2.6 fusion.121
  565.1 2.8 add_add_fusion
  568.0 11.6 %all-to-all-done.1 = bf16[16,400,128]{2,1,0:T(8,128)(2,1)S(1)} async-done(((bf16[16,400,128]{2,1,0:T(8,128)(2,1)}), bf16[16,400,128]{2,1,0:T(8,128)(2,1)S(1)}, u32[]{:S(2)}, u32[]{:S(2)}) %all-to-all-start.1) | async-done | bytes 1638432 | tf_op jit(solution)/shard_map/all_to_all | solution.py:1545
  582.8 2.5 collective-permute-start.24
  587.8 4.7 collective-permute-start.25
  593.0 3.2 collective-permute-done.25
  596.4 2.9 collective-permute-start.26
  599.3 7.0 %collective-permute-start.29 = (f32[3,5,32,256]{3,2,1,0:T(8,128)S(1)}, f32[3,5,32,256]{3,2,1,0:T(8,128)S(1)}, u32[]{:S(2)}, u32[]{:S(2)}) collective-permute-start(f32[3,5,32,256]{3,2,1,0:T(8,128)S(1)} %slice_select_fusion.1), channel_id=1, source_target_pairs={{0,1},{1,0},{2,3},{3,2},{4,5},{5,4},{6,7},{7,6},{8,9},{9,8},{10,11... | collective-permute-start | bytes 1474568 | tf_op jit(solution)/shard_map/ppermute | solution.py:972
  608.9 11.4 %collective-permute-done.26 = f32[1024,128]{1,0:T(8,128)S(1)} collective-permute-done((f32[1024,128]{1,0:T(8,128)S(1)}, f32[1024,128]{1,0:T(8,128)S(1)}, u32[]{:S(2)}, u32[]{:S(2)}) %collective-permute-start.26) | collective-permute-done | bytes 524320 | tf_op jit(solution)/shard_map/ppermute | solution.py:988
  621.5 3.1 collective-permute-start.27
  (520 shorter events, 140.8 us)
Async XLA Ops:
  7.2 145.4 %all-gather.7.cloned.1.call-start = ((), (), s32[]{:S(2)}) async-start(), calls=%async_computation.3 | async-start | bytes 11141120 | tf_op jit(solution)/shard_map/all_gather | solution.py:1001
  10.0 251.1 %all-gather.5.cloned.1.call-start = ((), (), s32[]{:S(2)}) async-start(), calls=%async_computation.2 | async-start | bytes 7798784 | tf_op jit(solution)/shard_map/all_gather | solution.py:1001
  11.2 344.5 %all-gather.11.cloned.1.call-start = ((), (), s32[]{:S(2)}) async-start(), calls=%async_computation.5 | async-start | bytes 4177920 | tf_op jit(solution)/shard_map/all_gather | solution.py:1008
  13.1 42.4 %collective-permute-start = (bf16[12,6,1024]{2,1,0:T(8,128)(2,1)}, bf16[12,6,1024]{2,1,0:T(8,128)(2,1)}, u32[]{:S(2)}, u32[]{:S(2)}) collective-permute-start(bf16[12,6,1024]{2,1,0:T(8,128)(2,1)} %add_convert_fusion.1), channel_id=1, source_target_pairs={{0,1},{1,0},{2,3},{3,2},{4,5},{5,4},{6,7},{7,6},{8,9},{9,8},{10,11... | collective-permute-start | bytes 442376 | tf_op jit(solution)/shard_map/ppermute | solution.py:972
  13.9 26.1 %collective-permute-start.1 = (f32[2,2048]{1,0:T(2,128)}, f32[2,2048]{1,0:T(2,128)}, u32[]{:S(2)}, u32[]{:S(2)}) collective-permute-start(f32[2,2048]{1,0:T(2,128)} %pad_maximum_fusion.37), channel_id=1, source_target_pairs={{0,1},{1,0},{2,3},{3,2},{4,5},{5,4},{6,7},{7,6},{8,9},{9,8},{10,11... | collective-permute-start | bytes 49160 | tf_op jit(solution)/shard_map/ppermute | solution.py:972
  14.7 26.7 %collective-permute-start.2 = (f32[12,6,81]{0,2,1:T(8,128)S(1)}, f32[12,6,81]{0,2,1:T(8,128)}, u32[]{:S(2)}, u32[]{:S(2)}) collective-permute-start(f32[12,6,81]{0,2,1:T(8,128)S(1)} %maximum_convert_fusion), channel_id=1, source_target_pairs={{0,2},{2,0},{4,6},{6,4},{8,10},{10,8},{12,14},{14,12},{16,18},{18,... | collective-permute-start | bytes 69992 | tf_op jit(solution)/shard_map/ppermute | solution.py:988
  16.9 143.5 %collective-permute-start.6 = (bf16[5,80,256]{2,1,0:T(8,128)(2,1)}, bf16[5,80,256]{2,1,0:T(8,128)(2,1)}, u32[]{:S(2)}, u32[]{:S(2)}) collective-permute-start(bf16[5,80,256]{2,1,0:T(8,128)(2,1)} %param.47), channel_id=1, source_target_pairs={{0,1},{1,0},{2,3},{3,2},{4,5},{5,4},{6,7},{7,6},{8,9},{9,8},{10,11... | collective-permute-start | bytes 614408 | tf_op jit(solution)/shard_map/ppermute | solution.py:972
  17.7 16.5 %collective-permute-start.13 = (f32[2,40]{1,0:T(2,128)S(1)}, f32[2,40]{1,0:T(2,128)S(1)}, u32[]{:S(2)}, u32[]{:S(2)}) collective-permute-start(f32[2,40]{1,0:T(2,128)S(1)} %copy-done.71), channel_id=1, source_target_pairs={{0,1},{1,0},{2,3},{3,2},{4,5},{5,4},{6,7},{7,6},{8,9},{9,8},{10,11... | collective-permute-start | bytes 968 | tf_op jit(solution)/shard_map/ppermute | solution.py:972
  42.5 8.7 %collective-permute-start.3 = (f32[24,6,81]{0,2,1:T(8,128)S(1)}, f32[24,6,81]{0,2,1:T(8,128)S(1)}, u32[]{:S(2)}, u32[]{:S(2)}) collective-permute-start(f32[24,6,81]{0,2,1:T(8,128)S(1)} %pad_maximum_fusion.15), channel_id=1, source_target_pairs={{0,4},{2,6},{4,0},{6,2},{8,12},{10,14},{12,8},{14,10},{16,20},{18,... | collective-permute-start | bytes 139976 | tf_op jit(solution)/shard_map/ppermute | solution.py:988
  42.8 10.7 %collective-permute-start.9 = (bf16[128,200]{1,0:T(8,128)(2,1)S(1)}, bf16[128,200]{1,0:T(8,128)(2,1)S(1)}, u32[]{:S(2)}, u32[]{:S(2)}) collective-permute-start(bf16[128,200]{1,0:T(8,128)(2,1)S(1)} %pad_maximum_fusion.31), channel_id=1, source_target_pairs={{0,8},{2,10},{4,12},{6,14},{8,0},{10,2},{12,4},{14,6},{16,24},{18,... | collective-permute-start | bytes 153608 | tf_op jit(solution)/shard_map/ppermute | solution.py:988
  52.2 103.8 %collective-permute-start.4 = (f32[48,6,81]{0,2,1:T(8,128)}, f32[48,6,81]{0,2,1:T(8,128)}, u32[]{:S(2)}, u32[]{:S(2)}) collective-permute-start(f32[48,6,81]{0,2,1:T(8,128)} %pad_maximum_fusion.16), channel_id=1, source_target_pairs={{0,8},{2,10},{4,12},{6,14},{8,0},{10,2},{12,4},{14,6},{16,24},{18,... | collective-permute-start | bytes 279944 | tf_op jit(solution)/shard_map/ppermute | solution.py:988
  54.3 104.4 %collective-permute-start.10 = (bf16[256,200]{1,0:T(8,128)(2,1)}, bf16[256,200]{1,0:T(8,128)(2,1)}, u32[]{:S(2)}, u32[]{:S(2)}) collective-permute-start(bf16[256,200]{1,0:T(8,128)(2,1)} %pad_maximum_fusion.27), channel_id=1, source_target_pairs={{0,16},{2,18},{4,20},{6,22},{8,24},{10,26},{12,28},{14,30},{16,0},... | collective-permute-start | bytes 307208 | tf_op jit(solution)/shard_map/ppermute | solution.py:988
  152.6 123.7 %collective-permute-start.15 = (bf16[16,2560,128]{2,1,0:T(8,128)(2,1)}, bf16[16,2560,128]{2,1,0:T(8,128)(2,1)}, u32[]{:S(2)}, u32[]{:S(2)}) collective-permute-start(bf16[16,2560,128]{2,1,0:T(8,128)(2,1)} %all-gather.7.cloned.1.call-done.own_two), channel_id=1, source_target_pairs={{0,1},{1,0},{2,3},{3,2},{4,5},{5,4},{6,7},{7,6},{8,9},{9,8},{10,11... | collective-permute-start | bytes 31457288 | tf_op jit(solution)/shard_map/ppermute | solution.py:972
  157.3 22.2 %collective-permute-start.5 = (f32[96,6,81]{0,2,1:T(8,128)S(1)}, f32[96,6,81]{0,2,1:T(8,128)S(1)}, u32[]{:S(2)}, u32[]{:S(2)}) collective-permute-start(f32[96,6,81]{0,2,1:T(8,128)S(1)} %pad_maximum_fusion.17), channel_id=1, source_target_pairs={{0,16},{2,18},{4,20},{6,22},{8,24},{10,26},{12,28},{14,30},{16,0},... | collective-permute-start | bytes 559880 | tf_op jit(solution)/shard_map/ppermute | solution.py:988
  159.8 20.9 %collective-permute-start.11 = (bf16[5,512,40]{1,2,0:T(8,128)(2,1)S(1)}, bf16[5,512,40]{1,2,0:T(8,128)(2,1)}, u32[]{:S(2)}, u32[]{:S(2)}) collective-permute-start(bf16[5,512,40]{1,2,0:T(8,128)(2,1)S(1)} %bitcast.293), channel_id=1, source_target_pairs={{0,1},{1,0},{2,3},{3,2},{4,5},{5,4},{6,7},{7,6},{8,9},{9,8},{10,11... | collective-permute-start | bytes 614408 | tf_op jit(solution)/shard_map/ppermute | solution.py:972
  263.7 12.7 %collective-permute-start.14 = (bf16[16,1792,128]{2,1,0:T(8,128)(2,1)}, bf16[16,1792,128]{2,1,0:T(8,128)(2,1)}, u32[]{:S(2)}, u32[]{:S(2)}) collective-permute-start(bf16[16,1792,128]{2,1,0:T(8,128)(2,1)} %all-gather.5.cloned.1.call-done.own_one), channel_id=1, source_target_pairs={{0,1},{1,0},{2,3},{3,2},{4,5},{5,4},{6,7},{7,6},{8,9},{9,8},{10,11... | collective-permute-start | bytes 22020104 | tf_op jit(solution)/shard_map/ppermute | solution.py:972
  264.8 250.6 %all-gather.9.cloned.1.call-start = ((), (), s32[]{:S(2)}) async-start(), calls=%async_computation.4 | async-start | bytes 7659520 | tf_op jit(solution)/shard_map/all_gather | solution.py:1230
  321.7 5.4 collective-permute-start.17
  327.2 12.4 %collective-permute-start.18 = (f32[48,6,80]{2,0,1:T(8,128)S(1)}, f32[48,6,80]{2,0,1:T(8,128)S(1)}, u32[]{:S(2)}, u32[]{:S(2)}) collective-permute-start(f32[48,6,80]{2,0,1:T(8,128)S(1)} %pad_maximum_fusion.24), channel_id=1, source_target_pairs={{0,8},{2,10},{4,12},{6,14},{8,0},{10,2},{12,4},{14,6},{16,24},{18,... | collective-permute-start | bytes 276488 | tf_op jit(solution)/shard_map/ppermute | solution.py:988
  339.6 15.1 %collective-permute-start.19 = (f32[96,6,80]{2,0,1:T(8,128)S(1)}, f32[96,6,80]{2,0,1:T(8,128)S(1)}, u32[]{:S(2)}, u32[]{:S(2)}) collective-permute-start(f32[96,6,80]{2,0,1:T(8,128)S(1)} %pad_maximum_fusion.14), channel_id=1, source_target_pairs={{0,16},{2,18},{4,20},{6,22},{8,24},{10,26},{12,28},{14,30},{16,0},... | collective-permute-start | bytes 552968 | tf_op jit(solution)/shard_map/ppermute | solution.py:988
  355.7 7.3 %collective-permute-start.20 = (bf16[15,512,256]{2,1,0:T(8,128)(2,1)}, bf16[15,512,256]{2,1,0:T(8,128)(2,1)}, u32[]{:S(2)}, u32[]{:S(2)}) collective-permute-start(bf16[15,512,256]{2,1,0:T(8,128)(2,1)} %all-gather.11.cloned.1.call-done.own_ref), channel_id=1, source_target_pairs={{0,1},{1,0},{2,3},{3,2},{4,5},{5,4},{6,7},{7,6},{8,9},{9,8},{10,11... | collective-permute-start | bytes 11796488 | tf_op jit(solution)/shard_map/ppermute | solution.py:972
  481.1 32.1 %all-to-all-start = ((bf16[16,80,512]{2,1,0:T(8,128)(2,1)}), bf16[16,80,512]{2,1,0:T(8,128)(2,1)}, u32[]{:S(2)}, u32[]{:S(2)}) async-start(bf16[16,80,512]{2,1,0:T(8,128)(2,1)} %get-tuple-element.132), calls=%async_computation | async-start | bytes 2621440 | tf_op jit(solution)/shard_map/all_to_all | solution.py:1400
  526.4 8.5 %collective-permute-start.22 = (f32[16,272,128]{2,1,0:T(8,128)}, f32[16,272,128]{2,1,0:T(8,128)}, u32[]{:S(2)}, u32[]{:S(2)}) collective-permute-start(f32[16,272,128]{2,1,0:T(8,128)} %broadcast_select_fusion), channel_id=1, source_target_pairs={{0,1},{1,0},{2,3},{3,2},{4,5},{5,4},{6,7},{7,6},{8,9},{9,8},{10,11... | collective-permute-start | bytes 6684680 | tf_op jit(solution)/shard_map/ppermute | solution.py:972
  539.0 40.6 %all-to-all-start.1 = ((bf16[16,400,128]{2,1,0:T(8,128)(2,1)}), bf16[16,400,128]{2,1,0:T(8,128)(2,1)S(1)}, u32[]{:S(2)}, u32[]{:S(2)}) async-start(bf16[16,400,128]{2,1,0:T(8,128)(2,1)} %pad_maximum_fusion.4), calls=%async_computation.1 | async-start | bytes 3276800 | tf_op jit(solution)/shard_map/all_to_all | solution.py:1545
  552.4 54.6 %collective-permute-start.28 = (f32[5,80,256]{2,1,0:T(8,128)}, f32[5,80,256]{2,1,0:T(8,128)}, u32[]{:S(2)}, u32[]{:S(2)}) collective-permute-start(f32[5,80,256]{2,1,0:T(8,128)} %slice_select_fusion.2), channel_id=1, source_target_pairs={{0,1},{1,0},{2,3},{3,2},{4,5},{5,4},{6,7},{7,6},{8,9},{9,8},{10,11... | collective-permute-start | bytes 1228808 | tf_op jit(solution)/shard_map/ppermute | solution.py:972
  560.5 45.9 %collective-permute-start.30 = (f32[5,32,40]{2,1,0:T(8,128)S(1)}, f32[5,32,40]{2,1,0:T(8,128)S(1)}, u32[]{:S(2)}, u32[]{:S(2)}) collective-permute-start(f32[5,32,40]{2,1,0:T(8,128)S(1)} %slice_select_fusion.3), channel_id=1, source_target_pairs={{0,1},{1,0},{2,3},{3,2},{4,5},{5,4},{6,7},{7,6},{8,9},{9,8},{10,11... | collective-permute-start | bytes 76808 | tf_op jit(solution)/shard_map/ppermute | solution.py:972
  567.9 57.6 %collective-permute-start.33 = (f32[12,64,512]{2,1,0:T(8,128)}, f32[12,64,512]{2,1,0:T(8,128)}, u32[]{:S(2)}, u32[]{:S(2)}) collective-permute-start(f32[12,64,512]{2,1,0:T(8,128)} %bitcast.116), channel_id=1, source_target_pairs={{0,1},{1,0},{2,3},{3,2},{4,5},{5,4},{6,7},{7,6},{8,9},{9,8},{10,11... | collective-permute-start | bytes 4718600 | tf_op jit(solution)/shard_map/ppermute | solution.py:972
  582.8 4.9 collective-permute-start.24
  587.8 8.5 %collective-permute-start.25 = (f32[512,128]{1,0:T(8,128)S(1)}, f32[512,128]{1,0:T(8,128)S(1)}, u32[]{:S(2)}, u32[]{:S(2)}) collective-permute-start(f32[512,128]{1,0:T(8,128)S(1)} %pad_maximum_fusion.20), channel_id=1, source_target_pairs={{0,8},{2,10},{4,12},{6,14},{8,0},{10,2},{12,4},{14,6},{16,24},{18,... | collective-permute-start | bytes 786440 | tf_op jit(solution)/shard_map/ppermute | solution.py:988
  596.4 23.9 %collective-permute-start.26 = (f32[1024,128]{1,0:T(8,128)S(1)}, f32[1024,128]{1,0:T(8,128)S(1)}, u32[]{:S(2)}, u32[]{:S(2)}) collective-permute-start(f32[1024,128]{1,0:T(8,128)S(1)} %pad_maximum_fusion.11), channel_id=1, source_target_pairs={{0,16},{2,18},{4,20},{6,22},{8,24},{10,26},{12,28},{14,30},{16,0},... | collective-permute-start | bytes 1572872 | tf_op jit(solution)/shard_map/ppermute | solution.py:988
  599.3 25.3 %collective-permute-start.29 = (f32[3,5,32,256]{3,2,1,0:T(8,128)S(1)}, f32[3,5,32,256]{3,2,1,0:T(8,128)S(1)}, u32[]{:S(2)}, u32[]{:S(2)}) collective-permute-start(f32[3,5,32,256]{3,2,1,0:T(8,128)S(1)} %slice_select_fusion.1), channel_id=1, source_target_pairs={{0,1},{1,0},{2,3},{3,2},{4,5},{5,4},{6,7},{7,6},{8,9},{9,8},{10,11... | collective-permute-start | bytes 1474568 | tf_op jit(solution)/shard_map/ppermute | solution.py:972
  621.5 13.9 %collective-permute-start.27 = (f32[2048,128]{1,0:T(8,128)}, f32[2048,128]{1,0:T(8,128)}, u32[]{:S(2)}, u32[]{:S(2)}) collective-permute-start(f32[2048,128]{1,0:T(8,128)} %pad_maximum_fusion.5), channel_id=1, source_target_pairs={{0,1},{1,0},{2,3},{3,2},{4,5},{5,4},{6,7},{7,6},{8,9},{9,8},{10,11... | collective-permute-start | bytes 3145736 | tf_op jit(solution)/shard_map/ppermute | solution.py:972
  (92 other events, 469.6 us)
Sparse Core Ops, SparseCore 0:
  11.3 141.2 all-gather.6
  155.9 105.1 all-gather.4
  264.9 76.3 all-gather.10
  355.8 100.5 all-gather.8
where the time goes:
time: 660 us; the launch traced here: 651 us
  waiting for transfers between devices  293 us (44%)
  Pallas kernels  154 us (23%)
  other arithmetic  56.2 us (9%)
  starting transfers between devices  55.7 us (8%)
  local copies, waits for them, and re-layouts  52.8 us (8%)
  matrix products  23.3 us (4%)
  between operations  16.1 us (2%)
    all_gather x2, waiting for transfers between devices, gather_tiles(): return lax.all_gather(tiles, 'batch', axis=1, tiled=True)  173 us
    ppermute x16, waiting for transfers between devices, swapped(): other = lax.ppermute(value, 'batch', pairs)  75 us
    pallas_call x1, Pallas kernels, call_backward(): pl.pallas_call(backward_kernel, out_shape=outs, in_specs=[pl.BlockSpec(me...  57.8 us
    pallas_call x1, Pallas kernels, call_postnet(): pl.pallas_call(functools.partial(postnet_kernel, mel_width, loss_scale),...  56.7 us
    pallas_call x1, Pallas kernels, call_forward(): pl.pallas_call(forward_kernel, out_shape=outs, in_specs=[pl.BlockSpec(mem...  39.8 us
    ppermute x16, starting transfers between devices, swapped(): other = lax.ppermute(value, 'batch', pairs)  23.4 us
    ppermute x18, waiting for transfers between devices, exchange(): return lax.ppermute(value, 'unit', [(0, 1), (1, 0)])  22.2 us
    ppermute x18, starting transfers between devices, exchange(): return lax.ppermute(value, 'unit', [(0, 1), (1, 0)])  19.9 us
  transfers between devices with their start and end apart: 40, of which 20 were waited for; matrix products, arithmetic and copies ran while one was open for 16% of the time, Pallas kernels for 24%

commit v1 on v0

--- a/solution.py
+++ b/solution.py
@@ -152,12 +152,12 @@
 
     def gates_into(held, depth, bias_ref, out_ref, step):
         def one(block, _):
-            side = block // 4
+            side = block // 2
             inputs = input_ref[:, :depth]
-            for pair in range(per_half // 2):
-                tile = (block % 4) * per_half + 2 * pair
+            for pair in range(per_half):
+                tile = (block % 2) * 2 * per_half + 2 * pair
                 outside = pl.ds(
-                    pl.multiple_of(block * half + 2 * pair * lanes, 2 * lanes), 2 * lanes
+                    pl.multiple_of(block * 2 * half + 2 * pair * lanes, 2 * lanes), 2 * lanes
                 )
                 kernel = jnp.concatenate(
                     [held[side, tile, :depth, :], held[side, tile + 1, :depth, :]], axis=1
@@ -165,7 +165,7 @@
                 out_ref[step, :, outside] = dot(inputs, kernel) + bias_ref[:, outside]
             return 0
 
-        lax.fori_loop(0, 8, one, 0)
+        lax.fori_loop(0, 4, one, 0)
 
     def cell(gates_ref, zone_ref, prior_ref, state, cells, round_ref, step):
         def one(chunk, _):
@@ -404,7 +404,7 @@
     def inputs_back(grads_ref, held, out_ref, step, blocks):
         def one(block, _):
             spot = pl.ds(pl.multiple_of(block * 256, 256), 256)
-            total = None
+            totals = [None] * 4
             for tile in range(0, 8 * per_half, 2):
                 side, inside = tile // (4 * per_half), tile % (4 * per_half)
                 kernel = jnp.concatenate(
@@ -412,8 +412,9 @@
                 )
                 grads = grads_ref[step, :, tile * lanes : (tile + 2) * lanes]
                 product = dot(grads, kernel, lanes_both)
-                total = product if total is None else total + product
-            out_ref[:, spot] = total
+                which = tile // 2 % 4
+                totals[which] = product if totals[which] is None else totals[which] + product
+            out_ref[:, spot] = (totals[0] + totals[1]) + (totals[2] + totals[3])
             return 0
 
         lax.fori_loop(0, blocks, one, 0)
@@ -737,16 +738,17 @@
     activate(0)
 
     def middle(index, _):
-        for which, ref in ((0, own_ref), (1, peer_ref)):
-
-            def middle_chunk(start, which=which, ref=ref):
-                total = None
-                for tap in range(5):
-                    product = dot(piece(padded, start, tap, channels), ref[index * 5 + tap])
-                    total = product if total is None else total + product
-                held[pl.ds(start, chunk), pl.ds(half_spot(which), side)] = total
-
-            chunks(middle_chunk)
+        def middle_chunk(start):
+            totals = [None, None]
+            for tap in range(5):
+                value = piece(padded, start, tap, channels)
+                for which, ref in ((0, own_ref), (1, peer_ref)):
+                    product = dot(value, ref[index * 5 + tap])
+                    totals[which] = product if tap == 0 else totals[which] + product
+            for which in range(2):
+                held[pl.ds(start, chunk), pl.ds(half_spot(which), side)] = totals[which]
+
+        chunks(middle_chunk)
         activate(index + 1)
         return 0
 
@@ -989,6 +991,15 @@
         upper = (place & bit) != 0
         return jnp.where(upper, other, value), jnp.where(upper, value, other)
 
+    def gather_far_first(value):
+        inner, bit, count = value.ndim, batch_size // 2, 0
+        while bit:
+            value = jnp.stack(swapped(value, bit))
+            bit //= 2
+            count += 1
+        order = tuple(range(count - 1, -1, -1)) + tuple(range(count, count + inner))
+        return jnp.transpose(value, order).reshape((batch_size,) + value.shape[count:])
+
     def gather_rows(value):
         bit = 1
         while bit < batch_size:
@@ -1352,7 +1363,7 @@
     frame_weight_grad = lax.dot_general(
         frame_in, grad_frame, (((0,), (0,)), ((), ())), preferred_element_type=f32
     )
-    frame_bias_grad = jnp.sum(grad_frame.astype(f32), axis=0)
+    frame_bias_grad = jnp.sum(grad_frame.astype(f32), axis=0)[None, :]
     grad_frame_slots = to_slots(
         jnp.pad(grad_frame, ((0, 0), (0, lanes - mel_width - 1))), f32
     ).reshape(longest, slots, lanes)
@@ -1450,7 +1461,7 @@
         dense_grad,
         bias_sums,
         vector_back,
-        to_lanes(frame_bias_grad[None, :]),
+        to_lanes(frame_bias_grad),
     ]
     heights = [value.shape[0] for value in packed]
     shares = 2 * batch_size
@@ -1564,7 +1575,8 @@
     )
     last_norm_grad = add_units(jnp.stack([gain_grads[4], shift_grads[4]]), 1)
 
-    packed = whole(gather_rows(share).reshape(-1, lanes), 0)
+    packed = gather_far_first(share.astype(bf16)).reshape(-1, lanes)
+    packed = whole(packed, 0).astype(f32)
     small, start = [], 0
     for height in heights:
         small.append(packed[start : start + height])

time: 660 us -> 640 us (0.970)
  waiting for transfers between devices: 293 us -> 266 us
  local copies, waits for them, and re-layouts: 52.8 us -> 59.7 us
    ppermute x16, waiting for transfers between devices: 75 us -> 63.3 us  [swapped(): other = lax.ppermute(value, 'batch', pairs)]
    all_to_all x1, waiting for transfers between devices: 11.6 us -> 1.96 us  [on_device(): parts = lax.all_to_all(parts, 'batch', 0, 0, tiled=True)]
  transfers between devices with their start and end apart: 40 -> 40, of which waited for: 20 -> 19; matrix products, arithmetic and copies ran while one was open for 16% -> 18% of each run, Pallas kernels for 24% -> 24%
where the time goes in v1:
time: 640 us; the launch traced here: 631 us
  waiting for transfers between devices  266 us (42%)
  Pallas kernels  151 us (24%)
  local copies, waits for them, and re-layouts  59.7 us (9%)
  other arithmetic  58.8 us (9%)
  starting transfers between devices  54.8 us (9%)
  matrix products  25.2 us (4%)
  between operations  16.2 us (3%)
    all_gather x2, waiting for transfers between devices, gather_tiles(): return lax.all_gather(tiles, 'batch', axis=1, tiled=True)  168 us
    ppermute x16, waiting for transfers between devices, swapped(): other = lax.ppermute(value, 'batch', pairs)  63.3 us
    pallas_call x1, Pallas kernels, call_backward(): pl.pallas_call(backward_kernel, out_shape=outs, in_specs=[pl.BlockSpec(me...  58 us
    pallas_call x1, Pallas kernels, call_postnet(): pl.pallas_call(functools.partial(postnet_kernel, mel_width, loss_scale),...  55.1 us
    pallas_call x1, Pallas kernels, call_forward(): pl.pallas_call(forward_kernel, out_shape=outs, in_specs=[pl.BlockSpec(mem...  37.8 us
    ppermute x16, starting transfers between devices, swapped(): other = lax.ppermute(value, 'batch', pairs)  22.7 us
    ppermute x18, waiting for transfers between devices, exchange(): return lax.ppermute(value, 'unit', [(0, 1), (1, 0)])  21.7 us
    ppermute x18, starting transfers between devices, exchange(): return lax.ppermute(value, 'unit', [(0, 1), (1, 0)])  17.7 us
  transfers between devices with their start and end apart: 40, of which 19 were waited for; matrix products, arithmetic and copies ran while one was open for 18% of the time, Pallas kernels for 24%

profile of v1, /device:TPU:1, one launch (start us, length us, event | category | flops | bytes accessed | tf_op | source)
XLA Modules:
  0.0 631.3 jit_solution(7768024890054586939)
XLA Ops:
  14.7 2.3 collective-permute-start.2
  37.1 2.9 collective-permute-done.7
  45.5 10.7 %collective-permute-done.3 = f32[24,6,81]{0,2,1:T(8,128)S(1)} collective-permute-done((f32[24,6,81]{0,2,1:T(8,128)S(1)}, f32[24,6,81]{0,2,1:T(8,128)S(1)}, u32[]{:S(2)}, u32[]{:S(2)}) %collective-permute-start.3) | collective-permute-done | bytes 46688 | tf_op jit(solution)/shard_map/ppermute | solution.py:990
  62.9 90.1 %all-gather.7.cloned.1.call-done.own_two = bf16[16,2560,128]{2,1,0:T(8,128)(2,1)} async-done(((bf16[16,160,128]{2,1,0:T(8,128)(2,1)}), bf16[16,2560,128]{2,1,0:T(8,128)(2,1)}) %all-gather.7.cloned.1.call-update) | async-done | bytes 10485776 | tf_op jit(solution)/shard_map/all_gather | solution.py:1012
  162.7 17.2 %collective-permute-done.5 = f32[96,6,81]{0,2,1:T(8,128)S(1)} collective-permute-done((f32[96,6,81]{0,2,1:T(8,128)S(1)}, f32[96,6,81]{0,2,1:T(8,128)S(1)}, u32[]{:S(2)}, u32[]{:S(2)}) %collective-permute-start.5) | collective-permute-done | bytes 186656 | tf_op jit(solution)/shard_map/ppermute | solution.py:990
  183.6 77.9 %all-gather.5.cloned.1.call-done.own_one = bf16[16,1792,128]{2,1,0:T(8,128)(2,1)} async-done(((bf16[16,112,128]{2,1,0:T(8,128)(2,1)}), bf16[16,1792,128]{2,1,0:T(8,128)(2,1)}) %all-gather.5.cloned.1.call-update) | async-done | bytes 7340048 | tf_op jit(solution)/shard_map/all_gather | solution.py:1012
  265.6 11.1 %collective-permute-done.14.peer_one = bf16[16,1792,128]{2,1,0:T(8,128)(2,1)} collective-permute-done((bf16[16,1792,128]{2,1,0:T(8,128)(2,1)}, bf16[16,1792,128]{2,1,0:T(8,128)(2,1)}, u32[]{:S(2)}, u32[]{:S(2)}) %collective-permute-start.14) | collective-permute-done | bytes 7340064 | tf_op jit(solution)/shard_map/ppermute | solution.py:974
  276.7 37.8 %decoder_forward.1 = (f32[3,48,4096]{2,1,0:T(8,128)}, f32[3,48,4096]{2,1,0:T(8,128)}, f32[3,48,1024]{2,1,0:T(8,128)}, f32[3,48,1024]{2,1,0:T(8,128)}, f32[3,48,1...) custom-call(s32[1]{0:T(128)} %bitcast.unit_ref, ...), custom_call_target="tpu_custom_call" | custom-call | tf_op jit(solution)/shard_map/decoder_forward/pallas_call | solution.py:563
  321.4 4.1 collective-permute-done.17
  326.2 7.4 %collective-permute-done.18 = f32[48,6,80]{2,0,1:T(8,128)S(1)} collective-permute-done((f32[48,6,80]{2,0,1:T(8,128)S(1)}, f32[48,6,80]{2,0,1:T(8,128)S(1)}, u32[]{:S(2)}, u32[]{:S(2)}) %collective-permute-start.18) | collective-permute-done | bytes 92192 | tf_op jit(solution)/shard_map/ppermute | solution.py:990
  334.7 14.6 %collective-permute-done.19 = f32[96,6,80]{2,0,1:T(8,128)S(1)} collective-permute-done((f32[96,6,80]{2,0,1:T(8,128)S(1)}, f32[96,6,80]{2,0,1:T(8,128)S(1)}, u32[]{:S(2)}, u32[]{:S(2)}) %collective-permute-start.19) | collective-permute-done | bytes 184352 | tf_op jit(solution)/shard_map/ppermute | solution.py:990
  350.2 3.1 collective-permute-start.20
  355.6 4.5 collective-permute-done.20.peer_ref
  360.1 55.1 %postnet.1 = (bf16[1152,80]{1,0:T(8,128)(2,1)}, bf16[4,1152,512]{2,1,0:T(8,128)(2,1)}, bf16[4,1152,512]{2,1,0:T(8,128)(2,1)}, bf16[1152,80]{1,0:T(8,128)(2,1)}, ...) custom-call(s32[1]{0:T(128)} %bitcast.unit_ref, f32[1152,80]{1,0:T(8,128)} %bitcast.300, f32[1152,80]{1,0:T(8,128)} %bitcast.301, ...), custom_call_target="tpu_custom_call" | custom-call | tf_op jit(solution)/shard_map/postnet/pallas_call | solution.py:863
  417.0 58.0 %decoder_backward.1 = (bf16[16,80,512]{2,1,0:T(8,128)(2,1)}, f32[3,48,256]{2,1,0:T(8,128)}, f32[3,48,512]{2,1,0:T(8,128)}, f32[3,48,128]{2,1,0:T(8,128)}, f32[76...) custom-call(s32[1]{0:T(128)} %bitcast.unit_ref, ...), custom_call_target="tpu_custom_call" | custom-call | tf_op jit(solution)/shard_map/decoder_backward/pallas_call | solution.py:609
  476.8 6.5 %all-to-all-start = ((bf16[16,80,512]{2,1,0:T(8,128)(2,1)}), bf16[16,80,512]{2,1,0:T(8,128)(2,1)}, u32[]{:S(2)}, u32[]{:S(2)}) async-start(bf16[16,80,512]{2,1,0:T(8,128)(2,1)} %get-tuple-element.132), calls=%async_computation | async-start | bytes 2621440 | tf_op jit(solution)/shard_map/all_to_all | solution.py:1411
  490.7 2.4 concatenate.197
  495.1 2.3 collective-permute-done.21
  499.6 10.4 %all-to-all-done = bf16[16,80,512]{2,1,0:T(8,128)(2,1)} async-done(((bf16[16,80,512]{2,1,0:T(8,128)(2,1)}), bf16[16,80,512]{2,1,0:T(8,128)(2,1)}, u32[]{:S(2)}, u32[]{:S(2)}) %all-to-all-start) | async-done | bytes 1310752 | tf_op jit(solution)/shard_map/all_to_all | solution.py:1411
  512.2 2.8 fusion.2
  516.1 2.3 fusion
  523.2 3.5 collective-permute-start.22
  527.4 3.1 collective-permute-done.32
  531.7 2.8 add_convert_fusion
  535.8 7.3 %all-to-all-start.1 = ((bf16[16,400,128]{2,1,0:T(8,128)(2,1)}), bf16[16,400,128]{2,1,0:T(8,128)(2,1)S(1)}, u32[]{:S(2)}, u32[]{:S(2)}) async-start(bf16[16,400,128]{2,1,0:T(8,128)(2,1)} %pad_maximum_fusion.4), calls=%async_computation.1 | async-start | bytes 3276800 | tf_op jit(solution)/shard_map/all_to_all | solution.py:1556
  543.3 4.1 fusion.122
  550.5 4.2 fusion.121
  569.4 2.5 fusion.25
  571.9 2.5 fusion.27
  576.5 7.1 %collective-permute-start.23 = (bf16[128,128]{1,0:T(8,128)(2,1)S(1)}, bf16[128,128]{1,0:T(8,128)(2,1)S(1)}, u32[]{:S(2)}, u32[]{:S(2)}) collective-permute-start(bf16[128,128]{1,0:T(8,128)(2,1)S(1)} %slice_reduce_fusion), channel_id=1, source_target_pairs={{0,16},{2,18},{4,20},{6,22},{8,24},{10,26},{12,28},{14,30},{16,0},... | collective-permute-start | bytes 98312 | tf_op jit(solution)/shard_map/ppermute | solution.py:990
  585.1 3.1 add_add_fusion
  588.2 3.6 collective-permute-start.33
  (505 shorter events, 147.9 us)
Async XLA Ops:
  7.2 145.8 %all-gather.7.cloned.1.call-start = ((), (), s32[]{:S(2)}) async-start(), calls=%async_computation.3 | async-start | bytes 11141120 | tf_op jit(solution)/shard_map/all_gather | solution.py:1012
  10.0 251.5 %all-gather.5.cloned.1.call-start = ((), (), s32[]{:S(2)}) async-start(), calls=%async_computation.2 | async-start | bytes 7798784 | tf_op jit(solution)/shard_map/all_gather | solution.py:1012
  11.2 339.0 %all-gather.11.cloned.1.call-start = ((), (), s32[]{:S(2)}) async-start(), calls=%async_computation.5 | async-start | bytes 4177920 | tf_op jit(solution)/shard_map/all_gather | solution.py:1019
  13.1 47.7 %collective-permute-start = (bf16[12,6,1024]{2,1,0:T(8,128)(2,1)}, bf16[12,6,1024]{2,1,0:T(8,128)(2,1)}, u32[]{:S(2)}, u32[]{:S(2)}) collective-permute-start(bf16[12,6,1024]{2,1,0:T(8,128)(2,1)} %add_convert_fusion.1), channel_id=1, source_target_pairs={{0,1},{1,0},{2,3},{3,2},{4,5},{5,4},{6,7},{7,6},{8,9},{9,8},{10,11... | collective-permute-start | bytes 442376 | tf_op jit(solution)/shard_map/ppermute | solution.py:974
  13.9 27.4 %collective-permute-start.1 = (f32[2,2048]{1,0:T(2,128)}, f32[2,2048]{1,0:T(2,128)}, u32[]{:S(2)}, u32[]{:S(2)}) collective-permute-start(f32[2,2048]{1,0:T(2,128)} %pad_maximum_fusion.36), channel_id=1, source_target_pairs={{0,1},{1,0},{2,3},{3,2},{4,5},{5,4},{6,7},{7,6},{8,9},{9,8},{10,11... | collective-permute-start | bytes 49160 | tf_op jit(solution)/shard_map/ppermute | solution.py:974
  14.7 28.0 %collective-permute-start.2 = (f32[12,6,81]{0,2,1:T(8,128)S(1)}, f32[12,6,81]{0,2,1:T(8,128)}, u32[]{:S(2)}, u32[]{:S(2)}) collective-permute-start(f32[12,6,81]{0,2,1:T(8,128)S(1)} %maximum_convert_fusion.1), channel_id=1, source_target_pairs={{0,2},{2,0},{4,6},{6,4},{8,10},{10,8},{12,14},{14,12},{16,18},{18,... | collective-permute-start | bytes 69992 | tf_op jit(solution)/shard_map/ppermute | solution.py:990
  16.9 143.9 %collective-permute-start.6 = (bf16[5,80,256]{2,1,0:T(8,128)(2,1)}, bf16[5,80,256]{2,1,0:T(8,128)(2,1)}, u32[]{:S(2)}, u32[]{:S(2)}) collective-permute-start(bf16[5,80,256]{2,1,0:T(8,128)(2,1)} %param.47), channel_id=1, source_target_pairs={{0,1},{1,0},{2,3},{3,2},{4,5},{5,4},{6,7},{7,6},{8,9},{9,8},{10,11... | collective-permute-start | bytes 614408 | tf_op jit(solution)/shard_map/ppermute | solution.py:974
  17.7 17.9 %collective-permute-start.13 = (f32[2,40]{1,0:T(2,128)S(1)}, f32[2,40]{1,0:T(2,128)S(1)}, u32[]{:S(2)}, u32[]{:S(2)}) collective-permute-start(f32[2,40]{1,0:T(2,128)S(1)} %copy-done.64), channel_id=1, source_target_pairs={{0,1},{1,0},{2,3},{3,2},{4,5},{5,4},{6,7},{7,6},{8,9},{9,8},{10,11... | collective-permute-start | bytes 968 | tf_op jit(solution)/shard_map/ppermute | solution.py:974
  43.8 12.5 %collective-permute-start.3 = (f32[24,6,81]{0,2,1:T(8,128)S(1)}, f32[24,6,81]{0,2,1:T(8,128)S(1)}, u32[]{:S(2)}, u32[]{:S(2)}) collective-permute-start(f32[24,6,81]{0,2,1:T(8,128)S(1)} %pad_maximum_fusion.14), channel_id=1, source_target_pairs={{0,4},{2,6},{4,0},{6,2},{8,12},{10,14},{12,8},{14,10},{16,20},{18,... | collective-permute-start | bytes 139976 | tf_op jit(solution)/shard_map/ppermute | solution.py:990
  44.2 14.5 %collective-permute-start.9 = (bf16[128,200]{1,0:T(8,128)(2,1)S(1)}, bf16[128,200]{1,0:T(8,128)(2,1)S(1)}, u32[]{:S(2)}, u32[]{:S(2)}) collective-permute-start(bf16[128,200]{1,0:T(8,128)(2,1)S(1)} %pad_maximum_fusion.29), channel_id=1, source_target_pairs={{0,8},{2,10},{4,12},{6,14},{8,0},{10,2},{12,4},{14,6},{16,24},{18,... | collective-permute-start | bytes 153608 | tf_op jit(solution)/shard_map/ppermute | solution.py:990
  57.3 99.1 %collective-permute-start.4 = (f32[48,6,81]{0,2,1:T(8,128)}, f32[48,6,81]{0,2,1:T(8,128)}, u32[]{:S(2)}, u32[]{:S(2)}) collective-permute-start(f32[48,6,81]{0,2,1:T(8,128)} %pad_maximum_fusion.15), channel_id=1, source_target_pairs={{0,8},{2,10},{4,12},{6,14},{8,0},{10,2},{12,4},{14,6},{16,24},{18,... | collective-permute-start | bytes 279944 | tf_op jit(solution)/shard_map/ppermute | solution.py:990
  59.4 99.6 %collective-permute-start.10 = (bf16[256,200]{1,0:T(8,128)(2,1)}, bf16[256,200]{1,0:T(8,128)(2,1)}, u32[]{:S(2)}, u32[]{:S(2)}) collective-permute-start(bf16[256,200]{1,0:T(8,128)(2,1)} %pad_maximum_fusion.25), channel_id=1, source_target_pairs={{0,16},{2,18},{4,20},{6,22},{8,24},{10,26},{12,28},{14,30},{16,0},... | collective-permute-start | bytes 307208 | tf_op jit(solution)/shard_map/ppermute | solution.py:990
  153.0 123.7 %collective-permute-start.15 = (bf16[16,2560,128]{2,1,0:T(8,128)(2,1)}, bf16[16,2560,128]{2,1,0:T(8,128)(2,1)}, u32[]{:S(2)}, u32[]{:S(2)}) collective-permute-start(bf16[16,2560,128]{2,1,0:T(8,128)(2,1)} %all-gather.7.cloned.1.call-done.own_two), channel_id=1, source_target_pairs={{0,1},{1,0},{2,3},{3,2},{4,5},{5,4},{6,7},{7,6},{8,9},{9,8},{10,11... | collective-permute-start | bytes 31457288 | tf_op jit(solution)/shard_map/ppermute | solution.py:974
  157.6 22.2 %collective-permute-start.5 = (f32[96,6,81]{0,2,1:T(8,128)S(1)}, f32[96,6,81]{0,2,1:T(8,128)S(1)}, u32[]{:S(2)}, u32[]{:S(2)}) collective-permute-start(f32[96,6,81]{0,2,1:T(8,128)S(1)} %pad_maximum_fusion.16), channel_id=1, source_target_pairs={{0,16},{2,18},{4,20},{6,22},{8,24},{10,26},{12,28},{14,30},{16,0},... | collective-permute-start | bytes 559880 | tf_op jit(solution)/shard_map/ppermute | solution.py:990
  160.1 20.9 %collective-permute-start.11 = (bf16[5,512,40]{1,2,0:T(8,128)(2,1)S(1)}, bf16[5,512,40]{1,2,0:T(8,128)(2,1)}, u32[]{:S(2)}, u32[]{:S(2)}) collective-permute-start(bf16[5,512,40]{1,2,0:T(8,128)(2,1)S(1)} %bitcast.322), channel_id=1, source_target_pairs={{0,1},{1,0},{2,3},{3,2},{4,5},{5,4},{6,7},{7,6},{8,9},{9,8},{10,11... | collective-permute-start | bytes 614408 | tf_op jit(solution)/shard_map/ppermute | solution.py:974
  264.0 12.7 %collective-permute-start.14 = (bf16[16,1792,128]{2,1,0:T(8,128)(2,1)}, bf16[16,1792,128]{2,1,0:T(8,128)(2,1)}, u32[]{:S(2)}, u32[]{:S(2)}) collective-permute-start(bf16[16,1792,128]{2,1,0:T(8,128)(2,1)} %all-gather.5.cloned.1.call-done.own_one), channel_id=1, source_target_pairs={{0,1},{1,0},{2,3},{3,2},{4,5},{5,4},{6,7},{7,6},{8,9},{9,8},{10,11... | collective-permute-start | bytes 22020104 | tf_op jit(solution)/shard_map/ppermute | solution.py:974
  265.1 247.1 %all-gather.9.cloned.1.call-start = ((), (), s32[]{:S(2)}) async-start(), calls=%async_computation.4 | async-start | bytes 7659520 | tf_op jit(solution)/shard_map/all_gather | solution.py:1241
  325.6 8.0 %collective-permute-start.18 = (f32[48,6,80]{2,0,1:T(8,128)S(1)}, f32[48,6,80]{2,0,1:T(8,128)S(1)}, u32[]{:S(2)}, u32[]{:S(2)}) collective-permute-start(f32[48,6,80]{2,0,1:T(8,128)S(1)} %pad_maximum_fusion.22), channel_id=1, source_target_pairs={{0,8},{2,10},{4,12},{6,14},{8,0},{10,2},{12,4},{14,6},{16,24},{18,... | collective-permute-start | bytes 276488 | tf_op jit(solution)/shard_map/ppermute | solution.py:990
  333.7 15.5 %collective-permute-start.19 = (f32[96,6,80]{2,0,1:T(8,128)S(1)}, f32[96,6,80]{2,0,1:T(8,128)S(1)}, u32[]{:S(2)}, u32[]{:S(2)}) collective-permute-start(f32[96,6,80]{2,0,1:T(8,128)S(1)} %pad_maximum_fusion.13), channel_id=1, source_target_pairs={{0,16},{2,18},{4,20},{6,22},{8,24},{10,26},{12,28},{14,30},{16,0},... | collective-permute-start | bytes 552968 | tf_op jit(solution)/shard_map/ppermute | solution.py:990
  350.2 9.8 %collective-permute-start.20 = (bf16[15,512,256]{2,1,0:T(8,128)(2,1)}, bf16[15,512,256]{2,1,0:T(8,128)(2,1)}, u32[]{:S(2)}, u32[]{:S(2)}) collective-permute-start(bf16[15,512,256]{2,1,0:T(8,128)(2,1)} %all-gather.11.cloned.1.call-done.own_ref), channel_id=1, source_target_pairs={{0,1},{1,0},{2,3},{3,2},{4,5},{5,4},{6,7},{7,6},{8,9},{9,8},{10,11... | collective-permute-start | bytes 11796488 | tf_op jit(solution)/shard_map/ppermute | solution.py:974
  476.8 33.3 %all-to-all-start = ((bf16[16,80,512]{2,1,0:T(8,128)(2,1)}), bf16[16,80,512]{2,1,0:T(8,128)(2,1)}, u32[]{:S(2)}, u32[]{:S(2)}) async-start(bf16[16,80,512]{2,1,0:T(8,128)(2,1)} %get-tuple-element.132), calls=%async_computation | async-start | bytes 2621440 | tf_op jit(solution)/shard_map/all_to_all | solution.py:1411
  523.2 8.5 %collective-permute-start.22 = (f32[16,272,128]{2,1,0:T(8,128)}, f32[16,272,128]{2,1,0:T(8,128)}, u32[]{:S(2)}, u32[]{:S(2)}) collective-permute-start(f32[16,272,128]{2,1,0:T(8,128)} %broadcast_select_fusion), channel_id=1, source_target_pairs={{0,1},{1,0},{2,3},{3,2},{4,5},{5,4},{6,7},{7,6},{8,9},{9,8},{10,11... | collective-permute-start | bytes 6684680 | tf_op jit(solution)/shard_map/ppermute | solution.py:974
  535.8 40.6 %all-to-all-start.1 = ((bf16[16,400,128]{2,1,0:T(8,128)(2,1)}), bf16[16,400,128]{2,1,0:T(8,128)(2,1)S(1)}, u32[]{:S(2)}, u32[]{:S(2)}) async-start(bf16[16,400,128]{2,1,0:T(8,128)(2,1)} %pad_maximum_fusion.4), calls=%async_computation.1 | async-start | bytes 3276800 | tf_op jit(solution)/shard_map/all_to_all | solution.py:1556
  550.0 48.8 %collective-permute-start.28 = (f32[5,80,256]{2,1,0:T(8,128)}, f32[5,80,256]{2,1,0:T(8,128)}, u32[]{:S(2)}, u32[]{:S(2)}) collective-permute-start(f32[5,80,256]{2,1,0:T(8,128)} %slice_select_fusion.2), channel_id=1, source_target_pairs={{0,1},{1,0},{2,3},{3,2},{4,5},{5,4},{6,7},{7,6},{8,9},{9,8},{10,11... | collective-permute-start | bytes 1228808 | tf_op jit(solution)/shard_map/ppermute | solution.py:974
  566.9 33.8 %collective-permute-start.29 = (f32[3,5,32,256]{3,2,1,0:T(8,128)}, f32[3,5,32,256]{3,2,1,0:T(8,128)}, u32[]{:S(2)}, u32[]{:S(2)}) collective-permute-start(f32[3,5,32,256]{3,2,1,0:T(8,128)} %slice_select_fusion.1), channel_id=1, source_target_pairs={{0,1},{1,0},{2,3},{3,2},{4,5},{5,4},{6,7},{7,6},{8,9},{9,8},{10,11... | collective-permute-start | bytes 1474568 | tf_op jit(solution)/shard_map/ppermute | solution.py:974
  568.1 25.4 %collective-permute-start.30 = (f32[5,32,40]{2,1,0:T(8,128)}, f32[5,32,40]{2,1,0:T(8,128)}, u32[]{:S(2)}, u32[]{:S(2)}) collective-permute-start(f32[5,32,40]{2,1,0:T(8,128)} %slice_select_fusion.3), channel_id=1, source_target_pairs={{0,1},{1,0},{2,3},{3,2},{4,5},{5,4},{6,7},{7,6},{8,9},{9,8},{10,11... | collective-permute-start | bytes 76808 | tf_op jit(solution)/shard_map/ppermute | solution.py:974
  576.5 8.5 %collective-permute-start.23 = (bf16[128,128]{1,0:T(8,128)(2,1)S(1)}, bf16[128,128]{1,0:T(8,128)(2,1)S(1)}, u32[]{:S(2)}, u32[]{:S(2)}) collective-permute-start(bf16[128,128]{1,0:T(8,128)(2,1)S(1)} %slice_reduce_fusion), channel_id=1, source_target_pairs={{0,16},{2,18},{4,20},{6,22},{8,24},{10,26},{12,28},{14,30},{16,0},... | collective-permute-start | bytes 98312 | tf_op jit(solution)/shard_map/ppermute | solution.py:990
  585.0 6.8 %collective-permute-start.24 = (bf16[2,128,128]{2,1,0:T(8,128)(2,1)S(1)}, bf16[2,128,128]{2,1,0:T(8,128)(2,1)S(1)}, u32[]{:S(2)}, u32[]{:S(2)}) collective-permute-start(bf16[2,128,128]{2,1,0:T(8,128)(2,1)S(1)} %pad_maximum_fusion.30), channel_id=1, source_target_pairs={{0,8},{2,10},{4,12},{6,14},{8,0},{10,2},{12,4},{14,6},{16,24},{18,... | collective-permute-start | bytes 196616 | tf_op jit(solution)/shard_map/ppermute | solution.py:990
  588.2 18.8 %collective-permute-start.33 = (f32[12,64,512]{2,1,0:T(8,128)S(1)}, f32[12,64,512]{2,1,0:T(8,128)S(1)}, u32[]{:S(2)}, u32[]{:S(2)}) collective-permute-start(f32[12,64,512]{2,1,0:T(8,128)S(1)} %bitcast.293), channel_id=1, source_target_pairs={{0,1},{1,0},{2,3},{3,2},{4,5},{5,4},{6,7},{7,6},{8,9},{9,8},{10,11... | collective-permute-start | bytes 4718600 | tf_op jit(solution)/shard_map/ppermute | solution.py:974
  591.8 5.5 collective-permute-start.25
  597.4 7.2 %collective-permute-start.26 = (bf16[2,2,2,128,128]{4,3,0,1,2:T(8,128)(2,1)S(1)}, bf16[2,2,2,128,128]{4,3,0,1,2:T(8,128)(2,1)S(1)}, u32[]{:S(2)}, u32[]{:S(2)}) collective-permute-start(bf16[2,2,2,128,128]{4,3,0,1,2:T(8,128)(2,1)S(1)} %pad_maximum_fusion.18), channel_id=1, source_target_pairs={{0,2},{2,0},{4,6},{6,4},{8,10},{10,8},{12,14},{14,12},{16,18},{18,... | collective-permute-start | bytes 786440 | tf_op jit(solution)/shard_map/ppermute | solution.py:990
  605.5 9.5 %collective-permute-start.27 = (bf16[2048,128]{1,0:T(8,128)(2,1)}, bf16[2048,128]{1,0:T(8,128)(2,1)}, u32[]{:S(2)}, u32[]{:S(2)}) collective-permute-start(bf16[2048,128]{1,0:T(8,128)(2,1)} %bitcast.60), channel_id=1, source_target_pairs={{0,1},{1,0},{2,3},{3,2},{4,5},{5,4},{6,7},{7,6},{8,9},{9,8},{10,11... | collective-permute-start | bytes 1572872 | tf_op jit(solution)/shard_map/ppermute | solution.py:974
  (84 other events, 478.8 us)
Sparse Core Ops, SparseCore 0:
  11.3 141.5 all-gather.6
  156.3 105.2 all-gather.4
  265.2 77.4 all-gather.10
  350.3 104.1 all-gather.8

commit v2 on v1

--- a/solution.py
+++ b/solution.py
@@ -77,12 +77,53 @@
     return pl.multiple_of(start * lanes, lanes)
 
 
+def weight_copies(refs, held, place, sems, start):
+    if len(refs) == 2:
+        return [
+            pltpu.make_async_copy(ref, held.at[side], sems.at[start + side])
+            for side, ref in enumerate(refs)
+        ]
+    copies = []
+    for index, ref in enumerate(refs):
+        side, turn, which = index // 4, index // 2 % 2, index % 2
+        _, _, _, tiles, rows, _ = ref.shape
+        near, last = (1, 2) if turn == 0 else (2, 1)
+        bit = (place // last + which) % 2
+        for k in range(2):
+            for far in range(4):
+                device = far * 4 + k * near + bit * last
+                spot = pl.ds(pl.multiple_of(device * rows, 16), rows)
+                copies.append(
+                    pltpu.make_async_copy(
+                        ref.at[k, far // 2, far % 2],
+                        held.at[side, turn * tiles : (turn + 1) * tiles, spot, :],
+                        sems.at[start + len(copies)],
+                    )
+                )
+    return copies
+
+
 def forward_kernel(
+    weight_count,
     unit_ref,
-    own_one,
-    peer_one,
-    own_two,
-    peer_two,
+    *refs,
+):
+    weight_refs, refs = refs[:weight_count], refs[weight_count:]
+    forward_body(unit_ref, weight_refs, *refs)
+
+
+def backward_kernel(
+    weight_count,
+    unit_ref,
+    *refs,
+):
+    weight_refs, refs = refs[:weight_count], refs[weight_count:]
+    backward_body(unit_ref, weight_refs, *refs)
+
+
+def forward_body(
+    unit_ref,
+    weight_refs,
     previous_ref,
     drop_one,
     drop_two,
@@ -137,14 +178,9 @@
     per_half = half // lanes
     position_count = hot_ref.shape[0]
     text_width = position_count // (slots // 4)
-    copies_two = [
-        pltpu.make_async_copy(own_two, held_two.at[0], sems.at[0]),
-        pltpu.make_async_copy(peer_two, held_two.at[1], sems.at[1]),
-    ]
-    copies_one = [
-        pltpu.make_async_copy(own_one, held_one.at[0], sems.at[2]),
-        pltpu.make_async_copy(peer_one, held_one.at[1], sems.at[3]),
-    ]
+    each = len(weight_refs) // 2
+    copies_two = weight_copies(weight_refs[each:], held_two, unit_ref[1], sems, 0)
+    copies_one = weight_copies(weight_refs[:each], held_one, unit_ref[1], sems, len(copies_two))
     for copy in copies_two + copies_one:
         copy.start()
     for ref in (state_one, cell_one, state_two, cell_two):
@@ -289,12 +325,9 @@
         frame_out[...] = (frame_bias[...] if step == 0 else frame_out[...]) + picked
 
 
-def backward_kernel(
+def backward_body(
     unit_ref,
-    own_one,
-    peer_one,
-    own_two,
-    peer_two,
+    weight_refs,
     gates_one,
     gates_two,
     prior_one,
@@ -345,14 +378,9 @@
     per_half = half // lanes
     position_count = hot_ref.shape[0]
     text_width = position_count // (slots // 4)
-    copies_two = [
-        pltpu.make_async_copy(own_two, held_two.at[0], sems.at[0]),
-        pltpu.make_async_copy(peer_two, held_two.at[1], sems.at[1]),
-    ]
-    copies_one = [
-        pltpu.make_async_copy(own_one, held_one.at[0], sems.at[2]),
-        pltpu.make_async_copy(peer_one, held_one.at[1], sems.at[3]),
-    ]
+    each = len(weight_refs) // 2
+    copies_two = weight_copies(weight_refs[each:], held_two, unit_ref[1], sems, 0)
+    copies_one = weight_copies(weight_refs[:each], held_one, unit_ref[1], sems, len(copies_two))
     for copy in copies_two + copies_one:
         copy.start()
     for ref in (
@@ -536,8 +564,10 @@
 
 
 def call_forward(unit, weights, small, sizes):
-    own_one, peer_one, own_two, peer_two = weights
     steps, slots, hidden, context_width, positions, frame_rows, prenet_width = sizes
+    tiles = 2 * hidden // lanes
+    held_one = (2, tiles, prenet_width + context_width + hidden, lanes)
+    held_two = (2, tiles, 2 * hidden + context_width, lanes)
 
     def shape(*dims):
         return jax.ShapeDtypeStruct(dims, f32)
@@ -561,16 +591,16 @@
     ]
     vmem = pl.BlockSpec(memory_space=pltpu.VMEM)
     return pl.pallas_call(
-        forward_kernel,
+        functools.partial(forward_kernel, len(weights)),
         out_shape=outs,
         in_specs=[pl.BlockSpec(memory_space=pltpu.SMEM)]
-        + [pl.BlockSpec(memory_space=pl.ANY)] * 4
+        + [pl.BlockSpec(memory_space=pl.ANY)] * len(weights)
         + [vmem] * len(small),
         out_specs=[vmem] * len(outs),
         scratch_shapes=[
-            pltpu.VMEM((2,) + own_one.shape, bf16),
-            pltpu.VMEM((2,) + own_two.shape, bf16),
-            pltpu.VMEM((slots, own_two.shape[1]), bf16),
+            pltpu.VMEM(held_one, bf16),
+            pltpu.VMEM(held_two, bf16),
+            pltpu.VMEM((slots, held_two[2]), bf16),
             pltpu.VMEM((steps, slots, prenet_width), f32),
             pltpu.VMEM((positions, lanes), f32),
             pltpu.VMEM((2, lanes, lanes), f32),
@@ -578,20 +608,21 @@
             pltpu.VMEM((slots, hidden), f32),
             pltpu.VMEM((slots, hidden), f32),
             pltpu.VMEM((slots, hidden), f32),
-            pltpu.SemaphoreType.DMA((4,)),
+            pltpu.SemaphoreType.DMA((8 * len(weights),)),
         ],
         compiler_params=pltpu.CompilerParams(vmem_limit_bytes=kernel_vmem),
         name="decoder_forward",
     )(unit, *weights, *small)
 
 
-def call_backward(unit, weights, small):
-    own_one, peer_one, own_two, peer_two = weights
+def call_backward(unit, weights, small, prenet_width):
     gates_one = small[0]
     steps, slots, gate_width = gates_one.shape
     hidden = gate_width // 4
     positions, context_width = small[7].shape
-    prenet_width = own_one.shape[1] - hidden - context_width
+    tiles = 2 * hidden // lanes
+    held_one = (2, tiles, prenet_width + context_width + hidden, lanes)
+    held_two = (2, tiles, 2 * hidden + context_width, lanes)
 
     def shape(dims, kind):
         return jax.ShapeDtypeStruct(dims, kind)
@@ -607,19 +638,19 @@
     ]
     vmem = pl.BlockSpec(memory_space=pltpu.VMEM)
     return pl.pallas_call(
-        backward_kernel,
+        functools.partial(backward_kernel, len(weights)),
         out_shape=outs,
         in_specs=[pl.BlockSpec(memory_space=pltpu.SMEM)]
-        + [pl.BlockSpec(memory_space=pl.ANY)] * 4
+        + [pl.BlockSpec(memory_space=pl.ANY)] * len(weights)
         + [vmem] * len(small),
         out_specs=[vmem] * len(outs),
         scratch_shapes=[
-            pltpu.VMEM((2,) + own_one.shape, bf16),
-            pltpu.VMEM((2,) + own_two.shape, bf16),
+            pltpu.VMEM(held_one, bf16),
+            pltpu.VMEM(held_two, bf16),
             pltpu.VMEM((steps, slots, gate_width), bf16),
             pltpu.VMEM((steps, slots, gate_width), bf16),
-            pltpu.VMEM((slots, own_one.shape[1]), f32),
-            pltpu.VMEM((slots, own_two.shape[1]), f32),
+            pltpu.VMEM((slots, held_one[2]), f32),
+            pltpu.VMEM((slots, held_two[2]), f32),
             pltpu.VMEM((slots, hidden), f32),
             pltpu.VMEM((slots, hidden), f32),
             pltpu.VMEM((slots, hidden), f32),
@@ -629,7 +660,7 @@
             pltpu.VMEM((slots, hidden), f32),
             pltpu.VMEM((steps, slots, hidden + context_width), f32),
             pltpu.VMEM((2, lanes, lanes), f32),
-            pltpu.SemaphoreType.DMA((4,)),
+            pltpu.SemaphoreType.DMA((8 * len(weights),)),
         ],
         compiler_params=pltpu.CompilerParams(vmem_limit_bytes=kernel_vmem),
         name="decoder_backward",
@@ -1007,17 +1038,40 @@
             bit *= 2
         return value
 
-    def gather_tiles(value):
-        tiles = jnp.transpose(value.reshape(value.shape[0], -1, lanes), (1, 0, 2))
-        return lax.all_gather(tiles, "batch", axis=1, tiled=True)
-
-    own_two = gather_tiles(lstm_second)
-    own_one = gather_tiles(lstm_first)
-    peer_two = exchange(own_two)
+    def to_tiles(value):
+        return jnp.transpose(value.reshape(value.shape[0], -1, lanes), (1, 0, 2))
+
+    def along_z(value):
+        value = jnp.stack(swapped(value, 8))
+        return jnp.stack(swapped(value, 4), axis=1)
+
+    def in_plane(value):
+        pieces = []
+        tall = value.shape[2] // 2
+        for turn, (near, last) in enumerate(((1, 2), (2, 1))):
+            part = jnp.stack(swapped(value[:, :, turn * tall : (turn + 1) * tall], near))
+            pairs = [(index, index ^ last) for index in range(batch_size)]
+            pieces += [part, lax.ppermute(part, "batch", pairs)]
+        return tuple(pieces)
+
+    crossed = batch_size == 16 and depth_one % 16 == 0 and depth_two % 16 == 0
+    if crossed:
+        line_two = along_z(to_tiles(lstm_second))
+        tiles_one, line_two = lax.optimization_barrier((to_tiles(lstm_first), line_two))
+        line_one = along_z(tiles_one)
+        own_two = in_plane(line_two)
+        own_one = in_plane(line_one)
+        peer_two = tuple(exchange(value) for value in own_two)
+        post_source = lax.optimization_barrier((post_middle, own_two[-1]))[0]
+    else:
+        own_two = (lax.all_gather(to_tiles(lstm_second), "batch", axis=1, tiled=True),)
+        own_one = (lax.all_gather(to_tiles(lstm_first), "batch", axis=1, tiled=True),)
+        peer_two = (exchange(own_two[0]),)
+        post_source = post_middle
     channel_rows = post_middle.shape[2]
     middle_width = post_middle.shape[3]
     middle_half = lax.all_gather(
-        post_middle.reshape(-1, channel_rows, middle_width), "batch", axis=1, tiled=True
+        post_source.reshape(-1, channel_rows, middle_width), "batch", axis=1, tiled=True
     )
     last_half = gather_rows(jnp.transpose(post_last, (1, 0, 2)).reshape(channel_rows, -1))
     last_half = jnp.transpose(
@@ -1118,7 +1172,7 @@
     vector_wide = jnp.broadcast_to(vector_float[:, None], (attention_width, lanes))
     memory_float = memory_now.astype(f32)
     query_float = query_weight.astype(f32)
-    unit_array = unit.astype(jnp.int32).reshape(1)
+    unit_array = jnp.stack([unit, place]).astype(jnp.int32)
 
     targets_all = jnp.transpose(frame_info[:, :, :mel_width].astype(f32), (1, 0, 2))
     segments_all = jnp.transpose(frame_info[:, :, mel_width].astype(jnp.int32))
@@ -1183,7 +1237,9 @@
             norms,
         )
     )
-    weights = (own_one, exchange(own_one), own_two, peer_two)
+    own_one, peer_two = lax.optimization_barrier((own_one, peer_two))
+    peer_one = tuple(exchange(value) for value in own_one)
+    weights = own_one + peer_one + own_two + peer_two
     slot_wide, zone_one, zone_two = forward_small[5], forward_small[6], forward_small[7]
     memory_float, query_float = forward_small[11], forward_small[13]
     dense_wide, frame_wide = forward_small[16], forward_small[17]
@@ -1399,6 +1455,7 @@
             frame_wide,
             slot_wide,
         ),
+        prenet_width,
     )
 
     bias_sums = jnp.transpose(

time: 640 us -> 683 us (1.067)
  waiting for transfers between devices: 266 us -> 226 us
  starting transfers between devices: 54.8 us -> 92.9 us
  other arithmetic: 58.8 us -> 82.7 us
  local copies, waits for them, and re-layouts: 59.7 us -> 69 us
    all_gather x3 -> x1, waiting for transfers between devices: 168 us -> 0.02 us  [on_device(): lax.all_gather(post_source.reshape(-1, channel_rows, middle_width), 'batc...]
    ppermute x16 -> x24, waiting for transfers between devices: 63.3 us -> 155 us  [swapped(): other = lax.ppermute(value, 'batch', pairs)]
    ppermute x0 -> x4, waiting for transfers between devices: none -> 36.1 us  [in_plane(): pieces += [part, lax.ppermute(part, 'batch', pairs)]]
    ppermute x16 -> x24, starting transfers between devices: 22.7 us -> 36.5 us  [swapped(): other = lax.ppermute(value, 'batch', pairs)]
    another operation x5 -> x21, other arithmetic: 2.16 us -> 15.4 us  [the longest x7 8.57 us: in_plane(): part = jnp.stack(swapped(value[:, :, turn * tall:(turn + 1) * tall], near))]
    ppermute x18 -> x24, starting transfers between devices: 17.7 us -> 30.7 us  [exchange(): return lax.ppermute(value, 'unit', [(0, 1), (1, 0)])]
    all_gather x1, starting transfers between devices: 0.51 us -> 10.2 us  [on_device(): inputs_all = lax.all_gather(inputs_own, 'batch', axis=0, tiled=True)]
    ppermute x18 -> x24, waiting for transfers between devices: 21.7 us -> 20.1 us  [exchange(): return lax.ppermute(value, 'unit', [(0, 1), (1, 0)])]
  transfers between devices with their start and end apart: 40 -> 56, of which waited for: 19 -> 24; matrix products, arithmetic and copies ran while one was open for 18% -> 22% of each run, Pallas kernels for 24% -> 23%
where the time goes in v2:
time: 683 us; the launch traced here: 670 us
  waiting for transfers between devices  226 us (33%)
  Pallas kernels  153 us (22%)
  starting transfers between devices  92.9 us (14%)
  other arithmetic  82.7 us (12%)
  local copies, waits for them, and re-layouts  69 us (10%)
  matrix products  29.5 us (4%)
  between operations  16.4 us (2%)
    ppermute x24, waiting for transfers between devices, swapped(): other = lax.ppermute(value, 'batch', pairs)  155 us
    pallas_call x1, Pallas kernels, call_backward(): pl.pallas_call(functools.partial(backward_kernel, len(weights)), out_shap...  59.3 us
    pallas_call x1, Pallas kernels, call_postnet(): pl.pallas_call(functools.partial(postnet_kernel, mel_width, loss_scale),...  55.1 us
    pallas_call x1, Pallas kernels, call_forward(): pl.pallas_call(functools.partial(forward_kernel, len(weights)), out_shape...  39.1 us
    ppermute x24, starting transfers between devices, swapped(): other = lax.ppermute(value, 'batch', pairs)  36.5 us
    ppermute x4, waiting for transfers between devices, in_plane(): pieces += [part, lax.ppermute(part, 'batch', pairs)]  36.1 us
    ppermute x24, starting transfers between devices, exchange(): return lax.ppermute(value, 'unit', [(0, 1), (1, 0)])  30.7 us
    ppermute x24, waiting for transfers between devices, exchange(): return lax.ppermute(value, 'unit', [(0, 1), (1, 0)])  20.1 us
  transfers between devices with their start and end apart: 56, of which 24 were waited for; matrix products, arithmetic and copies ran while one was open for 22% of the time, Pallas kernels for 23%

profile of v2, /device:TPU:1, one launch (start us, length us, event | category | flops | bytes accessed | tf_op | source)
XLA Modules:
  0.0 670.5 jit_solution(12822325991261522933)
XLA Ops:
  10.0 3.2 collective-permute-start
  53.6 22.7 %collective-permute-done.1 = bf16[2,16,160,128]{3,2,1,0:T(8,128)(2,1)S(1)} collective-permute-done((bf16[2,16,160,128]{3,2,1,0:T(8,128)(2,1)S(1)}, bf16[2,16,160,128]{3,2,1,0:T(8,128)(2,1)S(1)}, u32[]{:S(2)}, u32[]{:S(2)}) %collective-permute-start.1) | collective-permute-done | bytes 1310752 | tf_op jit(solution)/shard_map/ppermute | solution.py:1021
  82.7 18.6 %collective-permute-done.2 = bf16[16,112,128]{2,1,0:T(8,128)(2,1)S(1)} collective-permute-done((bf16[16,112,128]{2,1,0:T(8,128)(2,1)S(1)}, bf16[16,112,128]{2,1,0:T(8,128)(2,1)S(1)}, u32[]{:S(2)}, u32[]{:S(2)}) %collective-permute-start.2) | collective-permute-done | bytes 458784 | tf_op jit(solution)/shard_map/ppermute | solution.py:1021
  102.8 3.2 collective-permute-done.10
  110.2 11.7 %collective-permute-done.3 = bf16[2,16,112,128]{3,2,1,0:T(8,128)(2,1)S(1)} collective-permute-done((bf16[2,16,112,128]{3,2,1,0:T(8,128)(2,1)S(1)}, bf16[2,16,112,128]{3,2,1,0:T(8,128)(2,1)S(1)}, u32[]{:S(2)}, u32[]{:S(2)}) %collective-permute-start.3) | collective-permute-done | bytes 917536 | tf_op jit(solution)/shard_map/ppermute | solution.py:1021
  129.1 3.1 collective-permute-start.22
  135.0 46.6 %collective-permute-done.4 = bf16[2,2,8,112,128]{4,3,2,1,0:T(8,128)(2,1)} collective-permute-done((bf16[2,2,8,112,128]{4,3,2,1,0:T(8,128)(2,1)}, bf16[2,2,8,112,128]{4,3,2,1,0:T(8,128)(2,1)}, u32[]{:S(2)}, u32[]{:S(2)}) %collective-permute-start.4) | collective-permute-done | bytes 917536 | tf_op jit(solution)/shard_map/ppermute | solution.py:1021
  189.3 5.9 collective-permute-start.18
  195.2 10.2 %all-gather.3.cloned.1.call-start = ((), (), s32[]{:S(2)}) async-start(), calls=%async_computation.2 | async-start | bytes 7659520 | tf_op jit(solution)/shard_map/all_gather | solution.py:1297
  216.8 7.4 %collective-permute-done.17 = f32[96,6,81]{0,2,1:T(8,128)} collective-permute-done((f32[96,6,81]{0,2,1:T(8,128)}, f32[96,6,81]{0,2,1:T(8,128)}, u32[]{:S(2)}, u32[]{:S(2)}) %collective-permute-start.17) | collective-permute-done | bytes 186656 | tf_op jit(solution)/shard_map/ppermute | solution.py:1021
  225.0 21.4 %collective-permute-done.6 = bf16[2,2,8,112,128]{4,3,2,1,0:T(8,128)(2,1)} collective-permute-done((bf16[2,2,8,112,128]{4,3,2,1,0:T(8,128)(2,1)}, bf16[2,2,8,112,128]{4,3,2,1,0:T(8,128)(2,1)}, u32[]{:S(2)}, u32[]{:S(2)}) %collective-permute-start.6) | collective-permute-done | bytes 917536 | tf_op jit(solution)/shard_map/ppermute | solution.py:1021
  246.4 7.8 %collective-permute-start.29 = (bf16[2,2,2,8,160,128]{5,4,3,2,1,0:T(8,128)(2,1)}, bf16[2,2,2,8,160,128]{5,4,3,2,1,0:T(8,128)(2,1)}, u32[]{:S(2)}, u32[]{:S(2)}) collective-permute-start(bf16[2,2,2,8,160,128]{5,4,3,2,1,0:T(8,128)(2,1)} %collective-permute-done.11.refs_11_), channel_id=1, source_target_pairs={{0,1},{1,0},{2,3},{3,2},{4,5},{5,4},{6,7},{7,6},{8,9},{9,8},{10,11... | collective-permute-start | bytes 7864328 | tf_op jit(solution)/shard_map/ppermute | solution.py:1005
  268.2 36.1 %collective-permute-done.7.refs_3_ = bf16[2,2,2,8,112,128]{5,4,3,2,1,0:T(8,128)(2,1)} collective-permute-done((bf16[2,2,2,8,112,128]{5,4,3,2,1,0:T(8,128)(2,1)}, bf16[2,2,2,8,112,128]{5,4,3,2,1,0:T(8,128)(2,1)}, u32[]{:S(2)}, u32[]{:S(2)}) %collective-permute-start.7) | collective-permute-done | bytes 1835040 | tf_op jit(solution)/shard_map/ppermute | solution.py:1054
  308.7 4.3 collective-permute-done.30.refs_4_
  319.2 39.1 %decoder_forward.1 = (f32[3,48,4096]{2,1,0:T(8,128)}, f32[3,48,4096]{2,1,0:T(8,128)}, f32[3,48,1024]{2,1,0:T(8,128)}, f32[3,48,1024]{2,1,0:T(8,128)}, f32[3,48,1...) custom-call(s32[2]{0:T(128)} %pad_add_fusion.unit_ref, ...), custom_call_target="tpu_custom_call" | custom-call | tf_op jit(solution)/shard_map/decoder_forward/pallas_call | solution.py:593
  372.6 11.8 %collective-permute-done.37 = f32[96,6,80]{2,0,1:T(8,128)} collective-permute-done((f32[96,6,80]{2,0,1:T(8,128)S(1)}, f32[96,6,80]{2,0,1:T(8,128)}, u32[]{:S(2)}, u32[]{:S(2)}) %collective-permute-start.37) | collective-permute-done | bytes 184352 | tf_op jit(solution)/shard_map/ppermute | solution.py:1021
  390.7 4.5 collective-permute-done.38.peer_ref
  395.2 55.1 %postnet.1 = (bf16[1152,80]{1,0:T(8,128)(2,1)}, bf16[4,1152,512]{2,1,0:T(8,128)(2,1)}, bf16[4,1152,512]{2,1,0:T(8,128)(2,1)}, bf16[1152,80]{1,0:T(8,128)(2,1)}, ...) custom-call(s32[2]{0:T(128)} %pad_add_fusion.unit_ref, f32[1152,80]{1,0:T(8,128)} %bitcast.340, f32[1152,80]{1,0:T(8,128)} %bitcast.341, ...), custom_call_target="tpu_custom_call" | custom-call | tf_op jit(solution)/shard_map/postnet/pallas_call | solution.py:894
  452.2 59.3 %decoder_backward.1 = (bf16[16,80,512]{2,1,0:T(8,128)(2,1)}, f32[3,48,256]{2,1,0:T(8,128)}, f32[3,48,512]{2,1,0:T(8,128)}, f32[3,48,128]{2,1,0:T(8,128)}, f32[76...) custom-call(s32[2]{0:T(128)} %pad_add_fusion.unit_ref, ...), custom_call_target="tpu_custom_call" | custom-call | tf_op jit(solution)/shard_map/decoder_backward/pallas_call | solution.py:640
  513.3 6.4 all-to-all-start
  528.8 3.0 concatenate.197
  536.3 10.1 %all-to-all-done = bf16[16,80,512]{2,1,0:T(8,128)(2,1)} async-done(((bf16[16,80,512]{2,1,0:T(8,128)(2,1)}), bf16[16,80,512]{2,1,0:T(8,128)(2,1)}, u32[]{:S(2)}, u32[]{:S(2)}) %all-to-all-start) | async-done | bytes 1310752 | tf_op jit(solution)/shard_map/all_to_all | solution.py:1468
  548.7 3.1 fusion.2
  562.6 3.5 collective-permute-start.40
  566.8 3.1 collective-permute-done.50
  574.8 7.2 %all-to-all-start.1 = ((bf16[16,400,128]{2,1,0:T(8,128)(2,1)}), bf16[16,400,128]{2,1,0:T(8,128)(2,1)S(1)}, u32[]{:S(2)}, u32[]{:S(2)}) async-start(bf16[16,400,128]{2,1,0:T(8,128)(2,1)} %pad_maximum_fusion.9), calls=%async_computation.1 | async-start | bytes 3276800 | tf_op jit(solution)/shard_map/all_to_all | solution.py:1613
  582.2 4.2 fusion.123
  588.7 4.3 fusion.122
  610.3 5.2 all-to-all-done.1
  615.6 7.1 %collective-permute-start.41 = (bf16[128,128]{1,0:T(8,128)(2,1)S(1)}, bf16[128,128]{1,0:T(8,128)(2,1)S(1)}, u32[]{:S(2)}, u32[]{:S(2)}) collective-permute-start(bf16[128,128]{1,0:T(8,128)(2,1)S(1)} %slice_reduce_fusion), channel_id=1, source_target_pairs={{0,16},{2,18},{4,20},{6,22},{8,24},{10,26},{12,28},{14,30},{16,0},... | collective-permute-start | bytes 98312 | tf_op jit(solution)/shard_map/ppermute | solution.py:1021
  624.2 3.2 add_add_fusion
  627.3 3.5 collective-permute-start.51
  (582 shorter events, 218.1 us)
Async XLA Ops:
  7.2 379.1 %all-gather.5.cloned.1.call-start = ((), (), s32[]{:S(2)}) async-start(), calls=%async_computation.3 | async-start | bytes 4177920 | tf_op jit(solution)/shard_map/all_gather | solution.py:1073
  10.0 35.0 %collective-permute-start = (bf16[16,160,128]{2,1,0:T(8,128)(2,1)}, bf16[16,160,128]{2,1,0:T(8,128)(2,1)}, u32[]{:S(2)}, u32[]{:S(2)}) collective-permute-start(bf16[16,160,128]{2,1,0:T(8,128)(2,1)} %bitcast.314), channel_id=1, source_target_pairs={{0,16},{2,18},{4,20},{6,22},{8,24},{10,26},{12,28},{14,30},{16,0},... | collective-permute-start | bytes 1966088 | tf_op jit(solution)/shard_map/ppermute | solution.py:1021
  15.1 114.0 %collective-permute-start.12 = (bf16[12,6,1024]{2,1,0:T(8,128)(2,1)}, bf16[12,6,1024]{2,1,0:T(8,128)(2,1)}, u32[]{:S(2)}, u32[]{:S(2)}) collective-permute-start(bf16[12,6,1024]{2,1,0:T(8,128)(2,1)} %add_convert_fusion.1), channel_id=1, source_target_pairs={{0,1},{1,0},{2,3},{3,2},{4,5},{5,4},{6,7},{7,6},{8,9},{9,8},{10,11... | collective-permute-start | bytes 442376 | tf_op jit(solution)/shard_map/ppermute | solution.py:1005
  16.7 36.1 %collective-permute-start.13 = (f32[2,2048]{1,0:T(2,128)}, f32[2,2048]{1,0:T(2,128)}, u32[]{:S(2)}, u32[]{:S(2)}) collective-permute-start(f32[2,2048]{1,0:T(2,128)} %pad_maximum_fusion.44), channel_id=1, source_target_pairs={{0,1},{1,0},{2,3},{3,2},{4,5},{5,4},{6,7},{7,6},{8,9},{9,8},{10,11... | collective-permute-start | bytes 49160 | tf_op jit(solution)/shard_map/ppermute | solution.py:1005
  17.7 61.5 %collective-permute-start.14 = (f32[12,6,81]{0,2,1:T(8,128)}, f32[12,6,81]{0,2,1:T(8,128)}, u32[]{:S(2)}, u32[]{:S(2)}) collective-permute-start(f32[12,6,81]{0,2,1:T(8,128)} %maximum_convert_fusion.1), channel_id=1, source_target_pairs={{0,2},{2,0},{4,6},{6,4},{8,10},{10,8},{12,14},{14,12},{16,18},{18,... | collective-permute-start | bytes 69992 | tf_op jit(solution)/shard_map/ppermute | solution.py:1021
  18.9 27.5 %collective-permute-start.25 = (f32[2,40]{1,0:T(2,128)}, f32[2,40]{1,0:T(2,128)}, u32[]{:S(2)}, u32[]{:S(2)}) collective-permute-start(f32[2,40]{1,0:T(2,128)} %param.51), channel_id=1, source_target_pairs={{0,1},{1,0},{2,3},{3,2},{4,5},{5,4},{6,7},{7,6},{8,9},{9,8},{10,11... | collective-permute-start | bytes 968 | tf_op jit(solution)/shard_map/ppermute | solution.py:1005
  46.4 29.9 %collective-permute-start.1 = (bf16[2,16,160,128]{3,2,1,0:T(8,128)(2,1)S(1)}, bf16[2,16,160,128]{3,2,1,0:T(8,128)(2,1)S(1)}, u32[]{:S(2)}, u32[]{:S(2)}) collective-permute-start(bf16[2,16,160,128]{3,2,1,0:T(8,128)(2,1)S(1)} %pad_maximum_fusion.10), channel_id=1, source_target_pairs={{0,8},{2,10},{4,12},{6,14},{8,0},{10,2},{12,4},{14,6},{16,24},{18,... | collective-permute-start | bytes 3932168 | tf_op jit(solution)/shard_map/ppermute | solution.py:1021
  51.5 30.9 %collective-permute-start.20 = (bf16[64,200]{1,0:T(8,128)(2,1)S(1)}, bf16[64,200]{1,0:T(8,128)(2,1)S(1)}, u32[]{:S(2)}, u32[]{:S(2)}) collective-permute-start(bf16[64,200]{1,0:T(8,128)(2,1)S(1)} %pad_maximum_fusion.41), channel_id=1, source_target_pairs={{0,4},{2,6},{4,0},{6,2},{8,12},{10,14},{12,8},{14,10},{16,20},{18,... | collective-permute-start | bytes 76808 | tf_op jit(solution)/shard_map/ppermute | solution.py:1021
  77.0 29.0 %collective-permute-start.10 = (bf16[2,2,8,160,128]{4,3,2,1,0:T(8,128)(2,1)S(1)}, bf16[2,2,8,160,128]{4,3,2,1,0:T(8,128)(2,1)S(1)}, u32[]{:S(2)}, u32[]{:S(2)}) collective-permute-start(bf16[2,2,8,160,128]{4,3,2,1,0:T(8,128)(2,1)S(1)} %get-tuple-element.390), channel_id=1, source_target_pairs={{0,4},{2,6},{4,0},{6,2},{8,12},{10,14},{12,8},{14,10},{16,20},{18,... | collective-permute-start | bytes 3932168 | tf_op jit(solution)/shard_map/ppermute | solution.py:1021
  78.3 29.0 %collective-permute-start.8 = (bf16[2,2,8,160,128]{4,3,2,1,0:T(8,128)(2,1)S(1)}, bf16[2,2,8,160,128]{4,3,2,1,0:T(8,128)(2,1)S(1)}, u32[]{:S(2)}, u32[]{:S(2)}) collective-permute-start(bf16[2,2,8,160,128]{4,3,2,1,0:T(8,128)(2,1)S(1)} %get-tuple-element.391), channel_id=1, source_target_pairs={{0,2},{2,0},{4,6},{6,4},{8,10},{10,8},{12,14},{14,12},{16,18},{18,... | collective-permute-start | bytes 3932168 | tf_op jit(solution)/shard_map/ppermute | solution.py:1021
  79.2 22.1 %collective-permute-start.2 = (bf16[16,112,128]{2,1,0:T(8,128)(2,1)S(1)}, bf16[16,112,128]{2,1,0:T(8,128)(2,1)S(1)}, u32[]{:S(2)}, u32[]{:S(2)}) collective-permute-start(bf16[16,112,128]{2,1,0:T(8,128)(2,1)S(1)} %bitcast.347), channel_id=1, source_target_pairs={{0,16},{2,18},{4,20},{6,22},{8,24},{10,26},{12,28},{14,30},{16,0},... | collective-permute-start | bytes 1376264 | tf_op jit(solution)/shard_map/ppermute | solution.py:1021
  82.4 41.3 %collective-permute-start.15 = (f32[24,6,81]{0,2,1:T(8,128)S(1)}, f32[24,6,81]{0,2,1:T(8,128)S(1)}, u32[]{:S(2)}, u32[]{:S(2)}) collective-permute-start(f32[24,6,81]{0,2,1:T(8,128)S(1)} %pad_maximum_fusion.22), channel_id=1, source_target_pairs={{0,4},{2,6},{4,0},{6,2},{8,12},{10,14},{12,8},{14,10},{16,20},{18,... | collective-permute-start | bytes 139976 | tf_op jit(solution)/shard_map/ppermute | solution.py:1021
  106.0 20.6 %collective-permute-start.21 = (bf16[128,200]{1,0:T(8,128)(2,1)S(1)}, bf16[128,200]{1,0:T(8,128)(2,1)S(1)}, u32[]{:S(2)}, u32[]{:S(2)}) collective-permute-start(bf16[128,200]{1,0:T(8,128)(2,1)S(1)} %pad_maximum_fusion.37), channel_id=1, source_target_pairs={{0,8},{2,10},{4,12},{6,14},{8,0},{10,2},{12,4},{14,6},{16,24},{18,... | collective-permute-start | bytes 153608 | tf_op jit(solution)/shard_map/ppermute | solution.py:1021
  107.9 81.4 %collective-permute-start.11 = (bf16[2,2,2,8,160,128]{5,4,3,2,1,0:T(8,128)(2,1)S(1)}, bf16[2,2,2,8,160,128]{5,4,3,2,1,0:T(8,128)(2,1)}, u32[]{:S(2)}, u32[]{:S(2)}) collective-permute-start(bf16[2,2,2,8,160,128]{5,4,3,2,1,0:T(8,128)(2,1)S(1)} %pad_maximum_fusion.3.refs_10_), channel_id=1, source_target_pairs={{0,2},{2,0},{4,6},{6,4},{8,10},{10,8},{12,14},{14,12},{16,18},{18,... | collective-permute-start | bytes 7864328 | tf_op jit(solution)/shard_map/ppermute | solution.py:1054
  122.0 132.2 %collective-permute-start.9 = (bf16[2,2,2,8,160,128]{5,4,3,2,1,0:T(8,128)(2,1)}, bf16[2,2,2,8,160,128]{5,4,3,2,1,0:T(8,128)(2,1)}, u32[]{:S(2)}, u32[]{:S(2)}) collective-permute-start(bf16[2,2,2,8,160,128]{5,4,3,2,1,0:T(8,128)(2,1)} %pad_maximum_fusion.2.refs_8_), channel_id=1, source_target_pairs={{0,4},{2,6},{4,0},{6,2},{8,12},{10,14},{12,8},{14,10},{16,20},{18,... | collective-permute-start | bytes 7864328 | tf_op jit(solution)/shard_map/ppermute | solution.py:1054
  123.7 57.9 %collective-permute-start.4 = (bf16[2,2,8,112,128]{4,3,2,1,0:T(8,128)(2,1)}, bf16[2,2,8,112,128]{4,3,2,1,0:T(8,128)(2,1)}, u32[]{:S(2)}, u32[]{:S(2)}) collective-permute-start(bf16[2,2,8,112,128]{4,3,2,1,0:T(8,128)(2,1)} %get-tuple-element.397), channel_id=1, source_target_pairs={{0,2},{2,0},{4,6},{6,4},{8,10},{10,8},{12,14},{14,12},{16,18},{18,... | collective-permute-start | bytes 2752520 | tf_op jit(solution)/shard_map/ppermute | solution.py:1021
  126.6 60.3 %collective-permute-start.16 = (f32[48,6,81]{0,2,1:T(8,128)}, f32[48,6,81]{0,2,1:T(8,128)}, u32[]{:S(2)}, u32[]{:S(2)}) collective-permute-start(f32[48,6,81]{0,2,1:T(8,128)} %pad_maximum_fusion.23), channel_id=1, source_target_pairs={{0,8},{2,10},{4,12},{6,14},{8,0},{10,2},{12,4},{14,6},{16,24},{18,... | collective-permute-start | bytes 279944 | tf_op jit(solution)/shard_map/ppermute | solution.py:1021
  129.1 76.4 %collective-permute-start.22 = (bf16[256,200]{1,0:T(8,128)(2,1)}, bf16[256,200]{1,0:T(8,128)(2,1)}, u32[]{:S(2)}, u32[]{:S(2)}) collective-permute-start(bf16[256,200]{1,0:T(8,128)(2,1)} %pad_maximum_fusion.33), channel_id=1, source_target_pairs={{0,16},{2,18},{4,20},{6,22},{8,24},{10,26},{12,28},{14,30},{16,0},... | collective-permute-start | bytes 307208 | tf_op jit(solution)/shard_map/ppermute | solution.py:1021
  184.6 74.4 %collective-permute-start.5 = (bf16[2,2,2,8,112,128]{5,4,3,2,1,0:T(8,128)(2,1)}, bf16[2,2,2,8,112,128]{5,4,3,2,1,0:T(8,128)(2,1)}, u32[]{:S(2)}, u32[]{:S(2)}) collective-permute-start(bf16[2,2,2,8,112,128]{5,4,3,2,1,0:T(8,128)(2,1)} %pad_maximum_fusion.6.refs_0_), channel_id=1, source_target_pairs={{0,4},{2,6},{4,0},{6,2},{8,12},{10,14},{12,8},{14,10},{16,20},{18,... | collective-permute-start | bytes 5505032 | tf_op jit(solution)/shard_map/ppermute | solution.py:1054
  186.9 59.5 %collective-permute-start.6 = (bf16[2,2,8,112,128]{4,3,2,1,0:T(8,128)(2,1)}, bf16[2,2,8,112,128]{4,3,2,1,0:T(8,128)(2,1)}, u32[]{:S(2)}, u32[]{:S(2)}) collective-permute-start(bf16[2,2,8,112,128]{4,3,2,1,0:T(8,128)(2,1)} %get-tuple-element.396), channel_id=1, source_target_pairs={{0,4},{2,6},{4,0},{6,2},{8,12},{10,14},{12,8},{14,10},{16,20},{18,... | collective-permute-start | bytes 2752520 | tf_op jit(solution)/shard_map/ppermute | solution.py:1021
  189.3 21.4 %collective-permute-start.18 = (bf16[5,80,256]{2,1,0:T(8,128)(2,1)}, bf16[5,80,256]{2,1,0:T(8,128)(2,1)}, u32[]{:S(2)}, u32[]{:S(2)}) collective-permute-start(bf16[5,80,256]{2,1,0:T(8,128)(2,1)} %param.47), channel_id=1, source_target_pairs={{0,1},{1,0},{2,3},{3,2},{4,5},{5,4},{6,7},{7,6},{8,9},{9,8},{10,11... | collective-permute-start | bytes 614408 | tf_op jit(solution)/shard_map/ppermute | solution.py:1005
  195.2 353.5 %all-gather.3.cloned.1.call-start = ((), (), s32[]{:S(2)}) async-start(), calls=%async_computation.2 | async-start | bytes 7659520 | tf_op jit(solution)/shard_map/all_gather | solution.py:1297
  224.2 82.5 %collective-permute-start.26 = (bf16[2,2,2,8,160,128]{5,4,3,2,1,0:T(8,128)(2,1)}, bf16[2,2,2,8,160,128]{5,4,3,2,1,0:T(8,128)(2,1)}, u32[]{:S(2)}, u32[]{:S(2)}) collective-permute-start(bf16[2,2,2,8,160,128]{5,4,3,2,1,0:T(8,128)(2,1)} %pad_maximum_fusion.2.refs_8_), channel_id=1, source_target_pairs={{0,1},{1,0},{2,3},{3,2},{4,5},{5,4},{6,7},{7,6},{8,9},{9,8},{10,11... | collective-permute-start | bytes 7864328 | tf_op jit(solution)/shard_map/ppermute | solution.py:1005
  224.9 81.8 %collective-permute-start.28 = (bf16[2,2,2,8,160,128]{5,4,3,2,1,0:T(8,128)(2,1)S(1)}, bf16[2,2,2,8,160,128]{5,4,3,2,1,0:T(8,128)(2,1)}, u32[]{:S(2)}, u32[]{:S(2)}) collective-permute-start(bf16[2,2,2,8,160,128]{5,4,3,2,1,0:T(8,128)(2,1)S(1)} %pad_maximum_fusion.3.refs_10_), channel_id=1, source_target_pairs={{0,1},{1,0},{2,3},{3,2},{4,5},{5,4},{6,7},{7,6},{8,9},{9,8},{10,11... | collective-permute-start | bytes 7864328 | tf_op jit(solution)/shard_map/ppermute | solution.py:1005
  246.4 60.4 %collective-permute-start.29 = (bf16[2,2,2,8,160,128]{5,4,3,2,1,0:T(8,128)(2,1)}, bf16[2,2,2,8,160,128]{5,4,3,2,1,0:T(8,128)(2,1)}, u32[]{:S(2)}, u32[]{:S(2)}) collective-permute-start(bf16[2,2,2,8,160,128]{5,4,3,2,1,0:T(8,128)(2,1)} %collective-permute-done.11.refs_11_), channel_id=1, source_target_pairs={{0,1},{1,0},{2,3},{3,2},{4,5},{5,4},{6,7},{7,6},{8,9},{9,8},{10,11... | collective-permute-start | bytes 7864328 | tf_op jit(solution)/shard_map/ppermute | solution.py:1005
  254.2 52.5 %collective-permute-start.27 = (bf16[2,2,2,8,160,128]{5,4,3,2,1,0:T(8,128)(2,1)}, bf16[2,2,2,8,160,128]{5,4,3,2,1,0:T(8,128)(2,1)}, u32[]{:S(2)}, u32[]{:S(2)}) collective-permute-start(bf16[2,2,2,8,160,128]{5,4,3,2,1,0:T(8,128)(2,1)} %collective-permute-done.9.refs_9_), channel_id=1, source_target_pairs={{0,1},{1,0},{2,3},{3,2},{4,5},{5,4},{6,7},{7,6},{8,9},{9,8},{10,11... | collective-permute-start | bytes 7864328 | tf_op jit(solution)/shard_map/ppermute | solution.py:1005
  259.1 45.2 %collective-permute-start.7 = (bf16[2,2,2,8,112,128]{5,4,3,2,1,0:T(8,128)(2,1)}, bf16[2,2,2,8,112,128]{5,4,3,2,1,0:T(8,128)(2,1)}, u32[]{:S(2)}, u32[]{:S(2)}) collective-permute-start(bf16[2,2,2,8,112,128]{5,4,3,2,1,0:T(8,128)(2,1)} %pad_maximum_fusion.7.refs_2_), channel_id=1, source_target_pairs={{0,2},{2,0},{4,6},{6,4},{8,10},{10,8},{12,14},{14,12},{16,18},{18,... | collective-permute-start | bytes 5505032 | tf_op jit(solution)/shard_map/ppermute | solution.py:1054
  513.3 33.2 %all-to-all-start = ((bf16[16,80,512]{2,1,0:T(8,128)(2,1)}), bf16[16,80,512]{2,1,0:T(8,128)(2,1)}, u32[]{:S(2)}, u32[]{:S(2)}) async-start(bf16[16,80,512]{2,1,0:T(8,128)(2,1)} %get-tuple-element.166), calls=%async_computation | async-start | bytes 2621440 | tf_op jit(solution)/shard_map/all_to_all | solution.py:1468
  574.8 40.6 %all-to-all-start.1 = ((bf16[16,400,128]{2,1,0:T(8,128)(2,1)}), bf16[16,400,128]{2,1,0:T(8,128)(2,1)S(1)}, u32[]{:S(2)}, u32[]{:S(2)}) async-start(bf16[16,400,128]{2,1,0:T(8,128)(2,1)} %pad_maximum_fusion.9), calls=%async_computation.1 | async-start | bytes 3276800 | tf_op jit(solution)/shard_map/all_to_all | solution.py:1613
  588.2 49.7 %collective-permute-start.46 = (f32[5,80,256]{2,1,0:T(8,128)}, f32[5,80,256]{2,1,0:T(8,128)}, u32[]{:S(2)}, u32[]{:S(2)}) collective-permute-start(f32[5,80,256]{2,1,0:T(8,128)} %slice_select_fusion.2), channel_id=1, source_target_pairs={{0,1},{1,0},{2,3},{3,2},{4,5},{5,4},{6,7},{7,6},{8,9},{9,8},{10,11... | collective-permute-start | bytes 1228808 | tf_op jit(solution)/shard_map/ppermute | solution.py:1005
  602.7 37.1 %collective-permute-start.47 = (f32[3,5,32,256]{3,2,1,0:T(8,128)}, f32[3,5,32,256]{3,2,1,0:T(8,128)}, u32[]{:S(2)}, u32[]{:S(2)}) collective-permute-start(f32[3,5,32,256]{3,2,1,0:T(8,128)} %slice_select_fusion.1), channel_id=1, source_target_pairs={{0,1},{1,0},{2,3},{3,2},{4,5},{5,4},{6,7},{7,6},{8,9},{9,8},{10,11... | collective-permute-start | bytes 1474568 | tf_op jit(solution)/shard_map/ppermute | solution.py:1005
  603.9 28.7 %collective-permute-start.48 = (f32[5,32,40]{2,1,0:T(8,128)}, f32[5,32,40]{2,1,0:T(8,128)}, u32[]{:S(2)}, u32[]{:S(2)}) collective-permute-start(f32[5,32,40]{2,1,0:T(8,128)} %slice_select_fusion.3), channel_id=1, source_target_pairs={{0,1},{1,0},{2,3},{3,2},{4,5},{5,4},{6,7},{7,6},{8,9},{9,8},{10,11... | collective-permute-start | bytes 76808 | tf_op jit(solution)/shard_map/ppermute | solution.py:1005
  (115 other events, 876.2 us)
Sparse Core Ops, SparseCore 0:
  195.3 83.0 all-gather.4
  386.5 103.2 all-gather.2

commit v3 on v2

--- a/solution.py
+++ b/solution.py
@@ -77,30 +77,32 @@
     return pl.multiple_of(start * lanes, lanes)
 
 
-def weight_copies(refs, held, place, sems, start):
-    if len(refs) == 2:
-        return [
-            pltpu.make_async_copy(ref, held.at[side], sems.at[start + side])
-            for side, ref in enumerate(refs)
-        ]
-    copies = []
-    for index, ref in enumerate(refs):
-        side, turn, which = index // 4, index // 2 % 2, index % 2
-        _, _, _, tiles, rows, _ = ref.shape
-        near, last = (1, 2) if turn == 0 else (2, 1)
-        bit = (place // last + which) % 2
-        for k in range(2):
-            for far in range(4):
-                device = far * 4 + k * near + bit * last
-                spot = pl.ds(pl.multiple_of(device * rows, 16), rows)
-                copies.append(
-                    pltpu.make_async_copy(
-                        ref.at[k, far // 2, far % 2],
-                        held.at[side, turn * tiles : (turn + 1) * tiles, spot, :],
-                        sems.at[start + len(copies)],
-                    )
+def weight_copies(refs, held_one, held_two, sems):
+    copies_one, copies_two = [], []
+
+    def copy(copies, source, target):
+        count = len(copies_one) + len(copies_two)
+        copies.append(pltpu.make_async_copy(source, target, sems.at[count]))
+
+    if len(refs) == 4:
+        for side in range(2):
+            copy(copies_one, refs[side], held_one.at[side])
+            copy(copies_two, refs[2 + side], held_two.at[side])
+        return copies_one, copies_two
+    devices = refs[0].shape[1]
+    rows_one, rows_two = held_one.shape[2] // devices, held_two.shape[2] // devices
+    for held, copies, rows, start in (
+        (held_two, copies_two, rows_two, rows_one),
+        (held_one, copies_one, rows_one, 0),
+    ):
+        for side in range(2):
+            for device in range(devices):
+                copy(
+                    copies,
+                    refs[side].at[:, device, start : start + rows, :],
+                    held.at[side, :, device * rows : (device + 1) * rows, :],
                 )
-    return copies
+    return copies_one, copies_two
 
 
 def forward_kernel(
@@ -178,9 +180,7 @@
     per_half = half // lanes
     position_count = hot_ref.shape[0]
     text_width = position_count // (slots // 4)
-    each = len(weight_refs) // 2
-    copies_two = weight_copies(weight_refs[each:], held_two, unit_ref[1], sems, 0)
-    copies_one = weight_copies(weight_refs[:each], held_one, unit_ref[1], sems, len(copies_two))
+    copies_one, copies_two = weight_copies(weight_refs, held_one, held_two, sems)
     for copy in copies_two + copies_one:
         copy.start()
     for ref in (state_one, cell_one, state_two, cell_two):
@@ -378,9 +378,7 @@
     per_half = half // lanes
     position_count = hot_ref.shape[0]
     text_width = position_count // (slots // 4)
-    each = len(weight_refs) // 2
-    copies_two = weight_copies(weight_refs[each:], held_two, unit_ref[1], sems, 0)
-    copies_one = weight_copies(weight_refs[:each], held_one, unit_ref[1], sems, len(copies_two))
+    copies_one, copies_two = weight_copies(weight_refs, held_one, held_two, sems)
     for copy in copies_two + copies_one:
         copy.start()
     for ref in (
@@ -608,7 +606,7 @@
             pltpu.VMEM((slots, hidden), f32),
             pltpu.VMEM((slots, hidden), f32),
             pltpu.VMEM((slots, hidden), f32),
-            pltpu.SemaphoreType.DMA((8 * len(weights),)),
+            pltpu.SemaphoreType.DMA((4 if len(weights) == 4 else 4 * weights[0].shape[1],)),
         ],
         compiler_params=pltpu.CompilerParams(vmem_limit_bytes=kernel_vmem),
         name="decoder_forward",
@@ -660,7 +658,7 @@
             pltpu.VMEM((slots, hidden), f32),
             pltpu.VMEM((steps, slots, hidden + context_width), f32),
             pltpu.VMEM((2, lanes, lanes), f32),
-            pltpu.SemaphoreType.DMA((8 * len(weights),)),
+            pltpu.SemaphoreType.DMA((4 if len(weights) == 4 else 4 * weights[0].shape[1],)),
         ],
         compiler_params=pltpu.CompilerParams(vmem_limit_bytes=kernel_vmem),
         name="decoder_backward",
@@ -1041,37 +1039,20 @@
     def to_tiles(value):
         return jnp.transpose(value.reshape(value.shape[0], -1, lanes), (1, 0, 2))
 
-    def along_z(value):
-        value = jnp.stack(swapped(value, 8))
-        return jnp.stack(swapped(value, 4), axis=1)
-
-    def in_plane(value):
-        pieces = []
-        tall = value.shape[2] // 2
-        for turn, (near, last) in enumerate(((1, 2), (2, 1))):
-            part = jnp.stack(swapped(value[:, :, turn * tall : (turn + 1) * tall], near))
-            pairs = [(index, index ^ last) for index in range(batch_size)]
-            pieces += [part, lax.ppermute(part, "batch", pairs)]
-        return tuple(pieces)
-
-    crossed = batch_size == 16 and depth_one % 16 == 0 and depth_two % 16 == 0
-    if crossed:
-        line_two = along_z(to_tiles(lstm_second))
-        tiles_one, line_two = lax.optimization_barrier((to_tiles(lstm_first), line_two))
-        line_one = along_z(tiles_one)
-        own_two = in_plane(line_two)
-        own_one = in_plane(line_one)
-        peer_two = tuple(exchange(value) for value in own_two)
-        post_source = lax.optimization_barrier((post_middle, own_two[-1]))[0]
+    together = depth_one % 16 == 0 and depth_two % 16 == 0
+
+    def gathered(value):
+        return lax.all_gather(value, "batch", axis=1, tiled=True)
+
+    if together:
+        both = jnp.concatenate([to_tiles(lstm_first), to_tiles(lstm_second)], axis=1)
+        own = (gathered(both).reshape(both.shape[0], batch_size, both.shape[1], lanes),)
     else:
-        own_two = (lax.all_gather(to_tiles(lstm_second), "batch", axis=1, tiled=True),)
-        own_one = (lax.all_gather(to_tiles(lstm_first), "batch", axis=1, tiled=True),)
-        peer_two = (exchange(own_two[0]),)
-        post_source = post_middle
+        own = (gathered(to_tiles(lstm_first)), gathered(to_tiles(lstm_second)))
     channel_rows = post_middle.shape[2]
     middle_width = post_middle.shape[3]
     middle_half = lax.all_gather(
-        post_source.reshape(-1, channel_rows, middle_width), "batch", axis=1, tiled=True
+        post_middle.reshape(-1, channel_rows, middle_width), "batch", axis=1, tiled=True
     )
     last_half = gather_rows(jnp.transpose(post_last, (1, 0, 2)).reshape(channel_rows, -1))
     last_half = jnp.transpose(
@@ -1172,7 +1153,7 @@
     vector_wide = jnp.broadcast_to(vector_float[:, None], (attention_width, lanes))
     memory_float = memory_now.astype(f32)
     query_float = query_weight.astype(f32)
-    unit_array = jnp.stack([unit, place]).astype(jnp.int32)
+    unit_array = unit.astype(jnp.int32).reshape(1)
 
     targets_all = jnp.transpose(frame_info[:, :, :mel_width].astype(f32), (1, 0, 2))
     segments_all = jnp.transpose(frame_info[:, :, mel_width].astype(jnp.int32))
@@ -1213,8 +1194,7 @@
         frame_bias_wide,
     )
     (
-        own_one,
-        own_two,
+        own,
         forward_small,
         taps_back,
         vector_row,
@@ -1225,8 +1205,7 @@
         norms,
     ) = lax.optimization_barrier(
         (
-            own_one,
-            own_two,
+            own,
             forward_small,
             taps_back,
             vector_float[None, :],
@@ -1237,9 +1216,7 @@
             norms,
         )
     )
-    own_one, peer_two = lax.optimization_barrier((own_one, peer_two))
-    peer_one = tuple(exchange(value) for value in own_one)
-    weights = own_one + peer_one + own_two + peer_two
+    weights = sum(((value, exchange(value)) for value in own), ())
     slot_wide, zone_one, zone_two = forward_small[5], forward_small[6], forward_small[7]
     memory_float, query_float = forward_small[11], forward_small[13]
     dense_wide, frame_wide = forward_small[16], forward_small[17]

time: 683 us -> 611 us (0.89)
  starting transfers between devices: 92.9 us -> 59.9 us
  other arithmetic: 82.7 us -> 58.3 us
  local copies, waits for them, and re-layouts: 69 us -> 56.4 us
  waiting for transfers between devices: 226 us -> 235 us
    all_gather x1 -> x2, waiting for transfers between devices: 0.02 us -> 133 us  [the longest x1 133 us: gathered(): return lax.all_gather(value, 'batch', axis=1, tiled=True)]
    ppermute x24 -> x16, waiting for transfers between devices: 155 us -> 53.2 us  [swapped(): other = lax.ppermute(value, 'batch', pairs)]
    ppermute x4 -> x0, waiting for transfers between devices: 36.1 us -> none  [in_plane(): pieces += [part, lax.ppermute(part, 'batch', pairs)]]
    ppermute x24 -> x17, waiting for transfers between devices: 20.1 us -> 36 us  [exchange(): return lax.ppermute(value, 'unit', [(0, 1), (1, 0)])]
    another operation x21 -> x5, other arithmetic: 15.4 us -> 2.14 us  [the longest x7 8.57 us: in_plane(): part = jnp.stack(swapped(value[:, :, turn * tall:(turn + 1) * tall], near))]
    ppermute x24 -> x16, starting transfers between devices: 36.5 us -> 23.9 us  [swapped(): other = lax.ppermute(value, 'batch', pairs)]
    all_gather x1, starting transfers between devices: 10.2 us -> 0.51 us  [on_device(): inputs_all = lax.all_gather(inputs_own, 'batch', axis=0, tiled=True)]
    ppermute x24 -> x17, starting transfers between devices: 30.7 us -> 23.4 us  [exchange(): return lax.ppermute(value, 'unit', [(0, 1), (1, 0)])]
  transfers between devices with their start and end apart: 56 -> 38, of which waited for: 24 -> 19; matrix products, arithmetic and copies ran while one was open for 22% -> 18% of each run, Pallas kernels for 23% -> 25%
where the time goes in v3:
time: 611 us; the launch traced here: 603 us
  waiting for transfers between devices  235 us (38%)
  Pallas kernels  152 us (25%)
  starting transfers between devices  59.9 us (10%)
  other arithmetic  58.3 us (10%)
  local copies, waits for them, and re-layouts  56.4 us (9%)
  matrix products  25.2 us (4%)
  between operations  16.1 us (3%)
    all_gather x1, waiting for transfers between devices, gathered(): return lax.all_gather(value, 'batch', axis=1, tiled=True)  133 us
    pallas_call x1, Pallas kernels, call_backward(): pl.pallas_call(functools.partial(backward_kernel, len(weights)), out_shap...  58.7 us
    pallas_call x1, Pallas kernels, call_postnet(): pl.pallas_call(functools.partial(postnet_kernel, mel_width, loss_scale),...  54.7 us
    ppermute x16, waiting for transfers between devices, swapped(): other = lax.ppermute(value, 'batch', pairs)  53.2 us
    pallas_call x1, Pallas kernels, call_forward(): pl.pallas_call(functools.partial(forward_kernel, len(weights)), out_shape...  38.5 us
    ppermute x17, waiting for transfers between devices, exchange(): return lax.ppermute(value, 'unit', [(0, 1), (1, 0)])  36 us
    ppermute x16, starting transfers between devices, swapped(): other = lax.ppermute(value, 'batch', pairs)  23.9 us
    ppermute x17, starting transfers between devices, exchange(): return lax.ppermute(value, 'unit', [(0, 1), (1, 0)])  23.4 us
  transfers between devices with their start and end apart: 38, of which 19 were waited for; matrix products, arithmetic and copies ran while one was open for 18% of the time, Pallas kernels for 25%

profile of v3, /device:TPU:1, one launch (start us, length us, event | category | flops | bytes accessed | tf_op | source)
XLA Modules:
  0.0 602.7 jit_solution(4259903728710147923)
XLA Ops:
  14.2 2.2 collective-permute-start.2
  34.4 2.9 collective-permute-done.7
  42.2 5.1 collective-permute-done.3
  50.3 2.3 collective-permute-start.10
  59.8 8.9 %collective-permute-start.11 = (bf16[5,512,40]{1,2,0:T(8,128)(2,1)S(1)}, bf16[5,512,40]{1,2,0:T(8,128)(2,1)}, u32[]{:S(2)}, u32[]{:S(2)}) collective-permute-start(bf16[5,512,40]{1,2,0:T(8,128)(2,1)S(1)} %bitcast.326), channel_id=1, source_target_pairs={{0,1},{1,0},{2,3},{3,2},{4,5},{5,4},{6,7},{7,6},{8,9},{9,8},{10,11... | collective-permute-start | bytes 614408 | tf_op jit(solution)/shard_map/ppermute | solution.py:1003
  70.9 19.9 %collective-permute-done.5 = f32[96,6,81]{0,2,1:T(8,128)} collective-permute-done((f32[96,6,81]{0,2,1:T(8,128)}, f32[96,6,81]{0,2,1:T(8,128)}, u32[]{:S(2)}, u32[]{:S(2)}) %collective-permute-start.5) | collective-permute-done | bytes 186656 | tf_op jit(solution)/shard_map/ppermute | solution.py:1019
  95.3 132.9 %all-gather.4.cloned.1.call-done = bf16[16,4352,128]{2,1,0:T(8,128)(2,1)} async-done(((bf16[16,272,128]{2,1,0:T(8,128)(2,1)}), bf16[16,4352,128]{2,1,0:T(8,128)(2,1)}) %all-gather.4.cloned.1.call-update) | async-done | bytes 17825808 | tf_op jit(solution)/shard_map/all_gather | solution.py:1045
  232.3 26.1 %collective-permute-done.14.refs_1_ = bf16[16,16,272,128]{3,2,1,0:T(8,128)(2,1)} collective-permute-done((bf16[16,16,272,128]{3,2,1,0:T(8,128)(2,1)}, bf16[16,16,272,128]{3,2,1,0:T(8,128)(2,1)}, u32[]{:S(2)}, u32[]{:S(2)}) %collective-permute-start.14) | collective-permute-done | bytes 17825824 | tf_op jit(solution)/shard_map/ppermute | solution.py:1003
  258.4 38.5 %decoder_forward.1 = (f32[3,48,4096]{2,1,0:T(8,128)}, f32[3,48,4096]{2,1,0:T(8,128)}, f32[3,48,1024]{2,1,0:T(8,128)}, f32[3,48,1024]{2,1,0:T(8,128)}, f32[3,48,1...) custom-call(s32[1]{0:T(128)} %bitcast.unit_ref, ...), custom_call_target="tpu_custom_call" | custom-call | tf_op jit(solution)/shard_map/decoder_forward/pallas_call | solution.py:591
  305.0 3.6 collective-permute-done.17
  310.8 13.6 %collective-permute-done.18 = f32[96,6,80]{2,0,1:T(8,128)S(1)} collective-permute-done((f32[96,6,80]{2,0,1:T(8,128)S(1)}, f32[96,6,80]{2,0,1:T(8,128)S(1)}, u32[]{:S(2)}, u32[]{:S(2)}) %collective-permute-start.18) | collective-permute-done | bytes 184352 | tf_op jit(solution)/shard_map/ppermute | solution.py:1019
  328.6 4.5 collective-permute-done.19.peer_ref
  333.1 54.7 %postnet.1 = (bf16[1152,80]{1,0:T(8,128)(2,1)}, bf16[4,1152,512]{2,1,0:T(8,128)(2,1)}, bf16[4,1152,512]{2,1,0:T(8,128)(2,1)}, bf16[1152,80]{1,0:T(8,128)(2,1)}, ...) custom-call(s32[1]{0:T(128)} %bitcast.unit_ref, f32[1152,80]{1,0:T(8,128)} %bitcast.304, f32[1152,80]{1,0:T(8,128)} %bitcast.305, ...), custom_call_target="tpu_custom_call" | custom-call | tf_op jit(solution)/shard_map/postnet/pallas_call | solution.py:892
  389.7 58.7 %decoder_backward.1 = (bf16[16,80,512]{2,1,0:T(8,128)(2,1)}, f32[3,48,256]{2,1,0:T(8,128)}, f32[3,48,512]{2,1,0:T(8,128)}, f32[3,48,128]{2,1,0:T(8,128)}, f32[76...) custom-call(s32[1]{0:T(128)} %bitcast.unit_ref, bf16[16,16,272,128]{3,2,1,0:T(8,128)(2,1)} %bitcast.291, ...), custom_call_target="tpu_custom_call" | custom-call | tf_op jit(solution)/shard_map/decoder_backward/pallas_call | solution.py:638
  450.1 4.8 all-to-all-start
  462.2 2.4 concatenate.201
  466.5 2.3 collective-permute-done.20
  468.8 2.2 select_add_fusion
  471.0 10.6 %all-to-all-done = bf16[16,80,512]{2,1,0:T(8,128)(2,1)} async-done(((bf16[16,80,512]{2,1,0:T(8,128)(2,1)}), bf16[16,80,512]{2,1,0:T(8,128)(2,1)}, u32[]{:S(2)}, u32[]{:S(2)}) %all-to-all-start) | async-done | bytes 1310752 | tf_op jit(solution)/shard_map/all_to_all | solution.py:1445
  483.8 2.8 fusion.2
  487.6 2.3 fusion
  494.7 3.4 collective-permute-start.21
  498.8 3.1 collective-permute-done.31
  503.2 2.8 add_convert_fusion
  507.3 7.3 %all-to-all-start.1 = ((bf16[16,400,128]{2,1,0:T(8,128)(2,1)}), bf16[16,400,128]{2,1,0:T(8,128)(2,1)S(1)}, u32[]{:S(2)}, u32[]{:S(2)}) async-start(bf16[16,400,128]{2,1,0:T(8,128)(2,1)} %pad_maximum_fusion.4), calls=%async_computation.1 | async-start | bytes 3276800 | tf_op jit(solution)/shard_map/all_to_all | solution.py:1590
  514.7 4.0 fusion.122
  521.9 4.2 fusion.121
  540.8 2.5 fusion.25
  543.4 2.5 fusion.27
  548.0 7.1 %collective-permute-start.22 = (bf16[128,128]{1,0:T(8,128)(2,1)S(1)}, bf16[128,128]{1,0:T(8,128)(2,1)S(1)}, u32[]{:S(2)}, u32[]{:S(2)}) collective-permute-start(bf16[128,128]{1,0:T(8,128)(2,1)S(1)} %slice_reduce_fusion), channel_id=1, source_target_pairs={{0,16},{2,18},{4,20},{6,22},{8,24},{10,26},{12,28},{14,30},{16,0},... | collective-permute-start | bytes 98312 | tf_op jit(solution)/shard_map/ppermute | solution.py:1019
  556.6 3.1 add_add_fusion
  559.7 3.6 collective-permute-start.32
  (461 shorter events, 141.8 us)
Async XLA Ops:
  7.2 221.0 %all-gather.4.cloned.1.call-start = ((), (), s32[]{:S(2)}) async-start(), calls=%async_computation.2 | async-start | bytes 18939904 | tf_op jit(solution)/shard_map/all_gather | solution.py:1045
  10.6 314.6 %all-gather.8.cloned.1.call-start = ((), (), s32[]{:S(2)}) async-start(), calls=%async_computation.4 | async-start | bytes 4177920 | tf_op jit(solution)/shard_map/all_gather | solution.py:1054
  12.6 40.0 %collective-permute-start = (bf16[12,6,1024]{2,1,0:T(8,128)(2,1)}, bf16[12,6,1024]{2,1,0:T(8,128)(2,1)}, u32[]{:S(2)}, u32[]{:S(2)}) collective-permute-start(bf16[12,6,1024]{2,1,0:T(8,128)(2,1)} %add_convert_fusion.1), channel_id=1, source_target_pairs={{0,1},{1,0},{2,3},{3,2},{4,5},{5,4},{6,7},{7,6},{8,9},{9,8},{10,11... | collective-permute-start | bytes 442376 | tf_op jit(solution)/shard_map/ppermute | solution.py:1003
  12.7 25.9 %collective-permute-start.1 = (f32[2,2048]{1,0:T(2,128)S(1)}, f32[2,2048]{1,0:T(2,128)S(1)}, u32[]{:S(2)}, u32[]{:S(2)}) collective-permute-start(f32[2,2048]{1,0:T(2,128)S(1)} %pad_maximum_fusion.37), channel_id=1, source_target_pairs={{0,1},{1,0},{2,3},{3,2},{4,5},{5,4},{6,7},{7,6},{8,9},{9,8},{10,11... | collective-permute-start | bytes 49160 | tf_op jit(solution)/shard_map/ppermute | solution.py:1003
  14.2 25.1 %collective-permute-start.2 = (f32[12,6,81]{0,2,1:T(8,128)}, f32[12,6,81]{0,2,1:T(8,128)}, u32[]{:S(2)}, u32[]{:S(2)}) collective-permute-start(f32[12,6,81]{0,2,1:T(8,128)} %maximum_convert_fusion.1), channel_id=1, source_target_pairs={{0,2},{2,0},{4,6},{6,4},{8,10},{10,8},{12,14},{14,12},{16,18},{18,... | collective-permute-start | bytes 69992 | tf_op jit(solution)/shard_map/ppermute | solution.py:1019
  16.5 52.5 %collective-permute-start.6 = (bf16[5,80,256]{2,1,0:T(8,128)(2,1)}, bf16[5,80,256]{2,1,0:T(8,128)(2,1)}, u32[]{:S(2)}, u32[]{:S(2)}) collective-permute-start(bf16[5,80,256]{2,1,0:T(8,128)(2,1)} %param.47), channel_id=1, source_target_pairs={{0,1},{1,0},{2,3},{3,2},{4,5},{5,4},{6,7},{7,6},{8,9},{9,8},{10,11... | collective-permute-start | bytes 614408 | tf_op jit(solution)/shard_map/ppermute | solution.py:1003
  17.2 15.7 %collective-permute-start.13 = (f32[2,40]{1,0:T(2,128)}, f32[2,40]{1,0:T(2,128)S(1)}, u32[]{:S(2)}, u32[]{:S(2)}) collective-permute-start(f32[2,40]{1,0:T(2,128)} %param.51), channel_id=1, source_target_pairs={{0,1},{1,0},{2,3},{3,2},{4,5},{5,4},{6,7},{7,6},{8,9},{9,8},{10,11... | collective-permute-start | bytes 968 | tf_op jit(solution)/shard_map/ppermute | solution.py:1003
  40.5 6.8 %collective-permute-start.3 = (f32[24,6,81]{0,2,1:T(8,128)S(1)}, f32[24,6,81]{0,2,1:T(8,128)S(1)}, u32[]{:S(2)}, u32[]{:S(2)}) collective-permute-start(f32[24,6,81]{0,2,1:T(8,128)S(1)} %pad_maximum_fusion.15), channel_id=1, source_target_pairs={{0,4},{2,6},{4,0},{6,2},{8,12},{10,14},{12,8},{14,10},{16,20},{18,... | collective-permute-start | bytes 139976 | tf_op jit(solution)/shard_map/ppermute | solution.py:1019
  40.8 8.7 %collective-permute-start.9 = (bf16[128,200]{1,0:T(8,128)(2,1)S(1)}, bf16[128,200]{1,0:T(8,128)(2,1)S(1)}, u32[]{:S(2)}, u32[]{:S(2)}) collective-permute-start(bf16[128,200]{1,0:T(8,128)(2,1)S(1)} %pad_maximum_fusion.30), channel_id=1, source_target_pairs={{0,8},{2,10},{4,12},{6,14},{8,0},{10,2},{12,4},{14,6},{16,24},{18,... | collective-permute-start | bytes 153608 | tf_op jit(solution)/shard_map/ppermute | solution.py:1019
  48.3 7.5 %collective-permute-start.4 = (f32[48,6,81]{0,2,1:T(8,128)}, f32[48,6,81]{0,2,1:T(8,128)}, u32[]{:S(2)}, u32[]{:S(2)}) collective-permute-start(f32[48,6,81]{0,2,1:T(8,128)} %pad_maximum_fusion.16), channel_id=1, source_target_pairs={{0,8},{2,10},{4,12},{6,14},{8,0},{10,2},{12,4},{14,6},{16,24},{18,... | collective-permute-start | bytes 279944 | tf_op jit(solution)/shard_map/ppermute | solution.py:1019
  50.3 9.3 %collective-permute-start.10 = (bf16[256,200]{1,0:T(8,128)(2,1)}, bf16[256,200]{1,0:T(8,128)(2,1)S(1)}, u32[]{:S(2)}, u32[]{:S(2)}) collective-permute-start(bf16[256,200]{1,0:T(8,128)(2,1)} %pad_maximum_fusion.26), channel_id=1, source_target_pairs={{0,16},{2,18},{4,20},{6,22},{8,24},{10,26},{12,28},{14,30},{16,0},... | collective-permute-start | bytes 307208 | tf_op jit(solution)/shard_map/ppermute | solution.py:1019
  57.7 33.1 %collective-permute-start.5 = (f32[96,6,81]{0,2,1:T(8,128)}, f32[96,6,81]{0,2,1:T(8,128)}, u32[]{:S(2)}, u32[]{:S(2)}) collective-permute-start(f32[96,6,81]{0,2,1:T(8,128)} %pad_maximum_fusion.17), channel_id=1, source_target_pairs={{0,16},{2,18},{4,20},{6,22},{8,24},{10,26},{12,28},{14,30},{16,0},... | collective-permute-start | bytes 559880 | tf_op jit(solution)/shard_map/ppermute | solution.py:1019
  59.8 32.9 %collective-permute-start.11 = (bf16[5,512,40]{1,2,0:T(8,128)(2,1)S(1)}, bf16[5,512,40]{1,2,0:T(8,128)(2,1)}, u32[]{:S(2)}, u32[]{:S(2)}) collective-permute-start(bf16[5,512,40]{1,2,0:T(8,128)(2,1)S(1)} %bitcast.326), channel_id=1, source_target_pairs={{0,1},{1,0},{2,3},{3,2},{4,5},{5,4},{6,7},{7,6},{8,9},{9,8},{10,11... | collective-permute-start | bytes 614408 | tf_op jit(solution)/shard_map/ppermute | solution.py:1003
  230.7 27.7 %collective-permute-start.14 = (bf16[16,16,272,128]{3,2,1,0:T(8,128)(2,1)}, bf16[16,16,272,128]{3,2,1,0:T(8,128)(2,1)}, u32[]{:S(2)}, u32[]{:S(2)}) collective-permute-start(bf16[16,16,272,128]{3,2,1,0:T(8,128)(2,1)} %bitcast.289), channel_id=1, source_target_pairs={{0,1},{1,0},{2,3},{3,2},{4,5},{5,4},{6,7},{7,6},{8,9},{9,8},{10,11... | collective-permute-start | bytes 53477384 | tf_op jit(solution)/shard_map/ppermute | solution.py:1003
  231.8 251.9 %all-gather.6.cloned.1.call-start = ((), (), s32[]{:S(2)}) async-start(), calls=%async_computation.3 | async-start | bytes 7659520 | tf_op jit(solution)/shard_map/all_gather | solution.py:1274
  304.6 4.1 collective-permute-start.17
  308.7 15.6 %collective-permute-start.18 = (f32[96,6,80]{2,0,1:T(8,128)S(1)}, f32[96,6,80]{2,0,1:T(8,128)S(1)}, u32[]{:S(2)}, u32[]{:S(2)}) collective-permute-start(f32[96,6,80]{2,0,1:T(8,128)S(1)} %pad_maximum_fusion.14), channel_id=1, source_target_pairs={{0,16},{2,18},{4,20},{6,22},{8,24},{10,26},{12,28},{14,30},{16,0},... | collective-permute-start | bytes 552968 | tf_op jit(solution)/shard_map/ppermute | solution.py:1019
  325.3 7.8 %collective-permute-start.19 = (bf16[15,512,256]{2,1,0:T(8,128)(2,1)}, bf16[15,512,256]{2,1,0:T(8,128)(2,1)}, u32[]{:S(2)}, u32[]{:S(2)}) collective-permute-start(bf16[15,512,256]{2,1,0:T(8,128)(2,1)} %all-gather.8.cloned.1.call-done.own_ref), channel_id=1, source_target_pairs={{0,1},{1,0},{2,3},{3,2},{4,5},{5,4},{6,7},{7,6},{8,9},{9,8},{10,11... | collective-permute-start | bytes 11796488 | tf_op jit(solution)/shard_map/ppermute | solution.py:1003
  450.1 31.5 %all-to-all-start = ((bf16[16,80,512]{2,1,0:T(8,128)(2,1)}), bf16[16,80,512]{2,1,0:T(8,128)(2,1)}, u32[]{:S(2)}, u32[]{:S(2)}) async-start(bf16[16,80,512]{2,1,0:T(8,128)(2,1)} %get-tuple-element.130), calls=%async_computation | async-start | bytes 2621440 | tf_op jit(solution)/shard_map/all_to_all | solution.py:1445
  494.7 8.4 %collective-permute-start.21 = (f32[16,272,128]{2,1,0:T(8,128)}, f32[16,272,128]{2,1,0:T(8,128)}, u32[]{:S(2)}, u32[]{:S(2)}) collective-permute-start(f32[16,272,128]{2,1,0:T(8,128)} %broadcast_select_fusion), channel_id=1, source_target_pairs={{0,1},{1,0},{2,3},{3,2},{4,5},{5,4},{6,7},{7,6},{8,9},{9,8},{10,11... | collective-permute-start | bytes 6684680 | tf_op jit(solution)/shard_map/ppermute | solution.py:1003
  498.2 3.7 collective-permute-start.31
  498.3 4.3 collective-permute-start.30
  507.3 40.6 %all-to-all-start.1 = ((bf16[16,400,128]{2,1,0:T(8,128)(2,1)}), bf16[16,400,128]{2,1,0:T(8,128)(2,1)S(1)}, u32[]{:S(2)}, u32[]{:S(2)}) async-start(bf16[16,400,128]{2,1,0:T(8,128)(2,1)} %pad_maximum_fusion.4), calls=%async_computation.1 | async-start | bytes 3276800 | tf_op jit(solution)/shard_map/all_to_all | solution.py:1590
  521.4 48.8 %collective-permute-start.27 = (f32[5,80,256]{2,1,0:T(8,128)}, f32[5,80,256]{2,1,0:T(8,128)}, u32[]{:S(2)}, u32[]{:S(2)}) collective-permute-start(f32[5,80,256]{2,1,0:T(8,128)} %slice_select_fusion.2), channel_id=1, source_target_pairs={{0,1},{1,0},{2,3},{3,2},{4,5},{5,4},{6,7},{7,6},{8,9},{9,8},{10,11... | collective-permute-start | bytes 1228808 | tf_op jit(solution)/shard_map/ppermute | solution.py:1003
  538.3 33.8 %collective-permute-start.28 = (f32[3,5,32,256]{3,2,1,0:T(8,128)}, f32[3,5,32,256]{3,2,1,0:T(8,128)}, u32[]{:S(2)}, u32[]{:S(2)}) collective-permute-start(f32[3,5,32,256]{3,2,1,0:T(8,128)} %slice_select_fusion.1), channel_id=1, source_target_pairs={{0,1},{1,0},{2,3},{3,2},{4,5},{5,4},{6,7},{7,6},{8,9},{9,8},{10,11... | collective-permute-start | bytes 1474568 | tf_op jit(solution)/shard_map/ppermute | solution.py:1003
  539.6 25.4 %collective-permute-start.29 = (f32[5,32,40]{2,1,0:T(8,128)}, f32[5,32,40]{2,1,0:T(8,128)}, u32[]{:S(2)}, u32[]{:S(2)}) collective-permute-start(f32[5,32,40]{2,1,0:T(8,128)} %slice_select_fusion.3), channel_id=1, source_target_pairs={{0,1},{1,0},{2,3},{3,2},{4,5},{5,4},{6,7},{7,6},{8,9},{9,8},{10,11... | collective-permute-start | bytes 76808 | tf_op jit(solution)/shard_map/ppermute | solution.py:1003
  548.0 8.5 %collective-permute-start.22 = (bf16[128,128]{1,0:T(8,128)(2,1)S(1)}, bf16[128,128]{1,0:T(8,128)(2,1)S(1)}, u32[]{:S(2)}, u32[]{:S(2)}) collective-permute-start(bf16[128,128]{1,0:T(8,128)(2,1)S(1)} %slice_reduce_fusion), channel_id=1, source_target_pairs={{0,16},{2,18},{4,20},{6,22},{8,24},{10,26},{12,28},{14,30},{16,0},... | collective-permute-start | bytes 98312 | tf_op jit(solution)/shard_map/ppermute | solution.py:1019
  556.5 6.8 %collective-permute-start.23 = (bf16[2,128,128]{2,1,0:T(8,128)(2,1)S(1)}, bf16[2,128,128]{2,1,0:T(8,128)(2,1)S(1)}, u32[]{:S(2)}, u32[]{:S(2)}) collective-permute-start(bf16[2,128,128]{2,1,0:T(8,128)(2,1)S(1)} %pad_maximum_fusion.31), channel_id=1, source_target_pairs={{0,8},{2,10},{4,12},{6,14},{8,0},{10,2},{12,4},{14,6},{16,24},{18,... | collective-permute-start | bytes 196616 | tf_op jit(solution)/shard_map/ppermute | solution.py:1019
  559.7 18.8 %collective-permute-start.32 = (f32[12,64,512]{2,1,0:T(8,128)S(1)}, f32[12,64,512]{2,1,0:T(8,128)S(1)}, u32[]{:S(2)}, u32[]{:S(2)}) collective-permute-start(f32[12,64,512]{2,1,0:T(8,128)S(1)} %bitcast.297), channel_id=1, source_target_pairs={{0,1},{1,0},{2,3},{3,2},{4,5},{5,4},{6,7},{7,6},{8,9},{9,8},{10,11... | collective-permute-start | bytes 4718600 | tf_op jit(solution)/shard_map/ppermute | solution.py:1003
  563.3 5.5 collective-permute-start.24
  568.8 7.2 %collective-permute-start.25 = (bf16[2,2,2,128,128]{4,3,0,1,2:T(8,128)(2,1)S(1)}, bf16[2,2,2,128,128]{4,3,0,1,2:T(8,128)(2,1)S(1)}, u32[]{:S(2)}, u32[]{:S(2)}) collective-permute-start(bf16[2,2,2,128,128]{4,3,0,1,2:T(8,128)(2,1)S(1)} %pad_maximum_fusion.19), channel_id=1, source_target_pairs={{0,2},{2,0},{4,6},{6,4},{8,10},{10,8},{12,14},{14,12},{16,18},{18,... | collective-permute-start | bytes 786440 | tf_op jit(solution)/shard_map/ppermute | solution.py:1019
  576.9 9.6 %collective-permute-start.26 = (bf16[2048,128]{1,0:T(8,128)(2,1)}, bf16[2048,128]{1,0:T(8,128)(2,1)}, u32[]{:S(2)}, u32[]{:S(2)}) collective-permute-start(bf16[2048,128]{1,0:T(8,128)(2,1)} %bitcast.61), channel_id=1, source_target_pairs={{0,1},{1,0},{2,3},{3,2},{4,5},{5,4},{6,7},{7,6},{8,9},{9,8},{10,11... | collective-permute-start | bytes 1572872 | tf_op jit(solution)/shard_map/ppermute | solution.py:1003
  (62 other events, 415.3 us)
Sparse Core Ops, SparseCore 0:
  11.3 216.8 all-gather.3
  231.9 71.1 all-gather.7
  325.4 100.7 all-gather.5

commit v4 on v3

--- a/solution.py
+++ b/solution.py
@@ -1030,11 +1030,7 @@
         return jnp.transpose(value, order).reshape((batch_size,) + value.shape[count:])
 
     def gather_rows(value):
-        bit = 1
-        while bit < batch_size:
-            value = jnp.concatenate(swapped(value, bit), axis=0)
-            bit *= 2
-        return value
+        return gather_far_first(value).reshape((-1,) + value.shape[1:])
 
     def to_tiles(value):
         return jnp.transpose(value.reshape(value.shape[0], -1, lanes), (1, 0, 2))
@@ -1062,7 +1058,7 @@
     segments_now = mine(segments)
     targets_now = mine(targets)
     frame_info = gather_rows(
-        jnp.concatenate([targets_now, segments_now[:, :, None].astype(bf16)], axis=2).astype(f32)
+        jnp.concatenate([targets_now, segments_now[:, :, None].astype(bf16)], axis=2)
     )
 
     same_frames = segments_now[:, :, None] == segments_now[:, None, :]

time: 611 us -> 606 us (level)
    ppermute x16, waiting for transfers between devices: 53.2 us -> 31.9 us  [swapped(): other = lax.ppermute(value, 'batch', pairs)]
    all_gather x1, waiting for transfers between devices: 133 us -> 147 us  [gathered(): return lax.all_gather(value, 'batch', axis=1, tiled=True)]
  transfers between devices with their start and end apart: 38 -> 38, of which waited for: 19 -> 18; matrix products, arithmetic and copies ran while one was open for 18% -> 18% of each run, Pallas kernels for 25% -> 25%
where the time goes in v4:
time: 606 us; the launch traced here: 597 us
  waiting for transfers between devices  230 us (38%)
  Pallas kernels  152 us (25%)
  local copies, waits for them, and re-layouts  58 us (10%)
  starting transfers between devices  57.8 us (10%)
  other arithmetic  57.6 us (10%)
  matrix products  25.3 us (4%)
  between operations  16 us (3%)
    all_gather x1, waiting for transfers between devices, gathered(): return lax.all_gather(value, 'batch', axis=1, tiled=True)  147 us
    pallas_call x1, Pallas kernels, call_backward(): pl.pallas_call(functools.partial(backward_kernel, len(weights)), out_shap...  58.8 us
    pallas_call x1, Pallas kernels, call_postnet(): pl.pallas_call(functools.partial(postnet_kernel, mel_width, loss_scale),...  54.8 us
    pallas_call x1, Pallas kernels, call_forward(): pl.pallas_call(functools.partial(forward_kernel, len(weights)), out_shape...  38.5 us
    ppermute x17, waiting for transfers between devices, exchange(): return lax.ppermute(value, 'unit', [(0, 1), (1, 0)])  37.4 us
    ppermute x16, waiting for transfers between devices, swapped(): other = lax.ppermute(value, 'batch', pairs)  31.9 us
    ppermute x16, starting transfers between devices, swapped(): other = lax.ppermute(value, 'batch', pairs)  23.5 us
    ppermute x17, starting transfers between devices, exchange(): return lax.ppermute(value, 'unit', [(0, 1), (1, 0)])  21.8 us
  transfers between devices with their start and end apart: 38, of which 18 were waited for; matrix products, arithmetic and copies ran while one was open for 18% of the time, Pallas kernels for 25%

profile of v4, /device:TPU:1, one launch (start us, length us, event | category | flops | bytes accessed | tf_op | source)
XLA Modules:
  0.0 596.5 jit_solution(1167744722280170243)
XLA Ops:
  14.1 3.3 collective-permute-start.2
  46.8 2.8 collective-permute-done.8
  63.9 5.6 collective-permute-start.11
  73.0 147.4 %all-gather.4.cloned.1.call-done = bf16[16,4352,128]{2,1,0:T(8,128)(2,1)} async-done(((bf16[16,272,128]{2,1,0:T(8,128)(2,1)}), bf16[16,4352,128]{2,1,0:T(8,128)(2,1)}) %all-gather.4.cloned.1.call-update) | async-done | bytes 17825808 | tf_op jit(solution)/shard_map/all_gather | solution.py:1041
  224.2 26.4 %collective-permute-done.14.refs_1_ = bf16[16,16,272,128]{3,2,1,0:T(8,128)(2,1)} collective-permute-done((bf16[16,16,272,128]{3,2,1,0:T(8,128)(2,1)}, bf16[16,16,272,128]{3,2,1,0:T(8,128)(2,1)}, u32[]{:S(2)}, u32[]{:S(2)}) %collective-permute-start.14) | collective-permute-done | bytes 17825824 | tf_op jit(solution)/shard_map/ppermute | solution.py:1003
  250.6 38.5 %decoder_forward.1 = (f32[3,48,4096]{2,1,0:T(8,128)}, f32[3,48,4096]{2,1,0:T(8,128)}, f32[3,48,1024]{2,1,0:T(8,128)}, f32[3,48,1024]{2,1,0:T(8,128)}, f32[3,48,1...) custom-call(s32[1]{0:T(128)} %bitcast.unit_ref, ...), custom_call_target="tpu_custom_call" | custom-call | tf_op jit(solution)/shard_map/decoder_forward/pallas_call | solution.py:591
  293.4 4.4 collective-permute-done.15
  298.0 3.8 collective-permute-done.16
  303.5 3.5 collective-permute-done.17
  308.2 7.4 %collective-permute-done.18 = f32[2,2,2,12,6,80]{5,3,0,1,2,4:T(8,128)S(1)} collective-permute-done((f32[2,2,2,12,6,80]{5,3,0,1,2,4:T(8,128)S(1)}, f32[2,2,2,12,6,80]{5,3,0,1,2,4:T(8,128)S(1)}, u32[]{:S(2)}, u32[]{:S(2)}) %collective-permute-start.18) | collective-permute-done | bytes 184352 | tf_op jit(solution)/shard_map/ppermute | solution.py:1019
  316.8 3.2 collective-permute-start.19
  321.2 5.5 collective-permute-done.19.peer_ref
  326.7 54.8 %postnet.1 = (bf16[1152,80]{1,0:T(8,128)(2,1)}, bf16[4,1152,512]{2,1,0:T(8,128)(2,1)}, bf16[4,1152,512]{2,1,0:T(8,128)(2,1)}, bf16[1152,80]{1,0:T(8,128)(2,1)}, ...) custom-call(s32[1]{0:T(128)} %bitcast.unit_ref, f32[1152,80]{1,0:T(8,128)} %bitcast.363, f32[1152,80]{1,0:T(8,128)} %bitcast.362, ...), custom_call_target="tpu_custom_call" | custom-call | tf_op jit(solution)/shard_map/postnet/pallas_call | solution.py:892
  383.4 58.8 %decoder_backward.1 = (bf16[16,80,512]{2,1,0:T(8,128)(2,1)}, f32[3,48,256]{2,1,0:T(8,128)}, f32[3,48,512]{2,1,0:T(8,128)}, f32[3,48,128]{2,1,0:T(8,128)}, f32[76...) custom-call(s32[1]{0:T(128)} %bitcast.unit_ref, bf16[16,16,272,128]{3,2,1,0:T(8,128)(2,1)} %bitcast.349, ...), custom_call_target="tpu_custom_call" | custom-call | tf_op jit(solution)/shard_map/decoder_backward/pallas_call | solution.py:638
  443.8 4.9 all-to-all-start
  456.3 2.4 concatenate.153
  460.4 2.3 collective-permute-done.20
  462.7 2.2 select_add_fusion
  464.9 11.0 %all-to-all-done = bf16[16,80,512]{2,1,0:T(8,128)(2,1)} async-done(((bf16[16,80,512]{2,1,0:T(8,128)(2,1)}), bf16[16,80,512]{2,1,0:T(8,128)(2,1)}, u32[]{:S(2)}, u32[]{:S(2)}) %all-to-all-start) | async-done | bytes 1310752 | tf_op jit(solution)/shard_map/all_to_all | solution.py:1441
  478.1 2.8 fusion.2
  481.9 2.3 fusion
  489.1 3.0 collective-permute-start.21
  492.8 3.1 collective-permute-done.31
  497.2 2.8 add_convert_fusion
  501.3 7.3 %all-to-all-start.1 = ((bf16[16,400,128]{2,1,0:T(8,128)(2,1)}), bf16[16,400,128]{2,1,0:T(8,128)(2,1)S(1)}, u32[]{:S(2)}, u32[]{:S(2)}) async-start(bf16[16,400,128]{2,1,0:T(8,128)(2,1)} %pad_maximum_fusion.4), calls=%async_computation.1 | async-start | bytes 3276800 | tf_op jit(solution)/shard_map/all_to_all | solution.py:1586
  508.7 4.0 fusion.119
  515.9 4.2 fusion.118
  534.8 2.5 fusion.23
  537.3 2.5 fusion.25
  542.0 7.1 %collective-permute-start.22 = (bf16[128,128]{1,0:T(8,128)(2,1)S(1)}, bf16[128,128]{1,0:T(8,128)(2,1)S(1)}, u32[]{:S(2)}, u32[]{:S(2)}) collective-permute-start(bf16[128,128]{1,0:T(8,128)(2,1)S(1)} %slice_reduce_fusion), channel_id=1, source_target_pairs={{0,16},{2,18},{4,20},{6,22},{8,24},{10,26},{12,28},{14,30},{16,0},... | collective-permute-start | bytes 98312 | tf_op jit(solution)/shard_map/ppermute | solution.py:1019
  550.6 3.1 add_add_fusion
  553.8 3.6 collective-permute-start.32
  (485 shorter events, 144.0 us)
Async XLA Ops:
  7.2 213.2 %all-gather.4.cloned.1.call-start = ((), (), s32[]{:S(2)}) async-start(), calls=%async_computation.2 | async-start | bytes 18939904 | tf_op jit(solution)/shard_map/all_gather | solution.py:1041
  10.7 306.1 %all-gather.8.cloned.1.call-start = ((), (), s32[]{:S(2)}) async-start(), calls=%async_computation.4 | async-start | bytes 4177920 | tf_op jit(solution)/shard_map/all_gather | solution.py:1050
  11.9 43.2 %collective-permute-start = (bf16[12,6,1024]{2,1,0:T(8,128)(2,1)S(1)}, bf16[12,6,1024]{2,1,0:T(8,128)(2,1)}, u32[]{:S(2)}, u32[]{:S(2)}) collective-permute-start(bf16[12,6,1024]{2,1,0:T(8,128)(2,1)S(1)} %add_convert_fusion.1), channel_id=1, source_target_pairs={{0,1},{1,0},{2,3},{3,2},{4,5},{5,4},{6,7},{7,6},{8,9},{9,8},{10,11... | collective-permute-start | bytes 442376 | tf_op jit(solution)/shard_map/ppermute | solution.py:1003
  12.7 30.2 %collective-permute-start.1 = (f32[2,2048]{1,0:T(2,128)}, f32[2,2048]{1,0:T(2,128)}, u32[]{:S(2)}, u32[]{:S(2)}) collective-permute-start(f32[2,2048]{1,0:T(2,128)} %pad_maximum_fusion.37), channel_id=1, source_target_pairs={{0,1},{1,0},{2,3},{3,2},{4,5},{5,4},{6,7},{7,6},{8,9},{9,8},{10,11... | collective-permute-start | bytes 49160 | tf_op jit(solution)/shard_map/ppermute | solution.py:1003
  14.1 23.3 %collective-permute-start.2 = (bf16[12,6,81]{2,1,0:T(8,128)(2,1)}, bf16[12,6,81]{2,1,0:T(8,128)(2,1)}, u32[]{:S(2)}, u32[]{:S(2)}) collective-permute-start(bf16[12,6,81]{2,1,0:T(8,128)(2,1)} %pad_maximum_fusion.35), channel_id=1, source_target_pairs={{0,16},{2,18},{4,20},{6,22},{8,24},{10,26},{12,28},{14,30},{16,0},... | collective-permute-start | bytes 35000 | tf_op jit(solution)/shard_map/ppermute | solution.py:1019
  17.5 52.0 %collective-permute-start.6 = (bf16[5,80,256]{2,1,0:T(8,128)(2,1)}, bf16[5,80,256]{2,1,0:T(8,128)(2,1)}, u32[]{:S(2)}, u32[]{:S(2)}) collective-permute-start(bf16[5,80,256]{2,1,0:T(8,128)(2,1)} %param.47), channel_id=1, source_target_pairs={{0,1},{1,0},{2,3},{3,2},{4,5},{5,4},{6,7},{7,6},{8,9},{9,8},{10,11... | collective-permute-start | bytes 614408 | tf_op jit(solution)/shard_map/ppermute | solution.py:1003
  18.2 17.7 %collective-permute-start.13 = (f32[2,40]{1,0:T(2,128)}, f32[2,40]{1,0:T(2,128)}, u32[]{:S(2)}, u32[]{:S(2)}) collective-permute-start(f32[2,40]{1,0:T(2,128)} %param.51), channel_id=1, source_target_pairs={{0,1},{1,0},{2,3},{3,2},{4,5},{5,4},{6,7},{7,6},{8,9},{9,8},{10,11... | collective-permute-start | bytes 968 | tf_op jit(solution)/shard_map/ppermute | solution.py:1003
  37.3 4.3 collective-permute-start.7
  38.3 7.7 %collective-permute-start.3 = (bf16[2,12,6,81]{3,2,1,0:T(8,128)(2,1)S(1)}, bf16[2,12,6,81]{3,2,1,0:T(8,128)(2,1)S(1)}, u32[]{:S(2)}, u32[]{:S(2)}) collective-permute-start(bf16[2,12,6,81]{3,2,1,0:T(8,128)(2,1)S(1)} %pad_maximum_fusion.30), channel_id=1, source_target_pairs={{0,8},{2,10},{4,12},{6,14},{8,0},{10,2},{12,4},{14,6},{16,24},{18,... | collective-permute-start | bytes 69992 | tf_op jit(solution)/shard_map/ppermute | solution.py:1019
  41.6 8.0 %collective-permute-start.8 = (bf16[2,32,200]{2,1,0:T(8,128)(2,1)S(1)}, bf16[2,32,200]{2,1,0:T(8,128)(2,1)S(1)}, u32[]{:S(2)}, u32[]{:S(2)}) collective-permute-start(bf16[2,32,200]{2,1,0:T(8,128)(2,1)S(1)} %pad_maximum_fusion.33), channel_id=1, source_target_pairs={{0,8},{2,10},{4,12},{6,14},{8,0},{10,2},{12,4},{14,6},{16,24},{18,... | collective-permute-start | bytes 76808 | tf_op jit(solution)/shard_map/ppermute | solution.py:1019
  46.0 4.3 collective-permute-start.4
  50.4 7.8 %collective-permute-start.5 = (bf16[2,2,2,12,6,81]{5,4,3,2,1,0:T(8,128)(2,1)S(1)}, bf16[2,2,2,12,6,81]{5,4,3,2,1,0:T(8,128)(2,1)}, u32[]{:S(2)}, u32[]{:S(2)}) collective-permute-start(bf16[2,2,2,12,6,81]{5,4,3,2,1,0:T(8,128)(2,1)S(1)} %pad_maximum_fusion.19), channel_id=1, source_target_pairs={{0,2},{2,0},{4,6},{6,4},{8,10},{10,8},{12,14},{14,12},{16,18},{18,... | collective-permute-start | bytes 279944 | tf_op jit(solution)/shard_map/ppermute | solution.py:1019
  53.5 8.3 %collective-permute-start.10 = (bf16[2,2,2,32,200]{4,3,2,1,0:T(8,128)(2,1)}, bf16[2,2,2,32,200]{4,3,2,1,0:T(8,128)(2,1)S(1)}, u32[]{:S(2)}, u32[]{:S(2)}) collective-permute-start(bf16[2,2,2,32,200]{4,3,2,1,0:T(8,128)(2,1)} %pad_maximum_fusion.23), channel_id=1, source_target_pairs={{0,2},{2,0},{4,6},{6,4},{8,10},{10,8},{12,14},{14,12},{16,18},{18,... | collective-permute-start | bytes 307208 | tf_op jit(solution)/shard_map/ppermute | solution.py:1019
  63.9 7.5 %collective-permute-start.11 = (bf16[5,512,40]{1,2,0:T(8,128)(2,1)S(1)}, bf16[5,512,40]{1,2,0:T(8,128)(2,1)S(1)}, u32[]{:S(2)}, u32[]{:S(2)}) collective-permute-start(bf16[5,512,40]{1,2,0:T(8,128)(2,1)S(1)} %bitcast.382), channel_id=1, source_target_pairs={{0,1},{1,0},{2,3},{3,2},{4,5},{5,4},{6,7},{7,6},{8,9},{9,8},{10,11... | collective-permute-start | bytes 614408 | tf_op jit(solution)/shard_map/ppermute | solution.py:1003
  222.9 27.7 %collective-permute-start.14 = (bf16[16,16,272,128]{3,2,1,0:T(8,128)(2,1)}, bf16[16,16,272,128]{3,2,1,0:T(8,128)(2,1)}, u32[]{:S(2)}, u32[]{:S(2)}) collective-permute-start(bf16[16,16,272,128]{3,2,1,0:T(8,128)(2,1)} %bitcast.347), channel_id=1, source_target_pairs={{0,1},{1,0},{2,3},{3,2},{4,5},{5,4},{6,7},{7,6},{8,9},{9,8},{10,11... | collective-permute-start | bytes 53477384 | tf_op jit(solution)/shard_map/ppermute | solution.py:1003
  224.0 254.1 %all-gather.6.cloned.1.call-start = ((), (), s32[]{:S(2)}) async-start(), calls=%async_computation.3 | async-start | bytes 7659520 | tf_op jit(solution)/shard_map/all_gather | solution.py:1270
  290.0 7.8 %collective-permute-start.15 = (f32[12,6,80]{2,0,1:T(8,128)S(1)}, f32[12,6,80]{2,0,1:T(8,128)S(1)}, u32[]{:S(2)}, u32[]{:S(2)}) collective-permute-start(f32[12,6,80]{2,0,1:T(8,128)S(1)} %copy.325), channel_id=1, source_target_pairs={{0,16},{2,18},{4,20},{6,22},{8,24},{10,26},{12,28},{14,30},{16,0},... | collective-permute-start | bytes 69128 | tf_op jit(solution)/shard_map/ppermute | solution.py:1019
  301.9 5.2 collective-permute-start.17
  307.1 8.5 %collective-permute-start.18 = (f32[2,2,2,12,6,80]{5,3,0,1,2,4:T(8,128)S(1)}, f32[2,2,2,12,6,80]{5,3,0,1,2,4:T(8,128)S(1)}, u32[]{:S(2)}, u32[]{:S(2)}) collective-permute-start(f32[2,2,2,12,6,80]{5,3,0,1,2,4:T(8,128)S(1)} %pad_maximum_fusion.14), channel_id=1, source_target_pairs={{0,2},{2,0},{4,6},{6,4},{8,10},{10,8},{12,14},{14,12},{16,18},{18,... | collective-permute-start | bytes 552968 | tf_op jit(solution)/shard_map/ppermute | solution.py:1019
  316.8 10.0 %collective-permute-start.19 = (bf16[15,512,256]{2,1,0:T(8,128)(2,1)}, bf16[15,512,256]{2,1,0:T(8,128)(2,1)}, u32[]{:S(2)}, u32[]{:S(2)}) collective-permute-start(bf16[15,512,256]{2,1,0:T(8,128)(2,1)} %all-gather.8.cloned.1.call-done.own_ref), channel_id=1, source_target_pairs={{0,1},{1,0},{2,3},{3,2},{4,5},{5,4},{6,7},{7,6},{8,9},{9,8},{10,11... | collective-permute-start | bytes 11796488 | tf_op jit(solution)/shard_map/ppermute | solution.py:1003
  443.8 32.1 %all-to-all-start = ((bf16[16,80,512]{2,1,0:T(8,128)(2,1)}), bf16[16,80,512]{2,1,0:T(8,128)(2,1)}, u32[]{:S(2)}, u32[]{:S(2)}) async-start(bf16[16,80,512]{2,1,0:T(8,128)(2,1)} %get-tuple-element.130), calls=%async_computation | async-start | bytes 2621440 | tf_op jit(solution)/shard_map/all_to_all | solution.py:1441
  489.1 8.1 %collective-permute-start.21 = (f32[16,272,128]{2,1,0:T(8,128)}, f32[16,272,128]{2,1,0:T(8,128)}, u32[]{:S(2)}, u32[]{:S(2)}) collective-permute-start(f32[16,272,128]{2,1,0:T(8,128)} %broadcast_select_fusion), channel_id=1, source_target_pairs={{0,1},{1,0},{2,3},{3,2},{4,5},{5,4},{6,7},{7,6},{8,9},{9,8},{10,11... | collective-permute-start | bytes 6684680 | tf_op jit(solution)/shard_map/ppermute | solution.py:1003
  501.3 40.7 %all-to-all-start.1 = ((bf16[16,400,128]{2,1,0:T(8,128)(2,1)}), bf16[16,400,128]{2,1,0:T(8,128)(2,1)S(1)}, u32[]{:S(2)}, u32[]{:S(2)}) async-start(bf16[16,400,128]{2,1,0:T(8,128)(2,1)} %pad_maximum_fusion.4), calls=%async_computation.1 | async-start | bytes 3276800 | tf_op jit(solution)/shard_map/all_to_all | solution.py:1586
  515.4 48.9 %collective-permute-start.27 = (f32[5,80,256]{2,1,0:T(8,128)}, f32[5,80,256]{2,1,0:T(8,128)}, u32[]{:S(2)}, u32[]{:S(2)}) collective-permute-start(f32[5,80,256]{2,1,0:T(8,128)} %slice_select_fusion.2), channel_id=1, source_target_pairs={{0,1},{1,0},{2,3},{3,2},{4,5},{5,4},{6,7},{7,6},{8,9},{9,8},{10,11... | collective-permute-start | bytes 1228808 | tf_op jit(solution)/shard_map/ppermute | solution.py:1003
  532.3 33.9 %collective-permute-start.28 = (f32[3,5,32,256]{3,2,1,0:T(8,128)}, f32[3,5,32,256]{3,2,1,0:T(8,128)}, u32[]{:S(2)}, u32[]{:S(2)}) collective-permute-start(f32[3,5,32,256]{3,2,1,0:T(8,128)} %slice_select_fusion.1), channel_id=1, source_target_pairs={{0,1},{1,0},{2,3},{3,2},{4,5},{5,4},{6,7},{7,6},{8,9},{9,8},{10,11... | collective-permute-start | bytes 1474568 | tf_op jit(solution)/shard_map/ppermute | solution.py:1003
  533.5 25.5 %collective-permute-start.29 = (f32[5,32,40]{2,1,0:T(8,128)}, f32[5,32,40]{2,1,0:T(8,128)}, u32[]{:S(2)}, u32[]{:S(2)}) collective-permute-start(f32[5,32,40]{2,1,0:T(8,128)} %slice_select_fusion.3), channel_id=1, source_target_pairs={{0,1},{1,0},{2,3},{3,2},{4,5},{5,4},{6,7},{7,6},{8,9},{9,8},{10,11... | collective-permute-start | bytes 76808 | tf_op jit(solution)/shard_map/ppermute | solution.py:1003
  542.0 8.5 %collective-permute-start.22 = (bf16[128,128]{1,0:T(8,128)(2,1)S(1)}, bf16[128,128]{1,0:T(8,128)(2,1)S(1)}, u32[]{:S(2)}, u32[]{:S(2)}) collective-permute-start(bf16[128,128]{1,0:T(8,128)(2,1)S(1)} %slice_reduce_fusion), channel_id=1, source_target_pairs={{0,16},{2,18},{4,20},{6,22},{8,24},{10,26},{12,28},{14,30},{16,0},... | collective-permute-start | bytes 98312 | tf_op jit(solution)/shard_map/ppermute | solution.py:1019
  550.5 6.8 %collective-permute-start.23 = (bf16[2,128,128]{2,1,0:T(8,128)(2,1)S(1)}, bf16[2,128,128]{2,1,0:T(8,128)(2,1)S(1)}, u32[]{:S(2)}, u32[]{:S(2)}) collective-permute-start(bf16[2,128,128]{2,1,0:T(8,128)(2,1)S(1)} %pad_maximum_fusion.29), channel_id=1, source_target_pairs={{0,8},{2,10},{4,12},{6,14},{8,0},{10,2},{12,4},{14,6},{16,24},{18,... | collective-permute-start | bytes 196616 | tf_op jit(solution)/shard_map/ppermute | solution.py:1019
  553.8 18.8 %collective-permute-start.32 = (f32[12,64,512]{2,1,0:T(8,128)S(1)}, f32[12,64,512]{2,1,0:T(8,128)S(1)}, u32[]{:S(2)}, u32[]{:S(2)}) collective-permute-start(f32[12,64,512]{2,1,0:T(8,128)S(1)} %bitcast.355), channel_id=1, source_target_pairs={{0,1},{1,0},{2,3},{3,2},{4,5},{5,4},{6,7},{7,6},{8,9},{9,8},{10,11... | collective-permute-start | bytes 4718600 | tf_op jit(solution)/shard_map/ppermute | solution.py:1003
  557.3 5.5 collective-permute-start.24
  562.9 7.2 %collective-permute-start.25 = (bf16[2,2,2,128,128]{4,3,0,1,2:T(8,128)(2,1)S(1)}, bf16[2,2,2,128,128]{4,3,0,1,2:T(8,128)(2,1)S(1)}, u32[]{:S(2)}, u32[]{:S(2)}) collective-permute-start(bf16[2,2,2,128,128]{4,3,0,1,2:T(8,128)(2,1)S(1)} %pad_maximum_fusion.15), channel_id=1, source_target_pairs={{0,2},{2,0},{4,6},{6,4},{8,10},{10,8},{12,14},{14,12},{16,18},{18,... | collective-permute-start | bytes 786440 | tf_op jit(solution)/shard_map/ppermute | solution.py:1019
  571.0 9.5 %collective-permute-start.26 = (bf16[2048,128]{1,0:T(8,128)(2,1)}, bf16[2048,128]{1,0:T(8,128)(2,1)}, u32[]{:S(2)}, u32[]{:S(2)}) collective-permute-start(bf16[2048,128]{1,0:T(8,128)(2,1)} %bitcast.91), channel_id=1, source_target_pairs={{0,1},{1,0},{2,3},{3,2},{4,5},{5,4},{6,7},{7,6},{8,9},{9,8},{10,11... | collective-permute-start | bytes 1572872 | tf_op jit(solution)/shard_map/ppermute | solution.py:1003
  (73 other events, 513.1 us)
Sparse Core Ops, SparseCore 0:
  11.3 209.0 all-gather.3
  224.1 74.1 all-gather.7
  316.8 102.2 all-gather.5
